TPU v7x, 32 devices: a whole 2x2x4 slice. The times are simulated.
32 devices in a mesh: dp: 4 (over z), ctx: 8 (over y, x, core).
Axes of the slice: x: 2, y: 2, z: 4, core: 2. Of those that a mesh axis runs over, the one named last changes fastest.
Arguments:
- queries: bfloat16 [8192, 1024], P(('dp', 'ctx')), may hold values from -27 to 27, as said below
- keys: bfloat16 [8192, 128], P(('dp', 'ctx')), may hold values from -4 to 4, as said below
- values: bfloat16 [8192, 128], P(('dp', 'ctx')), may hold values from -6 to 6
- grad_out: bfloat16 [8192, 1024], P(('dp', 'ctx')), may hold values from -6 to 6
- lengths: int32 [16], replicated, may hold values from 1 to 2048, 8192 in all
Outputs:
- attn_out: bfloat16 [8192, 1024], P(('dp', 'ctx'))
- grad_queries: bfloat16 [8192, 1024], P(('dp', 'ctx'))
- grad_keys: bfloat16 [8192, 128], P(('dp', 'ctx'))
- grad_values: bfloat16 [8192, 128], P(('dp', 'ctx'))
Inputs may be any that keep to these rules, and one draw needn't show every extreme that they name: `queries`: query entries lie in this range. `keys`: key entries lie in this range.
All inputs are finite; a program needn't handle non-finite values.
Results may differ from a plain program's by a relative error of at most 0.029.
Values may be sent and summed in bfloat16 or wider, within the bound.
No kernel may reach another device: no remote copies, remote signals or barrier semaphores. Data moves between devices by JAX's collectives and lax.ppermute only.
A program may use at most 192 MiB of HBM per device.

v0:
```python
import functools
import math

import jax
import jax.numpy as jnp
from jax import lax
from jax.experimental import pallas as pl
from jax.experimental.pallas import tpu as pltpu
from jax.sharding import PartitionSpec as P

HEADS = 8
HDIM = 128
NEG_FILL = -1e30
SCALE = float(HDIM) ** -0.5
EXP2_SCALE = SCALE * math.log2(math.e)

NT = (((1,), (1,)), ((), ()))
NN = (((1,), (0,)), ((), ()))
F32, BF16 = jnp.float32, jnp.bfloat16


def dot(a, b, dims=NN):
    return lax.dot_general(a, b, dims, preferred_element_type=F32)


def wide(column):
    return jnp.concatenate([column, column], axis=1)


def run_route(n_dp, n_ctx):
    return [(d * n_ctx + c, (d + 1) * n_ctx + c) for d in range(n_dp - 1) for c in range(n_ctx)]


def flip_route(n_dp, n_ctx, flip):
    return [(d * n_ctx + c, d * n_ctx + (c ^ flip)) for d in range(n_dp) for c in range(n_ctx)]


def facts_of(n_ctx, rows, index, lengths_ref):
    base = index * rows
    ends, end = [], jnp.int32(0)
    for i in range(lengths_ref.shape[0]):
        end = end + lengths_ref[i]
        ends.append(end)
    low, high = jnp.int32(0), ends[-1]
    for end in ends:
        low = jnp.where(end <= base, end, low)
    for end in reversed(ends):
        high = jnp.where(end > base, end, high)
    before = lax.div(base - low + rows - 1, rows)
    short = (high - base <= rows - rows // n_ctx).astype(jnp.int32)
    return (lax.rem(index, n_ctx), base, before, short), ends


class Place:
    def __init__(self, n_ctx, rows, facts):
        self.n_ctx, self.rows = n_ctx, rows
        self.ctx, self.base, self.before, short = facts if isinstance(facts, tuple) else (facts[i, 0] for i in range(4))
        self.short = short == 1

    def hop(self, back):
        return lax.div(self.ctx ^ lax.rem(self.ctx - back + 2 * self.n_ctx, self.n_ctx), 2)

    def past(self, backs, body):
        first, step = backs[0], backs.step
        count = jnp.clip(lax.div(self.before - first + step, step), 0, len(backs))
        for short in (True, False):
            many = HEADS * (self.rows - self.rows // self.n_ctx if short else self.rows)
            fits = self.short if short else jnp.logical_not(self.short)

            if len(backs) > 1:

                @pl.when(fits)
                def _():
                    @pl.loop(0, lax.div(count, 2))
                    def _(i):
                        body((first + 2 * i * step, first + (2 * i + 1) * step), many)

            @pl.when(fits & (lax.rem(count, 2) == 1))
            def _():
                body((first + (count - 1) * step,), many)

        return count


def chunks(rows, n_ctx):
    size = rows // n_ctx
    for c in range(n_ctx):
        for h in range(HEADS):
            yield (pl.ds((c * HEADS + h) * size, size), (pl.ds(c * size, size), pl.ds(h * HDIM, HDIM)))


def fetch(pairs, sems):
    copies = [pltpu.make_async_copy(source, target, sems.at[i]) for i, (source, target) in enumerate(pairs)]
    for copy in copies:
        copy.start()
    return copies


def join(keys, values, kv, sems):
    for copy in fetch([(keys, kv.at[:, pl.ds(0, HDIM)]), (values, kv.at[:, pl.ds(HDIM, HDIM)])], sems):
        copy.wait()


def with_ones(kv):
    return jnp.concatenate([kv, jnp.ones((kv.shape[0], HDIM), BF16)], axis=1)


def levels(place, back, many, q_s, key_block, start):
    size, rows = place.rows // place.n_ctx, place.rows
    tokens = many // HEADS
    key = place.base - back * rows + lax.broadcasted_iota(jnp.int32, (tokens, rows), 1)
    query = place.base + lax.broadcasted_iota(jnp.int32, (tokens, rows), 0)
    off = jnp.where((key >= start[:tokens, :]) & (key <= query), 0.0, NEG_FILL)
    s = dot(q_s[:many, :], key_block, NT) * EXP2_SCALE
    s = s.reshape(tokens // size, HEADS, size, rows) + off.reshape(tokens // size, 1, size, rows)
    return s.reshape(many, rows)


def fold(s):
    return jnp.maximum(s[:, :HDIM], s[:, HDIM:])


def row_max(s):
    return jnp.broadcast_to(jnp.max(s, axis=1, keepdims=True), (s.shape[0], HDIM))


def prepare(n_ctx, lengths_hbm, q_hbm, do_hbm, kv_ref, facts_ref, kv_own, q_s, q_t, do_r, start, level, p_own, acc,
            lengths_ref, q_ref, do_ref, sems):
    copies = fetch([(lengths_hbm, lengths_ref), (q_hbm, q_ref), (do_hbm, do_ref)], sems)
    rows = q_ref.shape[0]
    index = lax.axis_index("dp") * n_ctx + lax.axis_index("ctx")
    kv_own[...] = with_ones(kv_ref[...])
    copies[0].wait()
    facts, ends = facts_of(n_ctx, rows, index, lengths_ref)
    place = Place(n_ctx, rows, facts)
    line = lax.broadcasted_iota(jnp.int32, facts_ref.shape, 0)
    held = jnp.zeros(facts_ref.shape, jnp.int32)
    for i, fact in enumerate(facts):
        held = jnp.where(line == i, fact, held)
    facts_ref[...] = held
    token = place.base + lax.broadcasted_iota(jnp.int32, (rows, HDIM), 0)
    begin = jnp.zeros((rows, HDIM), jnp.int32)
    for end in ends:
        begin = jnp.where(token >= end, end, begin)
    start[...] = wide(begin) if rows == 2 * HDIM else jnp.broadcast_to(begin[:, :1], (rows, rows))
    copies[1].wait()
    for here, there in chunks(rows, n_ctx):
        q_s[here, :] = q_ref[there]
    s = levels(place, 0, HEADS * rows, q_s, kv_own[:, :HDIM], start)
    top = row_max(fold(s))
    level[...] = top
    p = jnp.exp2(s - wide(top)).astype(BF16)
    p_own[...] = p
    acc[...] = dot(p, kv_own[:, HDIM:])
    copies[2].wait()
    for here, there in chunks(rows, n_ctx):
        do_r[here, :] = do_ref[there]
    for h in range(HEADS):
        here = pl.ds(h * rows, rows)
        q_t[:, here] = q_s[here, :].T


def side_by_side(parts, axis):
    return parts[0] if len(parts) == 1 else jnp.concatenate(parts, axis=axis)


def attend(place, backs, many, q_s, kvs, start, level, acc, probs):
    scores = [levels(place, back, many, q_s, kv[:, :HDIM], start) for back, kv in zip(backs, kvs)]
    p = [jnp.exp2(s - wide(level[:many, :])).astype(BF16) for s in scores]
    for ref, part in zip(probs, p):
        ref[:many, :] = part
    acc[:many, :] += dot(side_by_side(p, 1), side_by_side([kv[:, HDIM:] for kv in kvs], 0))


def attend_even(n_ctx, facts, q_s, start, level, acc_in, *refs):
    *got, kv_even, p_even, acc = refs
    rows = got[0].shape[0]
    place = Place(n_ctx, rows, facts)
    for i, ref in enumerate(got):
        kv_even[i] = with_ones(ref[...])
    acc[...] = acc_in[...]

    def body(backs, many):
        attend(place, backs, many, q_s, [kv_even.at[place.hop(back)] for back in backs], start, level, acc,
               [p_even.at[lax.div(back, 2) - 1] for back in backs])

    place.past(range(2, n_ctx + 1, 2), body)


def gradients(many, q_t, do_s, do_t, ps, kvs, corr):
    d = [dot(do_s[:many, :], kv[:, HDIM:2 * HDIM], NT) for kv in kvs]
    dv = [dot(do_t[:, :many], p) for p in ps]
    ds = [(p.astype(F32) * (each - wide(corr[:many, :]))).astype(BF16) for p, each in zip(ps, d)]
    dk = [dot(q_t[:, :many], each) for each in ds]
    return [(each, jnp.concatenate([k.T, v.T], axis=1)) for each, k, v in zip(ds, dk, dv)]


def forward(n_ctx, facts, q_s, q_t, do_r, start, level, acc_in, kv_own, kv_even, kv_passed, p_own_in, p_even_in,
            o_hbm, kv_odd, ds_odd, do_s, do_t, corr, g_passed, p_own, p_even, o_ref, p_odd, acc, top, p_new, kv_now, sems):
    rows = o_ref.shape[0]
    size = rows // n_ctx
    place = Place(n_ctx, rows, facts)
    pairs = n_ctx // 2
    everything = HEADS * rows
    odd_backs = range(1, n_ctx, 2)
    del p_own_in, p_even_in

    for i in range(pairs):
        kv_odd[i] = with_ones(kv_passed[i])

    def odd(backs):
        return [kv_odd.at[place.hop(back)] for back in backs]

    def attend_odd(backs, many):
        attend(place, backs, many, q_s, odd(backs), start, level, acc, [p_odd.at[lax.div(back, 2)] for back in backs])

    acc[...] = acc_in[...]
    place.past(odd_backs, attend_odd)

    @pl.when(jnp.logical_not(jnp.max(acc[:, HDIM:]) < 2.0 ** 40))
    def _():
        def each(step):
            @pl.loop(0, place.before + 1)
            def _(back):
                at = place.hop(back)

                @pl.when(back == 0)
                def _():
                    kv_now[...] = kv_own[...]

                @pl.when(lax.rem(back, 2) == 1)
                def _():
                    kv_now[...] = kv_odd[at]

                @pl.when((back > 0) & (lax.rem(back, 2) == 0))
                def _():
                    kv_now[...] = kv_even[at]

                @pl.loop(0, n_ctx)
                def _(c):
                    here = pl.ds(c * HEADS * size, HEADS * size)
                    tokens = pl.ds(c * size, size)
                    key = place.base - back * rows + lax.broadcasted_iota(jnp.int32, (size, rows), 1)
                    query = place.base + c * size + lax.broadcasted_iota(jnp.int32, (size, rows), 0)
                    off = jnp.where((key >= start[tokens, :]) & (key <= query), 0.0, NEG_FILL)
                    s = dot(q_s[here, :], kv_now[:, :HDIM], NT) * EXP2_SCALE
                    step(here, (s.reshape(HEADS, size, rows) + off[None]).reshape(HEADS * size, rows))

                if step is replace:
                    half = lax.div(back, 2)
                    for fits, target in ((back == 0, p_own), (lax.rem(back, 2) == 1, p_odd.at[half]),
                                         ((back > 0) & (lax.rem(back, 2) == 0), p_even.at[jnp.maximum(half - 1, 0)])):

                        @pl.when(fits)
                        def _():
                            copy = pltpu.make_async_copy(p_new, target, sems.at[0])
                            copy.start()
                            copy.wait()

        def highest(here, s):
            top[here, :] = jnp.maximum(top[here, :], row_max(fold(s)))

        def replace(here, s):
            p = jnp.exp2(s - wide(top[here, :])).astype(BF16)
            p_new[here, :] = p
            acc[here, :] += dot(p, kv_now[:, HDIM:])

        @pl.loop(0, n_ctx)
        def _(c):
            here = pl.ds(c * HEADS * size, HEADS * size)
            top[here, :] = jnp.full((HEADS * size, HDIM), NEG_FILL, F32)
            acc[here, :] = jnp.zeros((HEADS * size, 2 * HDIM), F32)

        each(highest)
        each(replace)

    for i in range(0, everything, rows):
        here = pl.ds(i, rows)
        total = acc[here, :]
        inverse = 1.0 / total[:, HDIM:]
        out = (total[:, :HDIM] * inverse).astype(BF16)
        grad = do_r[here, :].astype(F32)
        corr[here, :] = jnp.sum(grad * out.astype(F32), axis=1, keepdims=True) * inverse
        scaled = grad * inverse
        do_s[here, :] = scaled.astype(BF16)
        do_t[:, here] = scaled.T.astype(BF16)
        for part, there in chunks(rows, n_ctx):
            if i <= part.start < i + rows:
                o_ref[there] = out[part.start - i:part.start - i + size, :]

    leaving = pltpu.make_async_copy(o_ref, o_hbm, sems.at[1])
    leaving.start()

    def backward(backs, many):
        ps = [p_odd[lax.div(back, 2), :many, :] for back in backs]
        for back, (ds, terms) in zip(backs, gradients(many, q_t, do_s, do_t, ps, odd(backs), corr)):
            ds_odd[lax.div(back, 2), :many, :] = ds
            g_passed[place.hop(back)] = terms.astype(BF16)

    done = place.past(odd_backs, backward)

    @pl.loop(done, pairs)
    def _(i):
        g_passed[place.hop(2 * i + 1)] = jnp.zeros((rows, 2 * HDIM), BF16)

    leaving.wait()


def even(n_ctx, facts, q_t, do_s, do_t, kv_even, p_even, corr, ds_even, g_direct):
    rows = kv_even.shape[1]
    place = Place(n_ctx, rows, facts)

    def backward(backs, many):
        ps = [p_even[lax.div(back, 2) - 1, :many, :] for back in backs]
        kvs = [kv_even.at[place.hop(back)] for back in backs]
        for back, (ds, terms) in zip(backs, gradients(many, q_t, do_s, do_t, ps, kvs, corr)):
            ds_even[lax.div(back, 2) - 1, :many, :] = ds
            g_direct[place.hop(back) - 1] = terms

    done = place.past(range(2, n_ctx, 2), backward)

    @pl.loop(done, n_ctx // 2 - 1)
    def _(i):
        g_direct[place.hop(2 * i + 2) - 1] = jnp.zeros((rows, 2 * HDIM), F32)


def rest(n_ctx, facts, q_t, do_s, do_t, kv_even, p_even, corr, kv_own, p_own, kv_odd, ds_odd, ds_even,
         dq_ref, g_own, g_prev, dq_acc):
    rows = kv_own.shape[0]
    place = Place(n_ctx, rows, facts)

    (ds, g_own[...]), = gradients(HEADS * rows, q_t, do_s, do_t, [p_own[...]], [kv_own], corr)
    dq_acc[...] = dot(ds, kv_own[:, :HDIM])

    def add(backs, many, ds, kv):
        dq_acc[:many, :] += dot(side_by_side([ds(back)[:many, :] for back in backs], 1),
                                side_by_side([kv[place.hop(back), :, :HDIM] for back in backs], 0))

    def add_odd(backs, many):
        add(backs, many, lambda back: ds_odd.at[lax.div(back, 2)], kv_odd)

    def add_even(backs, many):
        add(backs, many, lambda back: ds_even.at[lax.div(back, 2) - 1], kv_even)

    def farthest(backs, many):
        at = place.hop(backs[0])
        (ds, g_prev[...]), = gradients(many, q_t, do_s, do_t, [p_even[n_ctx // 2 - 1, :many, :]], [kv_even.at[at]], corr)
        dq_acc[:many, :] += dot(ds, kv_even[at, :, :HDIM])

    place.past(range(1, n_ctx, 2), add_odd)
    place.past(range(2, n_ctx, 2), add_even)
    g_prev[...] = jnp.zeros(g_prev.shape, F32)
    place.past(range(n_ctx, n_ctx + 1), farthest)

    for here, there in chunks(rows, n_ctx):
        dq_ref[there] = (dq_acc[here, :] * SCALE).astype(BF16)


def finish(total, last, gk_ref, gv_ref):
    terms = total[...] + last[...].astype(F32)
    gk_ref[...] = (terms[:, :HDIM] * SCALE).astype(BF16)
    gv_ref[...] = terms[:, HDIM:].astype(BF16)


def size_of(arrays):
    return sum(math.prod(array.shape) * jnp.dtype(array.dtype).itemsize for array in arrays)


def call(body, name, outs, args, scratch, flops, resident, aliases=(), away=(), leaves=(), copies=0):
    vmem = pl.BlockSpec(memory_space=pltpu.VMEM)
    anywhere = pl.BlockSpec(memory_space=pl.ANY)
    hbm = pl.BlockSpec(memory_space=pltpu.HBM)
    outs = tuple(jax.ShapeDtypeStruct(shape, dtype) for shape, dtype in outs)
    held = size_of(scratch) + 8 * 2**20
    if not resident:
        held = min(held + size_of(outs) + size_of(args), 62 * 2**20)
    in_specs, out_specs = [vmem] * len(args), [vmem] * len(outs)
    for i in away:
        in_specs[i] = hbm
    for o in leaves:
        out_specs[o] = hbm
    for i, o in aliases:
        in_specs[i] = out_specs[o] = anywhere
    return pl.pallas_call(
        body,
        out_shape=outs,
        in_specs=in_specs,
        out_specs=tuple(out_specs),
        scratch_shapes=scratch + [pltpu.SemaphoreType.DMA((copies,))] * (copies > 0),
        input_output_aliases=dict(aliases),
        compiler_params=pltpu.CompilerParams(vmem_limit_bytes=held),
        cost_estimate=pl.CostEstimate(flops=flops, bytes_accessed=2**20, transcendentals=0),
        name=name,
    )(*(pltpu.with_memory_space_constraint(arg, pltpu.HBM) if i in away else arg for i, arg in enumerate(args)))


def shards(queries, keys, values, grad_out, lengths):
    rows = keys.shape[0]
    n_dp, n_ctx = lax.axis_size("dp"), lax.axis_size("ctx")
    axes = ("dp", "ctx")
    pairs = n_ctx // 2
    ctx = lax.axis_index("ctx")
    many = HEADS * rows
    once = 2 * many * rows * HDIM
    by_row, by_lane = (many, HDIM), (HDIM, many)
    block, kv_ones = (rows, 2 * HDIM), (rows, 3 * HDIM)
    run = functools.partial(call, resident=(n_ctx + 1) * many * rows <= 6 * 2**20)
    def kernel(body, *args, **kwargs):
        return run(functools.partial(body, n_ctx), body.__name__, *args, **kwargs)

    def swap(blocks, flip):
        return lax.ppermute(blocks, axes, flip_route(n_dp, n_ctx, flip))

    later = [ctx < ctx ^ max(2 * i, 1) for i in range(pairs)]

    kv, = run(join, "join", [(block, BF16)], (keys, values), [], 1, away=(0, 1), copies=2)
    prev = lax.ppermute(kv, axes, run_route(n_dp, n_ctx))
    facts, kv_own, q_s, q_t, do_r, start, level, p_own, acc = kernel(
        prepare, [((8, HDIM), jnp.int32), (kv_ones, BF16), (by_row, BF16), (by_lane, BF16), (by_row, BF16),
                  ((rows, rows), jnp.int32), (by_row, F32), ((many, rows), BF16), ((many, 2 * HDIM), F32)],
        (lengths, queries, grad_out, kv),
        [pltpu.SMEM(lengths.shape, jnp.int32), pltpu.VMEM(queries.shape, BF16), pltpu.VMEM(queries.shape, BF16)], 2 * once,
        away=(0, 1, 2), copies=3)
    ours = kv_own[:, :2 * HDIM]
    sent = [jnp.where(after, ours, prev) for after in later]
    got = [prev] + [swap(sent[i], 2 * i) for i in range(1, pairs)]
    passed = swap(jnp.stack(sent[:1] + got[1:]), 1)
    kv_even, p_even, acc = kernel(
        attend_even, [((pairs,) + kv_ones, BF16), ((pairs, many, rows), BF16), ((many, 2 * HDIM), F32)],
        (facts, q_s, start, level, acc, *got), [], 2 * pairs * once)
    attn_out, kv_odd, ds_odd, do_s, do_t, corr, g_passed, p_own, p_even = kernel(
        forward,
        [(queries.shape, BF16), ((pairs,) + kv_ones, BF16), ((pairs, many, rows), BF16),
         (by_row, BF16), (by_lane, BF16), (by_row, F32), ((pairs,) + block, BF16), (p_own.shape, BF16), (p_even.shape, BF16)],
        (facts, q_s, q_t, do_r, start, level, acc, kv_own, kv_even, passed, p_own, p_even),
        [pltpu.VMEM(queries.shape, BF16), pltpu.VMEM((pairs, many, rows), BF16), pltpu.VMEM((many, 2 * HDIM), F32),
         pltpu.VMEM(by_row, F32), pltpu.VMEM((many, rows), BF16), pltpu.VMEM(kv_ones, BF16)],
        5 * pairs * once, aliases=((10, 7), (11, 8)), leaves=(0,), copies=2)
    partner = swap(g_passed, 1).astype(F32)
    shared = (facts, q_t, do_s, do_t, kv_even, p_even, corr)
    ds_even, g_direct = kernel(even, [((pairs - 1, many, rows), BF16), ((pairs - 1,) + block, F32)],
                               shared, [], 3 * (pairs - 1) * once)
    terms = [partner[0]] + [swap((g_direct[i - 1] + partner[i]).astype(BF16), 2 * i).astype(F32) for i in range(1, pairs)]
    grad_queries, g_own, g_prev = kernel(rest, [(queries.shape, BF16), (block, F32), (block, F32)],
                                         shared + (kv_own, p_own, kv_odd, ds_odd, ds_even),
                                         [pltpu.VMEM(by_row, F32)], (n_ctx + 7) * once)
    own_total, prev_total = g_own, g_prev
    for after, term in zip(later, terms):
        own_total = own_total + jnp.where(after, term, 0.0)
        prev_total = prev_total + jnp.where(after, 0.0, term)
    back = [(b, a) for a, b in run_route(n_dp, n_ctx)]
    last = lax.ppermute(prev_total.astype(BF16), axes, back)
    grad_keys, grad_values = run(finish, "finish", [(keys.shape, BF16), (values.shape, BF16)], (own_total, last), [], 1)
    return (attn_out, grad_queries, grad_keys, grad_values)


def solution(mesh):
    tokens = P(("dp", "ctx"), None)
    return jax.shard_map(
        shards,
        mesh=mesh,
        in_specs=(tokens, tokens, tokens, tokens, P()),
        out_specs=(tokens, tokens, tokens, tokens),
        check_vma=False,
    )
```

profile of v0, /device:TPU:0, one launch (start us, length us, event | category | flops | bytes accessed | tf_op | source)
XLA Modules:
  0.0 47.2 jit_solution(9218706609823724184)
XLA Ops:
  0.6 0.9 %join.1.kv_ref = bf16[256,256]{1,0:T(8,128)(2,1)S(1)} custom-call(bf16[256,128]{1,0:T(8,128)(2,1)} %keys.1, bf16[256,128]{1,0:T(8,128)(2,1)} %values.1), custom_call_target="tpu_custom_call" | custom-call | flops 1 | bytes 1048576 | tf_op jit(solution)/shard_map/join/pallas_call | solution.py:384
  1.5 4.9 %collective-permute-start = (bf16[256,256]{1,0:T(8,128)(2,1)S(1)}, bf16[256,256]{1,0:T(8,128)(2,1)S(1)}, u32[]{:S(2)}, u32[]{:S(2)}) collective-permute-start(bf16[256,256]{1,0:T(8,128)(2,1)S(1)} %join.1.kv_ref), channel_id=1, source_target_pairs={{0,8},{1,9},{2,10},{3,11},{4,12},{5,13},{6,14},{7,15},{8,16},{9,17... | collective-permute-start | bytes 393224 | tf_op jit(solution)/shard_map/ppermute | solution.py:417
  6.5 2.3 %prepare.1 = (s32[8,128]{1,0:T(8,128)S(1)}, bf16[256,384]{1,0:T(8,128)(2,1)S(1)}, bf16[2048,128]{1,0:T(8,128)(2,1)S(1)}, bf16[128,2048]{1,0:T(8,128)(2,1)S(1)}, ...) custom-call(s32[16]{0:T(128)} %lengths_hbm.1, ...), custom_call_target="tpu_custom_call" | custom-call | flops 268435456 | bytes 1048576 | tf_op jit(solution)/shard_map/prepare/pallas_call | solution.py:384
  8.8 0.4 collective-permute-done.refs_0_
  9.2 2.5 %collective-permute-start.3 = (bf16[256,256]{1,0:T(8,128)(2,1)S(1)}, bf16[256,256]{1,0:T(8,128)(2,1)S(1)}, u32[]{:S(2)}, u32[]{:S(2)}) collective-permute-start(bf16[256,256]{1,0:T(8,128)(2,1)S(1)} %get-tuple-element.66), channel_id=1, source_target_pairs={{0,6},{1,7},{2,4},{3,5},{4,2},{5,3},{6,0},{7,1},{8,14},{9,15},{10,... | collective-permute-start | bytes 393224 | tf_op jit(solution)/shard_map/ppermute | solution.py:412
  11.8 0.5 %collective-permute-start.2 = (bf16[256,256]{1,0:T(8,128)(2,1)S(1)}, bf16[256,256]{1,0:T(8,128)(2,1)S(1)}, u32[]{:S(2)}, u32[]{:S(2)}) collective-permute-start(bf16[256,256]{1,0:T(8,128)(2,1)S(1)} %get-tuple-element.67), channel_id=1, source_target_pairs={{0,4},{1,5},{2,6},{3,7},{4,0},{5,1},{6,2},{7,3},{8,12},{9,13},{10,... | collective-permute-start | bytes 393224 | tf_op jit(solution)/shard_map/ppermute | solution.py:412
  12.3 0.5 %collective-permute-start.1 = (bf16[256,256]{1,0:T(8,128)(2,1)S(1)}, bf16[256,256]{1,0:T(8,128)(2,1)S(1)}, u32[]{:S(2)}, u32[]{:S(2)}) collective-permute-start(bf16[256,256]{1,0:T(8,128)(2,1)S(1)} %get-tuple-element.68), channel_id=1, source_target_pairs={{0,2},{1,3},{2,0},{3,1},{4,6},{5,7},{6,4},{7,5},{8,10},{9,11},{10,... | collective-permute-start | bytes 393224 | tf_op jit(solution)/shard_map/ppermute | solution.py:412
  12.8 3.2 %collective-permute-done.3.refs_3_ = bf16[256,256]{1,0:T(8,128)(2,1)S(1)} collective-permute-done((bf16[256,256]{1,0:T(8,128)(2,1)S(1)}, bf16[256,256]{1,0:T(8,128)(2,1)S(1)}, u32[]{:S(2)}, u32[]{:S(2)}) %collective-permute-start.3) | collective-permute-done | bytes 131104 | tf_op jit(solution)/shard_map/ppermute | solution.py:412
  16.0 1.5 %collective-permute-done.2.refs_2_ = bf16[256,256]{1,0:T(8,128)(2,1)S(1)} collective-permute-done((bf16[256,256]{1,0:T(8,128)(2,1)S(1)}, bf16[256,256]{1,0:T(8,128)(2,1)S(1)}, u32[]{:S(2)}, u32[]{:S(2)}) %collective-permute-start.2) | collective-permute-done | bytes 131104 | tf_op jit(solution)/shard_map/ppermute | solution.py:412
  17.5 0.1 collective-permute-done.1.refs_1_
  17.6 0.1 pad_maximum_fusion
  17.7 0.1 collective-permute-start.4
  17.8 0.2 attend_even.1
  18.0 1.6 %collective-permute-done.4.kv_passed = bf16[4,256,256]{2,1,0:T(8,128)(2,1)S(1)} collective-permute-done((bf16[4,256,256]{2,1,0:T(8,128)(2,1)S(1)}, bf16[4,256,256]{2,1,0:T(8,128)(2,1)S(1)}, u32[]{:S(2)}, u32[]{:S(2)}) %collective-permute-start.4) | collective-permute-done | bytes 524320 | tf_op jit(solution)/shard_map/ppermute | solution.py:412
  19.7 1.9 %forward.1 = (bf16[256,1024]{1,0:T(8,128)(2,1)}, bf16[4,256,384]{2,1,0:T(8,128)(2,1)S(1)}, bf16[4,2048,256]{2,1,0:T(8,128)(2,1)S(1)}, bf16[2048,128]{1,0:T(8,128...) custom-call(s32[8,128]{1,0:T(8,128)S(1)} %get-tuple-element.32.facts, ...), custom_call_target="tpu_custom_call", output_to_operand_aliasing={{7}: (10, {}), {8}: (11, {})} | custom-call | flops 2684354560 | bytes 1048576 | tf_op jit(solution)/shard_map/forward/pallas_call | solution.py:384
  21.5 1.6 %collective-permute-start.5 = (bf16[4,256,256]{2,1,0:T(8,128)(2,1)S(1)}, bf16[4,256,256]{2,1,0:T(8,128)(2,1)S(1)}, u32[]{:S(2)}, u32[]{:S(2)}) collective-permute-start(bf16[4,256,256]{2,1,0:T(8,128)(2,1)S(1)} %get-tuple-element.55), channel_id=1, source_target_pairs={{0,1},{1,0},{2,3},{3,2},{4,5},{5,4},{6,7},{7,6},{8,9},{9,8},{10,11... | collective-permute-start | bytes 1572872 | tf_op jit(solution)/shard_map/ppermute | solution.py:412
  23.2 0.1 even.1
  23.3 1.4 %collective-permute-done.5 = bf16[4,256,256]{2,1,0:T(8,128)(2,1)S(1)} collective-permute-done((bf16[4,256,256]{2,1,0:T(8,128)(2,1)S(1)}, bf16[4,256,256]{2,1,0:T(8,128)(2,1)S(1)}, u32[]{:S(2)}, u32[]{:S(2)}) %collective-permute-start.5) | collective-permute-done | bytes 524320 | tf_op jit(solution)/shard_map/ppermute | solution.py:412
  24.7 0.1 convert_element_type.33
  24.8 0.1 fusion.12
  24.9 2.9 %collective-permute-start.8 = (bf16[256,256]{1,0:T(8,128)(2,1)S(1)}, bf16[256,256]{1,0:T(8,128)(2,1)S(1)}, u32[]{:S(2)}, u32[]{:S(2)}) collective-permute-start(bf16[256,256]{1,0:T(8,128)(2,1)S(1)} %get-tuple-element.60), channel_id=1, source_target_pairs={{0,6},{1,7},{2,4},{3,5},{4,2},{5,3},{6,0},{7,1},{8,14},{9,15},{10,... | collective-permute-start | bytes 393224 | tf_op jit(solution)/shard_map/ppermute | solution.py:412
  27.8 0.2 collective-permute-start.7
  28.0 0.5 collective-permute-start.6
  28.5 2.3 %rest.1 = (bf16[256,1024]{1,0:T(8,128)(2,1)}, f32[256,256]{1,0:T(8,128)S(1)}, f32[256,256]{1,0:T(8,128)S(1)}) custom-call(s32[8,128]{1,0:T(8,128)S(1)} %get-tuple-element.32.facts, bf16[128,2048]{1,0:T(8,128)(2,1)S(1)} %get-tuple-element.34.q_t, bf16[2048,128]{1,0:T(8,128)(2,1)S(1)} %get-tuple-element.45.do_s, bf16[128,2048]{1,0:T(8,128)(2,1)S(1)} %get-tuple-element.46.do_t, ...), custom_call_target="tpu_custom_call" | custom-call | flops 2013265920 | bytes 1048576 | tf_op jit(solution)/shard_map/rest/pallas_call | solution.py:384
  30.8 1.1 %collective-permute-done.8 = bf16[256,256]{1,0:T(8,128)(2,1)S(1)} collective-permute-done((bf16[256,256]{1,0:T(8,128)(2,1)S(1)}, bf16[256,256]{1,0:T(8,128)(2,1)S(1)}, u32[]{:S(2)}, u32[]{:S(2)}) %collective-permute-start.8) | collective-permute-done | bytes 131104 | tf_op jit(solution)/shard_map/ppermute | solution.py:412
  31.9 2.7 %collective-permute-done.7 = bf16[256,256]{1,0:T(8,128)(2,1)S(1)} collective-permute-done((bf16[256,256]{1,0:T(8,128)(2,1)S(1)}, bf16[256,256]{1,0:T(8,128)(2,1)S(1)}, u32[]{:S(2)}, u32[]{:S(2)}) %collective-permute-start.7) | collective-permute-done | bytes 131104 | tf_op jit(solution)/shard_map/ppermute | solution.py:412
  34.6 0.0 collective-permute-done.6
  34.7 0.2 fusion.6
  34.8 1.3 %collective-permute-start.9 = (bf16[256,256]{1,0:T(8,128)(2,1)S(1)}, bf16[256,256]{1,0:T(8,128)(2,1)S(1)}, u32[]{:S(2)}, u32[]{:S(2)}) collective-permute-start(bf16[256,256]{1,0:T(8,128)(2,1)S(1)} %get-tuple-element.63), channel_id=1, source_target_pairs={{8,0},{9,1},{10,2},{11,3},{12,4},{13,5},{14,6},{15,7},{16,8},{17,9... | collective-permute-start | bytes 393224 | tf_op jit(solution)/shard_map/ppermute | solution.py:452
  36.1 10.4 %collective-permute-done.9.last = bf16[256,256]{1,0:T(8,128)(2,1)S(1)} collective-permute-done((bf16[256,256]{1,0:T(8,128)(2,1)S(1)}, bf16[256,256]{1,0:T(8,128)(2,1)S(1)}, u32[]{:S(2)}, u32[]{:S(2)}) %collective-permute-start.9) | collective-permute-done | bytes 131104 | tf_op jit(solution)/shard_map/ppermute | solution.py:452
  46.5 0.7 %finish.1 = (bf16[256,128]{1,0:T(8,128)(2,1)}, bf16[256,128]{1,0:T(8,128)(2,1)}) custom-call(f32[256,256]{1,0:T(8,128)S(1)} %get-tuple-element.64.total, bf16[256,256]{1,0:T(8,128)(2,1)S(1)} %collective-permute-done.9.last), custom_call_target="tpu_custom_call" | custom-call | flops 1 | bytes 1048576 | tf_op jit(solution)/shard_map/finish/pallas_call | solution.py:384
  (1 shorter events, 0.0 us)
Async XLA Ops:
  1.5 7.7 %collective-permute-start = (bf16[256,256]{1,0:T(8,128)(2,1)S(1)}, bf16[256,256]{1,0:T(8,128)(2,1)S(1)}, u32[]{:S(2)}, u32[]{:S(2)}) collective-permute-start(bf16[256,256]{1,0:T(8,128)(2,1)S(1)} %join.1.kv_ref), channel_id=1, source_target_pairs={{0,8},{1,9},{2,10},{3,11},{4,12},{5,13},{6,14},{7,15},{8,16},{9,17... | collective-permute-start | bytes 393224 | tf_op jit(solution)/shard_map/ppermute | solution.py:417
  9.2 6.8 %collective-permute-start.3 = (bf16[256,256]{1,0:T(8,128)(2,1)S(1)}, bf16[256,256]{1,0:T(8,128)(2,1)S(1)}, u32[]{:S(2)}, u32[]{:S(2)}) collective-permute-start(bf16[256,256]{1,0:T(8,128)(2,1)S(1)} %get-tuple-element.66), channel_id=1, source_target_pairs={{0,6},{1,7},{2,4},{3,5},{4,2},{5,3},{6,0},{7,1},{8,14},{9,15},{10,... | collective-permute-start | bytes 393224 | tf_op jit(solution)/shard_map/ppermute | solution.py:412
  11.8 5.8 %collective-permute-start.2 = (bf16[256,256]{1,0:T(8,128)(2,1)S(1)}, bf16[256,256]{1,0:T(8,128)(2,1)S(1)}, u32[]{:S(2)}, u32[]{:S(2)}) collective-permute-start(bf16[256,256]{1,0:T(8,128)(2,1)S(1)} %get-tuple-element.67), channel_id=1, source_target_pairs={{0,4},{1,5},{2,6},{3,7},{4,0},{5,1},{6,2},{7,3},{8,12},{9,13},{10,... | collective-permute-start | bytes 393224 | tf_op jit(solution)/shard_map/ppermute | solution.py:412
  12.3 5.4 %collective-permute-start.1 = (bf16[256,256]{1,0:T(8,128)(2,1)S(1)}, bf16[256,256]{1,0:T(8,128)(2,1)S(1)}, u32[]{:S(2)}, u32[]{:S(2)}) collective-permute-start(bf16[256,256]{1,0:T(8,128)(2,1)S(1)} %get-tuple-element.68), channel_id=1, source_target_pairs={{0,2},{1,3},{2,0},{3,1},{4,6},{5,7},{6,4},{7,5},{8,10},{9,11},{10,... | collective-permute-start | bytes 393224 | tf_op jit(solution)/shard_map/ppermute | solution.py:412
  17.7 2.0 %collective-permute-start.4 = (bf16[4,256,256]{2,1,0:T(8,128)(2,1)S(1)}, bf16[4,256,256]{2,1,0:T(8,128)(2,1)S(1)}, u32[]{:S(2)}, u32[]{:S(2)}) collective-permute-start(bf16[4,256,256]{2,1,0:T(8,128)(2,1)S(1)} %pad_maximum_fusion), channel_id=1, source_target_pairs={{0,1},{1,0},{2,3},{3,2},{4,5},{5,4},{6,7},{7,6},{8,9},{9,8},{10,11... | collective-permute-start | bytes 1572872 | tf_op jit(solution)/shard_map/ppermute | solution.py:412
  21.5 3.2 %collective-permute-start.5 = (bf16[4,256,256]{2,1,0:T(8,128)(2,1)S(1)}, bf16[4,256,256]{2,1,0:T(8,128)(2,1)S(1)}, u32[]{:S(2)}, u32[]{:S(2)}) collective-permute-start(bf16[4,256,256]{2,1,0:T(8,128)(2,1)S(1)} %get-tuple-element.55), channel_id=1, source_target_pairs={{0,1},{1,0},{2,3},{3,2},{4,5},{5,4},{6,7},{7,6},{8,9},{9,8},{10,11... | collective-permute-start | bytes 1572872 | tf_op jit(solution)/shard_map/ppermute | solution.py:412
  24.9 7.0 %collective-permute-start.8 = (bf16[256,256]{1,0:T(8,128)(2,1)S(1)}, bf16[256,256]{1,0:T(8,128)(2,1)S(1)}, u32[]{:S(2)}, u32[]{:S(2)}) collective-permute-start(bf16[256,256]{1,0:T(8,128)(2,1)S(1)} %get-tuple-element.60), channel_id=1, source_target_pairs={{0,6},{1,7},{2,4},{3,5},{4,2},{5,3},{6,0},{7,1},{8,14},{9,15},{10,... | collective-permute-start | bytes 393224 | tf_op jit(solution)/shard_map/ppermute | solution.py:412
  27.8 6.8 %collective-permute-start.7 = (bf16[256,256]{1,0:T(8,128)(2,1)S(1)}, bf16[256,256]{1,0:T(8,128)(2,1)S(1)}, u32[]{:S(2)}, u32[]{:S(2)}) collective-permute-start(bf16[256,256]{1,0:T(8,128)(2,1)S(1)} %get-tuple-element.61), channel_id=1, source_target_pairs={{0,4},{1,5},{2,6},{3,7},{4,0},{5,1},{6,2},{7,3},{8,12},{9,13},{10,... | collective-permute-start | bytes 393224 | tf_op jit(solution)/shard_map/ppermute | solution.py:412
  28.0 6.6 %collective-permute-start.6 = (bf16[256,256]{1,0:T(8,128)(2,1)S(1)}, bf16[256,256]{1,0:T(8,128)(2,1)S(1)}, u32[]{:S(2)}, u32[]{:S(2)}) collective-permute-start(bf16[256,256]{1,0:T(8,128)(2,1)S(1)} %get-tuple-element.62), channel_id=1, source_target_pairs={{0,2},{1,3},{2,0},{3,1},{4,6},{5,7},{6,4},{7,5},{8,10},{9,11},{10,... | collective-permute-start | bytes 393224 | tf_op jit(solution)/shard_map/ppermute | solution.py:412
  34.8 11.7 %collective-permute-start.9 = (bf16[256,256]{1,0:T(8,128)(2,1)S(1)}, bf16[256,256]{1,0:T(8,128)(2,1)S(1)}, u32[]{:S(2)}, u32[]{:S(2)}) collective-permute-start(bf16[256,256]{1,0:T(8,128)(2,1)S(1)} %get-tuple-element.63), channel_id=1, source_target_pairs={{8,0},{9,1},{10,2},{11,3},{12,4},{13,5},{14,6},{15,7},{16,8},{17,9... | collective-permute-start | bytes 393224 | tf_op jit(solution)/shard_map/ppermute | solution.py:452
where the time goes:
time: 46.9 us; the launch traced here: 47.2 us
  waiting for transfers between devices  22.5 us (48%)
  starting transfers between devices  15 us (32%)
  Pallas kernels  8.41 us (18%)
  between operations  0.74 us (2%)
  other arithmetic  0.49 us (1%)
    ppermute x8, waiting for transfers between devices, swap(): return lax.ppermute(blocks, axes, flip_route(n_dp, n_ctx, flip))  11.7 us
    ppermute x1, waiting for transfers between devices, shards(): last = lax.ppermute(prev_total.astype(BF16), axes, back)  10.4 us
    ppermute x8, starting transfers between devices, swap(): return lax.ppermute(blocks, axes, flip_route(n_dp, n_ctx, flip))  8.82 us
    pallas_call x7, Pallas kernels, call(): pl.pallas_call(body, out_shape=outs, in_specs=in_specs, out_specs=tuple(o...  8.41 us
    ppermute x1, starting transfers between devices, shards(): prev = lax.ppermute(kv, axes, run_route(n_dp, n_ctx))  4.94 us
    ppermute x1, starting transfers between devices, shards(): last = lax.ppermute(prev_total.astype(BF16), axes, back)  1.29 us
  transfers between devices with their start and end apart: 10, of which 9 were waited for; matrix products, arithmetic and copies ran while one was open for 0% of the time, Pallas kernels for 11%

commit v1 on v0

v1 whole, which is shorter than its diff:
```python
import functools
import math

import jax
import jax.numpy as jnp
from jax import lax
from jax.experimental import pallas as pl
from jax.experimental.pallas import tpu as pltpu
from jax.sharding import PartitionSpec as P

HEADS = 8
HDIM = 128
NEG_FILL = -1e30
SCALE = float(HDIM) ** -0.5
EXP2_SCALE = SCALE * math.log2(math.e)

NT = (((1,), (1,)), ((), ()))
NN = (((1,), (0,)), ((), ()))
F32, BF16 = jnp.float32, jnp.bfloat16


def dot(a, b, dims=NN):
    return lax.dot_general(a, b, dims, preferred_element_type=F32)


def wide(column):
    return jnp.concatenate([column, column], axis=1)


def run_route(n_dp, n_ctx):
    return [(d * n_ctx + c, (d + 1) * n_ctx + c) for d in range(n_dp - 1) for c in range(n_ctx)]


def flip_route(n_dp, n_ctx, flip):
    return [(d * n_ctx + c, d * n_ctx + (c ^ flip)) for d in range(n_dp) for c in range(n_ctx)]


class Flips:
    def __init__(self, n_ctx):
        even = range(2, n_ctx, 2)
        self.near = [flip for flip in even if flip & (flip - 1) == 0]
        self.far = [flip for flip in even if flip & (flip - 1) != 0]
        self.even = self.near + self.far
        self.first = [0] + self.near
        self.passed = [1] + [flip + 1 for flip in self.near]
        self.second = self.far + self.passed
        self.last = [flip + 1 for flip in self.far]
        self.odd = self.passed + self.last


def facts_of(n_ctx, rows, index, lengths_ref):
    base = index * rows
    ends, end = [], jnp.int32(0)
    for i in range(lengths_ref.shape[0]):
        end = end + lengths_ref[i]
        ends.append(end)
    low, high = jnp.int32(0), ends[-1]
    for end in ends:
        low = jnp.where(end <= base, end, low)
    for end in reversed(ends):
        high = jnp.where(end > base, end, high)
    before = lax.div(base - low + rows - 1, rows)
    short = (high - base <= rows - rows // n_ctx).astype(jnp.int32)
    return (lax.rem(index, n_ctx), base, before, short), ends


class Place:
    def __init__(self, n_ctx, rows, facts):
        self.n_ctx, self.rows = n_ctx, rows
        self.ctx, self.base, self.before, short = facts if isinstance(facts, tuple) else (facts[i, 0] for i in range(4))
        self.short = short == 1

    def back(self, flip):
        back = lax.rem(self.ctx - (self.ctx ^ flip) + 2 * self.n_ctx, self.n_ctx)
        return jnp.where(back == 0, self.n_ctx, back)

    def needed(self, flip):
        return self.back(flip) <= self.before

    def past(self, flips, body):
        backs = [self.back(flip) for flip in flips]
        needed = [(back <= self.before).astype(jnp.int32) for back in backs]
        count = sum(needed)

        def pick(k):
            at, back, seen = jnp.int32(0), jnp.int32(0), jnp.int32(0)
            for i in range(len(flips)):
                here = (needed[i] == 1) & (seen == k)
                at, back = jnp.where(here, i, at), jnp.where(here, backs[i], back)
                seen = seen + needed[i]
            return at, back

        for short in (True, False):
            many = HEADS * (self.rows - self.rows // self.n_ctx if short else self.rows)
            fits = self.short if short else jnp.logical_not(self.short)

            if len(flips) > 1:

                @pl.when(fits)
                def _():
                    @pl.loop(0, lax.div(count, 2))
                    def _(i):
                        body(*zip(pick(2 * i), pick(2 * i + 1)), many)

            @pl.when(fits & (lax.rem(count, 2) == 1))
            def _():
                body(*zip(pick(count - 1)), many)


def chunks(rows, n_ctx):
    size = rows // n_ctx
    for c in range(n_ctx):
        for h in range(HEADS):
            yield (pl.ds((c * HEADS + h) * size, size), (pl.ds(c * size, size), pl.ds(h * HDIM, HDIM)))


def fetch(pairs, sems):
    copies = [pltpu.make_async_copy(source, target, sems.at[i]) for i, (source, target) in enumerate(pairs)]
    for copy in copies:
        copy.start()
    return copies


def join(keys, values, kv, sems):
    for copy in fetch([(keys, kv.at[:, pl.ds(0, HDIM)]), (values, kv.at[:, pl.ds(HDIM, HDIM)])], sems):
        copy.wait()


def ones_beside(values):
    return jnp.concatenate([values, jnp.ones(values.shape, BF16)], axis=1)


def side_by_side(parts, axis):
    return parts[0] if len(parts) == 1 else jnp.concatenate(parts, axis=axis)


def offsets(place, back, first, tokens, start):
    shape = (tokens, place.rows)
    key = place.base - back * place.rows + lax.broadcasted_iota(jnp.int32, shape, 1)
    query = place.base + first + lax.broadcasted_iota(jnp.int32, shape, 0)
    return jnp.where((key >= start[pl.ds(first, tokens), :]) & (key <= query), 0.0, NEG_FILL)


def levels(place, back, many, q_s, key_block, start):
    size, rows = place.rows // place.n_ctx, place.rows
    tokens = many // HEADS
    off = offsets(place, back, 0, tokens, start)
    s = dot(q_s[:many, :], key_block, NT) * EXP2_SCALE
    s = s.reshape(tokens // size, HEADS, size, rows) + off.reshape(tokens // size, 1, size, rows)
    return s.reshape(many, rows)


def fold(s):
    return jnp.maximum(s[:, :HDIM], s[:, HDIM:])


def row_max(s):
    return jnp.broadcast_to(jnp.max(s, axis=1, keepdims=True), (s.shape[0], HDIM))


def prepare(n_ctx, lengths_hbm, q_hbm, do_hbm, kv_ref, facts_ref, kv_own, q_s, q_t, do_r, start, level, p_own, acc,
            lengths_ref, q_ref, do_ref, sems):
    copies = fetch([(lengths_hbm, lengths_ref), (q_hbm, q_ref), (do_hbm, do_ref)], sems)
    rows = q_ref.shape[0]
    index = lax.axis_index("dp") * n_ctx + lax.axis_index("ctx")
    kv_own[...] = kv_ref[...]
    copies[0].wait()
    facts, ends = facts_of(n_ctx, rows, index, lengths_ref)
    place = Place(n_ctx, rows, facts)
    line = lax.broadcasted_iota(jnp.int32, facts_ref.shape, 0)
    held = jnp.zeros(facts_ref.shape, jnp.int32)
    for i, fact in enumerate(facts):
        held = jnp.where(line == i, fact, held)
    facts_ref[...] = held
    token = place.base + lax.broadcasted_iota(jnp.int32, (rows, HDIM), 0)
    begin = jnp.zeros((rows, HDIM), jnp.int32)
    for end in ends:
        begin = jnp.where(token >= end, end, begin)
    start[...] = wide(begin) if rows == 2 * HDIM else jnp.broadcast_to(begin[:, :1], (rows, rows))
    copies[1].wait()
    for here, there in chunks(rows, n_ctx):
        q_s[here, :] = q_ref[there]
    s = levels(place, 0, HEADS * rows, q_s, kv_own[:, :HDIM], start)
    top = row_max(fold(s))
    level[...] = top
    p = jnp.exp2(s - wide(top)).astype(BF16)
    p_own[...] = p
    acc[...] = dot(p, ones_beside(kv_own[:, HDIM:]))
    copies[2].wait()
    for here, there in chunks(rows, n_ctx):
        do_r[here, :] = do_ref[there]
    for h in range(HEADS):
        here = pl.ds(h * rows, rows)
        q_t[:, here] = q_s[here, :].T


def attend(place, backs, many, q_s, kvs, start, level, source, acc, probs):
    scores = [levels(place, back, many, q_s, kv[:, :HDIM], start) for back, kv in zip(backs, kvs)]
    p = [jnp.exp2(s - wide(level[:many, :])).astype(BF16) for s in scores]
    for ref, part in zip(probs, p):
        ref[:many, :] = part
    acc[:many, :] = source[:many, :] + dot(side_by_side(p, 1), side_by_side([ones_beside(kv[:, HDIM:]) for kv in kvs], 0))


def attend_first(n_ctx, facts, q_s, start, level, acc_in, *refs):
    *got, kvs, probs, acc, facts_out = refs
    facts_out[...] = facts[...]
    place = Place(n_ctx, got[0].shape[0], facts)
    for i, ref in enumerate(got):
        kvs[i] = ref[...]
    acc[...] = acc_in[...]
    place.past(Flips(n_ctx).first, lambda at, backs, many: attend(
        place, backs, many, q_s, [kvs.at[i] for i in at], start, level, acc, acc, [probs.at[i] for i in at]))


def attend_second(n_ctx, facts, q_s, start, level, acc_in, *refs):
    *got, passed, kvs, probs, acc = refs
    place = Place(n_ctx, passed.shape[1], facts)
    for i, ref in enumerate(got):
        kvs[i] = ref[...]
    for i in range(passed.shape[0]):
        kvs[len(got) + i] = passed[i]
    acc[...] = acc_in[...]
    place.past(Flips(n_ctx).second, lambda at, backs, many: attend(
        place, backs, many, q_s, [kvs.at[i] for i in at], start, level, acc, acc, [probs.at[i] for i in at]))


def settle(n_ctx, facts, q_s, do_r, start, level, acc_in, kv_own, kv_first, kv_second, kv_last, p_own_in, p_first_in, p_second_in,
           o_ref, do_s, do_t, corr, p_last, p_own, p_first, p_second, acc, top, p_new, kv_now, sems):
    rows = o_ref.shape[0]
    size = rows // n_ctx
    place = Place(n_ctx, rows, facts)
    flips = Flips(n_ctx)
    everything = HEADS * rows
    del p_own_in, p_first_in, p_second_in

    if len(flips.last) == 1:

        def add_last(at, backs, many):
            attend(place, backs, many, q_s, [kv_last.at[0]], start, level, acc_in, acc, [p_last.at[0]])
            if many < everything:
                acc[many:, :] = acc_in[many:, :]

        place.past(flips.last, add_last)

        @pl.when(jnp.logical_not(place.needed(flips.last[0])))
        def _():
            acc[...] = acc_in[...]

    else:
        acc[...] = acc_in[...]
        place.past(flips.last, lambda at, backs, many: attend(
            place, backs, many, q_s, [kv_last.at[i] for i in at], start, level, acc, acc, [p_last.at[i] for i in at]))

    @pl.when(jnp.logical_not(jnp.max(acc[:, HDIM:]) < 2.0 ** 40))
    def _():
        def block(back, step):
            @pl.loop(0, n_ctx)
            def _(c):
                here = pl.ds(c * HEADS * size, HEADS * size)
                off = offsets(place, back, c * size, size, start)
                s = dot(q_s[here, :], kv_now[:, :HDIM], NT) * EXP2_SCALE
                step(here, (s.reshape(HEADS, size, rows) + off[None]).reshape(HEADS * size, rows))

        def store(target):
            copy = pltpu.make_async_copy(p_new, target, sems.at[0])
            copy.start()
            copy.wait()

        def each(step):
            kv_now[...] = kv_own[...]
            block(0, step)
            if step is replace:
                store(p_own)
            for group, kvs, probs in ((flips.first, kv_first, p_first), (flips.second, kv_second, p_second),
                                      (flips.last, kv_last, p_last)):

                @pl.loop(0, len(group))
                def _(i):
                    flip = sum(jnp.where(i == k, group[k], 0) for k in range(len(group)))

                    @pl.when(place.needed(flip))
                    def _():
                        kv_now[...] = kvs[i]
                        block(place.back(flip), step)
                        if step is replace:
                            store(probs.at[i])

        def highest(here, s):
            top[here, :] = jnp.maximum(top[here, :], row_max(fold(s)))

        def replace(here, s):
            p = jnp.exp2(s - wide(top[here, :])).astype(BF16)
            p_new[here, :] = p
            acc[here, :] += dot(p, ones_beside(kv_now[:, HDIM:]))

        @pl.loop(0, n_ctx)
        def _(c):
            here = pl.ds(c * HEADS * size, HEADS * size)
            top[here, :] = jnp.full((HEADS * size, HDIM), NEG_FILL, F32)
            acc[here, :] = jnp.zeros((HEADS * size, 2 * HDIM), F32)

        each(highest)
        each(replace)

    for i in range(0, everything, rows):
        here = pl.ds(i, rows)
        total = acc[here, :]
        inverse = 1.0 / total[:, HDIM:]
        out = (total[:, :HDIM] * inverse).astype(BF16)
        grad = do_r[here, :].astype(F32)
        corr[here, :] = jnp.sum(grad * out.astype(F32), axis=1, keepdims=True) * inverse
        scaled = grad * inverse
        do_s[here, :] = scaled.astype(BF16)
        do_t[:, here] = scaled.T.astype(BF16)
        for part, there in chunks(rows, n_ctx):
            if i <= part.start < i + rows:
                o_ref[there] = out[part.start - i:part.start - i + size, :]


def gradients(many, q_t, do_s, do_t, ps, kvs, corr):
    d = [dot(do_s[:many, :], kv[:, HDIM:], NT) for kv in kvs]
    dv = [dot(do_t[:, :many], p) for p in ps]
    ds = [(p.astype(F32) * (each - wide(corr[:many, :]))).astype(BF16) for p, each in zip(ps, d)]
    dk = [dot(q_t[:, :many], each) for each in ds]
    return [(each, jnp.concatenate([k.T, v.T], axis=1)) for each, k, v in zip(ds, dk, dv)]


def backward(place, groups, q_t, do_s, do_t, corr, ds, out):
    done = 0
    for flips, kvs, probs, first in groups:

        def body(at, backs, many):
            ps = [probs[first + i, :many, :] for i in at]
            for i, (each, terms) in zip(at, gradients(many, q_t, do_s, do_t, ps, [kvs.at[first + i] for i in at], corr)):
                ds[done + i, :many, :] = each
                out[done + i] = terms.astype(out.dtype)

        place.past(flips, body)
        for i, flip in enumerate(flips):

            @pl.when(jnp.logical_not(place.needed(flip)))
            def _():
                out[done + i] = jnp.zeros(out.shape[1:], out.dtype)

        done += len(flips)


def odd(n_ctx, facts, q_t, do_s, do_t, corr, kv_second, kv_last, p_second, p_last, o_ref, o_hbm, ds_odd, g_passed, sems):
    copies = fetch([(o_ref, o_hbm)], sems)
    flips = Flips(n_ctx)
    backward(Place(n_ctx, o_ref.shape[0], facts),
             ((flips.passed, kv_second, p_second, len(flips.far)), (flips.last, kv_last, p_last, 0)),
             q_t, do_s, do_t, corr, ds_odd, g_passed)
    copies[0].wait()


def even(n_ctx, facts, q_t, do_s, do_t, corr, kv_first, kv_second, p_first, p_second, ds_even, g_direct):
    flips = Flips(n_ctx)
    backward(Place(n_ctx, kv_first.shape[1], facts),
             ((flips.near, kv_first, p_first, 1), (flips.far, kv_second, p_second, 0)),
             q_t, do_s, do_t, corr, ds_even, g_direct)


def rest(n_ctx, facts, q_t, do_s, do_t, corr, kv_own, kv_first, kv_second, kv_last, p_own, p_first, ds_odd, ds_even,
         dq_ref, g_own, g_prev, dq_acc, k_odd, k_even):
    rows = kv_own.shape[0]
    place = Place(n_ctx, rows, facts)
    flips = Flips(n_ctx)
    (ds, g_own[...]), = gradients(HEADS * rows, q_t, do_s, do_t, [p_own[...]], [kv_own], corr)
    dq_acc[...] = dot(ds, kv_own[:, :HDIM])
    for i in range(len(flips.odd)):
        k_odd[i] = (kv_second[len(flips.far) + i] if i < len(flips.passed) else kv_last[i - len(flips.passed)])[:, :HDIM]
    for i in range(len(flips.even)):
        k_even[i] = (kv_first[1 + i] if i < len(flips.near) else kv_second[i - len(flips.near)])[:, :HDIM]

    for group, ds, keys in ((flips.odd, ds_odd, k_odd), (flips.even, ds_even, k_even)):

        def add(at, backs, many):
            dq_acc[:many, :] += dot(side_by_side([ds[i, :many, :] for i in at], 1), side_by_side([keys[i] for i in at], 0))

        place.past(group, add)

    def farthest(at, backs, many):
        (ds, g_prev[...]), = gradients(many, q_t, do_s, do_t, [p_first[0, :many, :]], [kv_first.at[0]], corr)
        dq_acc[:many, :] += dot(ds, kv_first[0, :, :HDIM])

    g_prev[...] = jnp.zeros(g_prev.shape, F32)
    place.past([0], farthest)

    for here, there in chunks(rows, n_ctx):
        dq_ref[there] = (dq_acc[here, :] * SCALE).astype(BF16)


def finish(total, last, gk_ref, gv_ref):
    terms = total[...] + last[...].astype(F32)
    gk_ref[...] = (terms[:, :HDIM] * SCALE).astype(BF16)
    gv_ref[...] = terms[:, HDIM:].astype(BF16)


def size_of(arrays):
    return sum(math.prod(array.shape) * jnp.dtype(array.dtype).itemsize for array in arrays)


def call(body, name, outs, args, scratch, flops, resident, aliases=(), away=(), leaves=(), copies=0):
    vmem = pl.BlockSpec(memory_space=pltpu.VMEM)
    anywhere = pl.BlockSpec(memory_space=pl.ANY)
    hbm = pl.BlockSpec(memory_space=pltpu.HBM)
    outs = tuple(jax.ShapeDtypeStruct(shape, dtype) for shape, dtype in outs)
    held = size_of(scratch) + 8 * 2**20
    if not resident:
        held = min(held + size_of(outs) + size_of(args), 62 * 2**20)
    in_specs, out_specs = [vmem] * len(args), [vmem] * len(outs)
    for i in away:
        in_specs[i] = hbm
    for o in leaves:
        out_specs[o] = hbm
    for i, o in aliases:
        in_specs[i] = out_specs[o] = anywhere
    return pl.pallas_call(
        body,
        out_shape=outs,
        in_specs=in_specs,
        out_specs=tuple(out_specs),
        scratch_shapes=scratch + [pltpu.SemaphoreType.DMA((copies,))] * (copies > 0),
        input_output_aliases=dict(aliases),
        compiler_params=pltpu.CompilerParams(vmem_limit_bytes=held),
        cost_estimate=pl.CostEstimate(flops=flops, bytes_accessed=2**20, transcendentals=0),
        name=name,
    )(*(pltpu.with_memory_space_constraint(arg, pltpu.HBM) if i in away else arg for i, arg in enumerate(args)))


def shards(queries, keys, values, grad_out, lengths):
    rows = keys.shape[0]
    n_dp, n_ctx = lax.axis_size("dp"), lax.axis_size("ctx")
    axes = ("dp", "ctx")
    flips = Flips(n_ctx)
    ctx = lax.axis_index("ctx")
    many = HEADS * rows
    once = 2 * many * rows * HDIM
    by_row, by_lane = (many, HDIM), (HDIM, many)
    block, pairs = (rows, 2 * HDIM), (many, rows)
    run = functools.partial(call, resident=(n_ctx + 1) * many * rows <= 6 * 2**20)

    def kernel(body, *args, **kwargs):
        return run(functools.partial(body, n_ctx), body.__name__, *args, **kwargs)

    def several(group, shape):
        return ((len(group),) + shape, BF16)

    def swap(blocks, flip):
        return lax.ppermute(blocks, axes, flip_route(n_dp, n_ctx, flip))

    def after(flip):
        return ctx < ctx ^ flip

    kv, = run(join, "join", [(block, BF16)], (keys, values), [], 1, away=(0, 1), copies=2)
    prev = lax.ppermute(kv, axes, run_route(n_dp, n_ctx))
    facts, kv_own, q_s, q_t, do_r, start, level, p_own, acc = kernel(
        prepare, [((8, HDIM), jnp.int32), (block, BF16), (by_row, BF16), (by_lane, BF16), (by_row, BF16),
                  ((rows, rows), jnp.int32), (by_row, F32), (pairs, BF16), ((many, 2 * HDIM), F32)],
        (lengths, queries, grad_out, kv),
        [pltpu.SMEM(lengths.shape, jnp.int32), pltpu.VMEM(queries.shape, BF16), pltpu.VMEM(queries.shape, BF16)], 2 * once,
        away=(0, 1, 2), copies=3)
    got = {flip: swap(jnp.where(after(flip), kv_own, prev), flip) for flip in flips.even}
    passed = swap(jnp.stack([jnp.where(after(1), kv_own, prev)] + [got[flip] for flip in flips.near]), 1)
    kv_first, p_first, acc, facts = kernel(
        attend_first, [several(flips.first, block), several(flips.first, pairs), ((many, 2 * HDIM), F32), (facts.shape, jnp.int32)],
        (facts, q_s, start, level, acc, prev) + tuple(got[flip] for flip in flips.near), [], 2 * len(flips.first) * once)
    kv_last = swap(jnp.where(facts[0, 0] < n_ctx, jnp.stack([got[flip] for flip in flips.far]), 0), 1)
    kv_second, p_second, acc = kernel(
        attend_second, [several(flips.second, block), several(flips.second, pairs), ((many, 2 * HDIM), F32)],
        (facts, q_s, start, level, acc) + tuple(got[flip] for flip in flips.far) + (passed,), [], 2 * len(flips.second) * once)
    out, do_s, do_t, corr, p_last, p_own, p_first, p_second = kernel(
        settle,
        [(queries.shape, BF16), (by_row, BF16), (by_lane, BF16), (by_row, F32), several(flips.last, pairs), (pairs, BF16),
         (p_first.shape, BF16), (p_second.shape, BF16)],
        (facts, q_s, do_r, start, level, acc, kv_own, kv_first, kv_second, kv_last, p_own, p_first, p_second),
        [pltpu.VMEM((many, 2 * HDIM), F32), pltpu.VMEM(by_row, F32), pltpu.VMEM(pairs, BF16), pltpu.VMEM(block, BF16)],
        2 * len(flips.last) * once, aliases=((10, 5), (11, 6), (12, 7)), copies=1)
    shared = (facts, q_t, do_s, do_t, corr)
    attn_out, ds_odd, g_passed = kernel(
        odd, [(queries.shape, BF16), several(flips.odd, pairs), several(flips.odd, block)],
        shared + (kv_second, kv_last, p_second, p_last, out), [], 3 * len(flips.odd) * once, leaves=(0,), copies=1)
    partner = swap(g_passed, 1).astype(F32)
    ds_even, g_direct = kernel(
        even, [several(flips.even, pairs), ((len(flips.even),) + block, F32)],
        shared + (kv_first, kv_second, p_first, p_second), [], 3 * len(flips.even) * once)
    terms = [(1, partner[0])]
    for i, flip in enumerate(flips.even):
        terms.append((flip, swap((g_direct[i] + partner[i + 1]).astype(BF16), flip).astype(F32)))
    grad_queries, g_own, g_prev = kernel(
        rest, [(queries.shape, BF16), (block, F32), (block, F32)],
        shared + (kv_own, kv_first, kv_second, kv_last, p_own, p_first, ds_odd, ds_even),
        [pltpu.VMEM(by_row, F32), pltpu.VMEM((len(flips.odd), rows, HDIM), BF16), pltpu.VMEM((len(flips.even), rows, HDIM), BF16)],
        (n_ctx + 7) * once)
    own_total, prev_total = g_own, g_prev
    for flip, term in terms:
        own_total = own_total + jnp.where(after(flip), term, 0.0)
        prev_total = prev_total + jnp.where(after(flip), 0.0, term)
    back = [(b, a) for a, b in run_route(n_dp, n_ctx)]
    last = lax.ppermute(prev_total.astype(BF16), axes, back)
    grad_keys, grad_values = run(finish, "finish", [(keys.shape, BF16), (values.shape, BF16)], (own_total, last), [], 1)
    return (attn_out, grad_queries, grad_keys, grad_values)


def solution(mesh):
    tokens = P(("dp", "ctx"), None)
    return jax.shard_map(
        shards,
        mesh=mesh,
        in_specs=(tokens, tokens, tokens, tokens, P()),
        out_specs=(tokens, tokens, tokens, tokens),
        check_vma=False,
    )
```

time: 46.9 us -> 50.5 us (1.077)
  the two profiles are of different devices: /device:TPU:0 before, /device:TPU:16 now
where the time goes in v1:
time: 50.5 us; the launch traced here: 50.6 us
  waiting for transfers between devices  20.1 us (40%)
  starting transfers between devices  17.9 us (35%)
  Pallas kernels  10.2 us (20%)
  between operations  1.44 us (3%)
  local copies, waits for them, and re-layouts  0.51 us (1%)
    ppermute x9, waiting for transfers between devices, swap(): return lax.ppermute(blocks, axes, flip_route(n_dp, n_ctx, flip))  13.4 us
    ppermute x9, starting transfers between devices, swap(): return lax.ppermute(blocks, axes, flip_route(n_dp, n_ctx, flip))  12.5 us
    pallas_call x9, Pallas kernels, call(): pl.pallas_call(body, out_shape=outs, in_specs=in_specs, out_specs=tuple(o...  10.2 us
    ppermute x1, waiting for transfers between devices, shards(): last = lax.ppermute(prev_total.astype(BF16), axes, back)  5.38 us
    ppermute x1, starting transfers between devices, shards(): prev = lax.ppermute(kv, axes, run_route(n_dp, n_ctx))  3.48 us
    ppermute x1, starting transfers between devices, shards(): last = lax.ppermute(prev_total.astype(BF16), axes, back)  1.92 us
    ppermute x1, waiting for transfers between devices, shards(): prev = lax.ppermute(kv, axes, run_route(n_dp, n_ctx))  1.35 us
  transfers between devices with their start and end apart: 11, of which 9 were waited for; matrix products, arithmetic and copies ran while one was open for 1% of the time, Pallas kernels for 11%

profile of v1, /device:TPU:16, one launch (start us, length us, event | category | flops | bytes accessed | tf_op | source)
XLA Modules:
  0.0 50.6 jit_solution(15345270739417850947)
XLA Ops:
  0.6 0.9 %join.1.kv_ref = bf16[256,256]{1,0:T(8,128)(2,1)S(1)} custom-call(bf16[256,128]{1,0:T(8,128)(2,1)} %keys.1, bf16[256,128]{1,0:T(8,128)(2,1)} %values.1), custom_call_target="tpu_custom_call" | custom-call | flops 1 | bytes 1048576 | tf_op jit(solution)/shard_map/join/pallas_call | solution.py:420
  1.5 3.5 %collective-permute-start = (bf16[256,256]{1,0:T(8,128)(2,1)S(1)}, bf16[256,256]{1,0:T(8,128)(2,1)S(1)}, u32[]{:S(2)}, u32[]{:S(2)}) collective-permute-start(bf16[256,256]{1,0:T(8,128)(2,1)S(1)} %join.1.kv_ref), channel_id=1, source_target_pairs={{0,8},{1,9},{2,10},{3,11},{4,12},{5,13},{6,14},{7,15},{8,16},{9,17... | collective-permute-start | bytes 393224 | tf_op jit(solution)/shard_map/ppermute | solution.py:458
  5.0 2.3 %prepare.1 = (s32[8,128]{1,0:T(8,128)S(1)}, bf16[256,256]{1,0:T(8,128)(2,1)S(1)}, bf16[2048,128]{1,0:T(8,128)(2,1)S(1)}, bf16[128,2048]{1,0:T(8,128)(2,1)S(1)}, ...) custom-call(s32[16]{0:T(128)} %lengths_hbm.1, ...), custom_call_target="tpu_custom_call" | custom-call | flops 268435456 | bytes 1048576 | tf_op jit(solution)/shard_map/prepare/pallas_call | solution.py:420
  7.3 1.4 %collective-permute-done.refs_0_ = bf16[256,256]{1,0:T(8,128)(2,1)S(1)} collective-permute-done((bf16[256,256]{1,0:T(8,128)(2,1)S(1)}, bf16[256,256]{1,0:T(8,128)(2,1)S(1)}, u32[]{:S(2)}, u32[]{:S(2)}) %collective-permute-start) | collective-permute-done | bytes 131104 | tf_op jit(solution)/shard_map/ppermute | solution.py:458
  8.7 1.6 %collective-permute-start.2 = (bf16[256,256]{1,0:T(8,128)(2,1)S(1)}, bf16[256,256]{1,0:T(8,128)(2,1)S(1)}, u32[]{:S(2)}, u32[]{:S(2)}) collective-permute-start(bf16[256,256]{1,0:T(8,128)(2,1)S(1)} %get-tuple-element.79), channel_id=1, source_target_pairs={{0,4},{1,5},{2,6},{3,7},{4,0},{5,1},{6,2},{7,3},{8,12},{9,13},{10,... | collective-permute-start | bytes 393224 | tf_op jit(solution)/shard_map/ppermute | solution.py:452
  10.3 1.5 %collective-permute-start.1 = (bf16[256,256]{1,0:T(8,128)(2,1)S(1)}, bf16[256,256]{1,0:T(8,128)(2,1)S(1)}, u32[]{:S(2)}, u32[]{:S(2)}) collective-permute-start(bf16[256,256]{1,0:T(8,128)(2,1)S(1)} %get-tuple-element.80), channel_id=1, source_target_pairs={{0,2},{1,3},{2,0},{3,1},{4,6},{5,7},{6,4},{7,5},{8,10},{9,11},{10,... | collective-permute-start | bytes 393224 | tf_op jit(solution)/shard_map/ppermute | solution.py:452
  11.8 2.0 %collective-permute-done.2.refs_2_ = bf16[256,256]{1,0:T(8,128)(2,1)S(1)} collective-permute-done((bf16[256,256]{1,0:T(8,128)(2,1)S(1)}, bf16[256,256]{1,0:T(8,128)(2,1)S(1)}, u32[]{:S(2)}, u32[]{:S(2)}) %collective-permute-start.2) | collective-permute-done | bytes 131104 | tf_op jit(solution)/shard_map/ppermute | solution.py:452
  13.7 1.5 %collective-permute-done.1.refs_1_ = bf16[256,256]{1,0:T(8,128)(2,1)S(1)} collective-permute-done((bf16[256,256]{1,0:T(8,128)(2,1)S(1)}, bf16[256,256]{1,0:T(8,128)(2,1)S(1)}, u32[]{:S(2)}, u32[]{:S(2)}) %collective-permute-start.1) | collective-permute-done | bytes 131104 | tf_op jit(solution)/shard_map/ppermute | solution.py:452
  15.3 0.1 collective-permute-start.4
  15.4 1.5 %collective-permute-start.3 = (bf16[256,256]{1,0:T(8,128)(2,1)S(1)}, bf16[256,256]{1,0:T(8,128)(2,1)S(1)}, u32[]{:S(2)}, u32[]{:S(2)}) collective-permute-start(bf16[256,256]{1,0:T(8,128)(2,1)S(1)} %get-tuple-element.78), channel_id=1, source_target_pairs={{0,6},{1,7},{2,4},{3,5},{4,2},{5,3},{6,0},{7,1},{8,14},{9,15},{10,... | collective-permute-start | bytes 393224 | tf_op jit(solution)/shard_map/ppermute | solution.py:452
  16.9 0.2 attend_first.1
  17.1 0.5 %slice.24 = s32[1,1]{1,0:T(1,128)} slice(s32[8,128]{1,0:T(8,128)S(1)} %get-tuple-element.44.facts), slice={[0:1], [0:1]} | slice | bytes 8 | tf_op jit(solution)/shard_map/slice | solution.py:470
  18.2 3.9 %collective-permute-done.3.refs_0_ = bf16[256,256]{1,0:T(8,128)(2,1)S(1)} collective-permute-done((bf16[256,256]{1,0:T(8,128)(2,1)S(1)}, bf16[256,256]{1,0:T(8,128)(2,1)S(1)}, u32[]{:S(2)}, u32[]{:S(2)}) %collective-permute-start.3) | collective-permute-done | bytes 131104 | tf_op jit(solution)/shard_map/ppermute | solution.py:452
  22.2 0.1 collective-permute-start.5
  22.3 0.0 collective-permute-done.4.refs_1_
  22.3 0.2 attend_second.1
  22.5 1.1 %collective-permute-done.5.kv_last = bf16[1,256,256]{2,1,0:T(8,128)(2,1)S(1)} collective-permute-done((bf16[1,256,256]{2,1,0:T(8,128)(2,1)S(1)}, bf16[1,256,256]{2,1,0:T(8,128)(2,1)S(1)}, u32[]{:S(2)}, u32[]{:S(2)}) %collective-permute-start.5) | collective-permute-done | bytes 131104 | tf_op jit(solution)/shard_map/ppermute | solution.py:452
  23.6 2.0 %settle.1 = (bf16[256,1024]{1,0:T(8,128)(2,1)S(1)}, bf16[2048,128]{1,0:T(8,128)(2,1)S(1)}, bf16[128,2048]{1,0:T(8,128)(2,1)S(1)}, f32[2048,128]{1,0:T(8,128)S(1)...) custom-call(s32[8,128]{1,0:T(8,128)S(1)} %get-tuple-element.44.facts, ...), custom_call_target="tpu_custom_call", output_to_operand_aliasing={{5}: (10, {}), {6}: (11, {}), {7}: (12, {})} | custom-call | flops 268435456 | bytes 1048576 | tf_op jit(solution)/shard_map/settle/pallas_call | solution.py:420
  25.7 1.1 %odd.1 = (bf16[256,1024]{1,0:T(8,128)(2,1)}, bf16[4,2048,256]{2,1,0:T(8,128)(2,1)S(1)}, bf16[4,256,256]{2,1,0:T(8,128)(2,1)S(1)}) custom-call(s32[8,128]{1,0:T(8,128)S(1)} %get-tuple-element.44.facts, bf16[128,2048]{1,0:T(8,128)(2,1)S(1)} %get-tuple-element.45.q_t, bf16[2048,128]{1,0:T(8,128)(2,1)S(1)} %get-tuple-element.54.do_s, ...), custom_call_target="tpu_custom_call" | custom-call | flops 1610612736 | bytes 1048576 | tf_op jit(solution)/shard_map/odd/pallas_call | solution.py:420
  26.8 0.1 collective-permute-start.6
  26.8 0.4 even.1
  27.2 1.5 %collective-permute-done.6 = bf16[4,256,256]{2,1,0:T(8,128)(2,1)S(1)} collective-permute-done((bf16[4,256,256]{2,1,0:T(8,128)(2,1)S(1)}, bf16[4,256,256]{2,1,0:T(8,128)(2,1)S(1)}, u32[]{:S(2)}, u32[]{:S(2)}) %collective-permute-start.6) | collective-permute-done | bytes 524320 | tf_op jit(solution)/shard_map/ppermute | solution.py:452
  28.7 0.1 convert_element_type.35
  28.8 0.1 fusion.12
  28.9 7.0 %collective-permute-start.9 = (bf16[256,256]{1,0:T(8,128)(2,1)S(1)}, bf16[256,256]{1,0:T(8,128)(2,1)S(1)}, u32[]{:S(2)}, u32[]{:S(2)}) collective-permute-start(bf16[256,256]{1,0:T(8,128)(2,1)S(1)} %get-tuple-element.72), channel_id=1, source_target_pairs={{0,6},{1,7},{2,4},{3,5},{4,2},{5,3},{6,0},{7,1},{8,14},{9,15},{10,... | collective-permute-start | bytes 393224 | tf_op jit(solution)/shard_map/ppermute | solution.py:452
  36.0 0.0 collective-permute-start.8
  36.0 0.6 %collective-permute-start.7 = (bf16[256,256]{1,0:T(8,128)(2,1)S(1)}, bf16[256,256]{1,0:T(8,128)(2,1)S(1)}, u32[]{:S(2)}, u32[]{:S(2)}) collective-permute-start(bf16[256,256]{1,0:T(8,128)(2,1)S(1)} %get-tuple-element.74), channel_id=1, source_target_pairs={{0,2},{1,3},{2,0},{3,1},{4,6},{5,7},{6,4},{7,5},{8,10},{9,11},{10,... | collective-permute-start | bytes 393224 | tf_op jit(solution)/shard_map/ppermute | solution.py:452
  36.6 2.6 %rest.1 = (bf16[256,1024]{1,0:T(8,128)(2,1)}, f32[256,256]{1,0:T(8,128)S(1)}, f32[256,256]{1,0:T(8,128)S(1)}) custom-call(s32[8,128]{1,0:T(8,128)S(1)} %get-tuple-element.44.facts, bf16[128,2048]{1,0:T(8,128)(2,1)S(1)} %get-tuple-element.45.q_t, bf16[2048,128]{1,0:T(8,128)(2,1)S(1)} %get-tuple-element.54.do_s, bf16[128,2048]{1,0:T(8,128)(2,1)S(1)} %get-tuple-element.55.do_t, ...), custom_call_target="tpu_custom_call" | custom-call | flops 2013265920 | bytes 1048576 | tf_op jit(solution)/shard_map/rest/pallas_call | solution.py:420
  39.2 0.7 %collective-permute-done.9 = bf16[256,256]{1,0:T(8,128)(2,1)S(1)} collective-permute-done((bf16[256,256]{1,0:T(8,128)(2,1)S(1)}, bf16[256,256]{1,0:T(8,128)(2,1)S(1)}, u32[]{:S(2)}, u32[]{:S(2)}) %collective-permute-start.9) | collective-permute-done | bytes 131104 | tf_op jit(solution)/shard_map/ppermute | solution.py:452
  39.9 2.6 %collective-permute-done.8 = bf16[256,256]{1,0:T(8,128)(2,1)S(1)} collective-permute-done((bf16[256,256]{1,0:T(8,128)(2,1)S(1)}, bf16[256,256]{1,0:T(8,128)(2,1)S(1)}, u32[]{:S(2)}, u32[]{:S(2)}) %collective-permute-start.8) | collective-permute-done | bytes 131104 | tf_op jit(solution)/shard_map/ppermute | solution.py:452
  42.5 0.0 collective-permute-done.7
  42.5 0.2 fusion.6
  42.6 1.9 %collective-permute-start.10 = (bf16[256,256]{1,0:T(8,128)(2,1)S(1)}, bf16[256,256]{1,0:T(8,128)(2,1)S(1)}, u32[]{:S(2)}, u32[]{:S(2)}) collective-permute-start(bf16[256,256]{1,0:T(8,128)(2,1)S(1)} %get-tuple-element.75), channel_id=1, source_target_pairs={{8,0},{9,1},{10,2},{11,3},{12,4},{13,5},{14,6},{15,7},{16,8},{17,9... | collective-permute-start | bytes 393224 | tf_op jit(solution)/shard_map/ppermute | solution.py:502
  44.6 5.4 %collective-permute-done.10.last = bf16[256,256]{1,0:T(8,128)(2,1)S(1)} collective-permute-done((bf16[256,256]{1,0:T(8,128)(2,1)S(1)}, bf16[256,256]{1,0:T(8,128)(2,1)S(1)}, u32[]{:S(2)}, u32[]{:S(2)}) %collective-permute-start.10) | collective-permute-done | bytes 131104 | tf_op jit(solution)/shard_map/ppermute | solution.py:502
  50.0 0.7 %finish.1 = (bf16[256,128]{1,0:T(8,128)(2,1)}, bf16[256,128]{1,0:T(8,128)(2,1)}) custom-call(f32[256,256]{1,0:T(8,128)S(1)} %get-tuple-element.76.total, bf16[256,256]{1,0:T(8,128)(2,1)S(1)} %collective-permute-done.10.last), custom_call_target="tpu_custom_call" | custom-call | flops 1 | bytes 1048576 | tf_op jit(solution)/shard_map/finish/pallas_call | solution.py:420
  (3 shorter events, 0.1 us)
Async XLA Ops:
  1.5 7.1 %collective-permute-start = (bf16[256,256]{1,0:T(8,128)(2,1)S(1)}, bf16[256,256]{1,0:T(8,128)(2,1)S(1)}, u32[]{:S(2)}, u32[]{:S(2)}) collective-permute-start(bf16[256,256]{1,0:T(8,128)(2,1)S(1)} %join.1.kv_ref), channel_id=1, source_target_pairs={{0,8},{1,9},{2,10},{3,11},{4,12},{5,13},{6,14},{7,15},{8,16},{9,17... | collective-permute-start | bytes 393224 | tf_op jit(solution)/shard_map/ppermute | solution.py:458
  8.7 5.0 %collective-permute-start.2 = (bf16[256,256]{1,0:T(8,128)(2,1)S(1)}, bf16[256,256]{1,0:T(8,128)(2,1)S(1)}, u32[]{:S(2)}, u32[]{:S(2)}) collective-permute-start(bf16[256,256]{1,0:T(8,128)(2,1)S(1)} %get-tuple-element.79), channel_id=1, source_target_pairs={{0,4},{1,5},{2,6},{3,7},{4,0},{5,1},{6,2},{7,3},{8,12},{9,13},{10,... | collective-permute-start | bytes 393224 | tf_op jit(solution)/shard_map/ppermute | solution.py:452
  10.3 5.0 %collective-permute-start.1 = (bf16[256,256]{1,0:T(8,128)(2,1)S(1)}, bf16[256,256]{1,0:T(8,128)(2,1)S(1)}, u32[]{:S(2)}, u32[]{:S(2)}) collective-permute-start(bf16[256,256]{1,0:T(8,128)(2,1)S(1)} %get-tuple-element.80), channel_id=1, source_target_pairs={{0,2},{1,3},{2,0},{3,1},{4,6},{5,7},{6,4},{7,5},{8,10},{9,11},{10,... | collective-permute-start | bytes 393224 | tf_op jit(solution)/shard_map/ppermute | solution.py:452
  15.3 7.0 %collective-permute-start.4 = (bf16[3,256,256]{2,1,0:T(8,128)(2,1)S(1)}, bf16[3,256,256]{2,1,0:T(8,128)(2,1)S(1)}, u32[]{:S(2)}, u32[]{:S(2)}) collective-permute-start(bf16[3,256,256]{2,1,0:T(8,128)(2,1)S(1)} %pad_maximum_fusion), channel_id=1, source_target_pairs={{0,1},{1,0},{2,3},{3,2},{4,5},{5,4},{6,7},{7,6},{8,9},{9,8},{10,11... | collective-permute-start | bytes 1179656 | tf_op jit(solution)/shard_map/ppermute | solution.py:452
  15.4 6.8 %collective-permute-start.3 = (bf16[256,256]{1,0:T(8,128)(2,1)S(1)}, bf16[256,256]{1,0:T(8,128)(2,1)S(1)}, u32[]{:S(2)}, u32[]{:S(2)}) collective-permute-start(bf16[256,256]{1,0:T(8,128)(2,1)S(1)} %get-tuple-element.78), channel_id=1, source_target_pairs={{0,6},{1,7},{2,4},{3,5},{4,2},{5,3},{6,0},{7,1},{8,14},{9,15},{10,... | collective-permute-start | bytes 393224 | tf_op jit(solution)/shard_map/ppermute | solution.py:452
  22.2 1.4 %collective-permute-start.5 = (bf16[1,256,256]{2,1,0:T(8,128)(2,1)S(1)}, bf16[1,256,256]{2,1,0:T(8,128)(2,1)S(1)}, u32[]{:S(2)}, u32[]{:S(2)}) collective-permute-start(bf16[1,256,256]{2,1,0:T(8,128)(2,1)S(1)} %select_bitcast_fusion), channel_id=1, source_target_pairs={{0,1},{1,0},{2,3},{3,2},{4,5},{5,4},{6,7},{7,6},{8,9},{9,8},{10,11... | collective-permute-start | bytes 393224 | tf_op jit(solution)/shard_map/ppermute | solution.py:452
  26.8 2.0 %collective-permute-start.6 = (bf16[4,256,256]{2,1,0:T(8,128)(2,1)S(1)}, bf16[4,256,256]{2,1,0:T(8,128)(2,1)S(1)}, u32[]{:S(2)}, u32[]{:S(2)}) collective-permute-start(bf16[4,256,256]{2,1,0:T(8,128)(2,1)S(1)} %get-tuple-element.67), channel_id=1, source_target_pairs={{0,1},{1,0},{2,3},{3,2},{4,5},{5,4},{6,7},{7,6},{8,9},{9,8},{10,11... | collective-permute-start | bytes 1572872 | tf_op jit(solution)/shard_map/ppermute | solution.py:452
  28.9 11.0 %collective-permute-start.9 = (bf16[256,256]{1,0:T(8,128)(2,1)S(1)}, bf16[256,256]{1,0:T(8,128)(2,1)S(1)}, u32[]{:S(2)}, u32[]{:S(2)}) collective-permute-start(bf16[256,256]{1,0:T(8,128)(2,1)S(1)} %get-tuple-element.72), channel_id=1, source_target_pairs={{0,6},{1,7},{2,4},{3,5},{4,2},{5,3},{6,0},{7,1},{8,14},{9,15},{10,... | collective-permute-start | bytes 393224 | tf_op jit(solution)/shard_map/ppermute | solution.py:452
  36.0 6.5 %collective-permute-start.8 = (bf16[256,256]{1,0:T(8,128)(2,1)S(1)}, bf16[256,256]{1,0:T(8,128)(2,1)S(1)}, u32[]{:S(2)}, u32[]{:S(2)}) collective-permute-start(bf16[256,256]{1,0:T(8,128)(2,1)S(1)} %get-tuple-element.73), channel_id=1, source_target_pairs={{0,4},{1,5},{2,6},{3,7},{4,0},{5,1},{6,2},{7,3},{8,12},{9,13},{10,... | collective-permute-start | bytes 393224 | tf_op jit(solution)/shard_map/ppermute | solution.py:452
  36.0 6.5 %collective-permute-start.7 = (bf16[256,256]{1,0:T(8,128)(2,1)S(1)}, bf16[256,256]{1,0:T(8,128)(2,1)S(1)}, u32[]{:S(2)}, u32[]{:S(2)}) collective-permute-start(bf16[256,256]{1,0:T(8,128)(2,1)S(1)} %get-tuple-element.74), channel_id=1, source_target_pairs={{0,2},{1,3},{2,0},{3,1},{4,6},{5,7},{6,4},{7,5},{8,10},{9,11},{10,... | collective-permute-start | bytes 393224 | tf_op jit(solution)/shard_map/ppermute | solution.py:452
  42.6 7.3 %collective-permute-start.10 = (bf16[256,256]{1,0:T(8,128)(2,1)S(1)}, bf16[256,256]{1,0:T(8,128)(2,1)S(1)}, u32[]{:S(2)}, u32[]{:S(2)}) collective-permute-start(bf16[256,256]{1,0:T(8,128)(2,1)S(1)} %get-tuple-element.75), channel_id=1, source_target_pairs={{8,0},{9,1},{10,2},{11,3},{12,4},{13,5},{14,6},{15,7},{16,8},{17,9... | collective-permute-start | bytes 393224 | tf_op jit(solution)/shard_map/ppermute | solution.py:502

commit v2 on v0

--- a/solution.py
+++ b/solution.py
@@ -51,6 +51,11 @@
     return (lax.rem(index, n_ctx), base, before, short), ends
 
 
+def straight_route(n_dp, n_ctx, flip):
+    pairs = [(d, c, d + int(c > c ^ flip)) for d in range(n_dp) for c in range(n_ctx)]
+    return [(d * n_ctx + c, run * n_ctx + (c ^ flip)) for d, c, run in pairs if run < n_dp]
+
+
 class Place:
     def __init__(self, n_ctx, rows, facts):
         self.n_ctx, self.rows = n_ctx, rows
@@ -101,8 +106,8 @@
         copy.wait()
 
 
-def with_ones(kv):
-    return jnp.concatenate([kv, jnp.ones((kv.shape[0], HDIM), BF16)], axis=1)
+def ones_beside(values):
+    return jnp.concatenate([values, jnp.ones(values.shape, BF16)], axis=1)
 
 
 def levels(place, back, many, q_s, key_block, start):
@@ -129,7 +134,7 @@
     copies = fetch([(lengths_hbm, lengths_ref), (q_hbm, q_ref), (do_hbm, do_ref)], sems)
     rows = q_ref.shape[0]
     index = lax.axis_index("dp") * n_ctx + lax.axis_index("ctx")
-    kv_own[...] = with_ones(kv_ref[...])
+    kv_own[...] = kv_ref[...]
     copies[0].wait()
     facts, ends = facts_of(n_ctx, rows, index, lengths_ref)
     place = Place(n_ctx, rows, facts)
@@ -151,7 +156,7 @@
     level[...] = top
     p = jnp.exp2(s - wide(top)).astype(BF16)
     p_own[...] = p
-    acc[...] = dot(p, kv_own[:, HDIM:])
+    acc[...] = dot(p, ones_beside(kv_own[:, HDIM:]))
     copies[2].wait()
     for here, there in chunks(rows, n_ctx):
         do_r[here, :] = do_ref[there]
@@ -169,7 +174,7 @@
     p = [jnp.exp2(s - wide(level[:many, :])).astype(BF16) for s in scores]
     for ref, part in zip(probs, p):
         ref[:many, :] = part
-    acc[:many, :] += dot(side_by_side(p, 1), side_by_side([kv[:, HDIM:] for kv in kvs], 0))
+    acc[:many, :] += dot(side_by_side(p, 1), side_by_side([ones_beside(kv[:, HDIM:]) for kv in kvs], 0))
 
 
 def attend_even(n_ctx, facts, q_s, start, level, acc_in, *refs):
@@ -177,7 +182,7 @@
     rows = got[0].shape[0]
     place = Place(n_ctx, rows, facts)
     for i, ref in enumerate(got):
-        kv_even[i] = with_ones(ref[...])
+        kv_even[i] = ref[...]
     acc[...] = acc_in[...]
 
     def body(backs, many):
@@ -188,15 +193,15 @@
 
 
 def gradients(many, q_t, do_s, do_t, ps, kvs, corr):
-    d = [dot(do_s[:many, :], kv[:, HDIM:2 * HDIM], NT) for kv in kvs]
+    d = [dot(do_s[:many, :], kv[:, HDIM:], NT) for kv in kvs]
     dv = [dot(do_t[:, :many], p) for p in ps]
     ds = [(p.astype(F32) * (each - wide(corr[:many, :]))).astype(BF16) for p, each in zip(ps, d)]
     dk = [dot(q_t[:, :many], each) for each in ds]
     return [(each, jnp.concatenate([k.T, v.T], axis=1)) for each, k, v in zip(ds, dk, dv)]
 
 
-def forward(n_ctx, facts, q_s, q_t, do_r, start, level, acc_in, kv_own, kv_even, kv_passed, p_own_in, p_even_in,
-            o_hbm, kv_odd, ds_odd, do_s, do_t, corr, g_passed, p_own, p_even, o_ref, p_odd, acc, top, p_new, kv_now, sems):
+def forward(n_ctx, facts, q_s, q_t, do_r, start, level, acc_in, kv_own, kv_even, kv_odd, p_own_in, p_even_in,
+            o_hbm, ds_odd, do_s, do_t, corr, g_passed, p_own, p_even, o_ref, p_odd, acc, top, p_new, kv_now, sems):
     rows = o_ref.shape[0]
     size = rows // n_ctx
     place = Place(n_ctx, rows, facts)
@@ -204,9 +209,6 @@
     everything = HEADS * rows
     odd_backs = range(1, n_ctx, 2)
     del p_own_in, p_even_in
-
-    for i in range(pairs):
-        kv_odd[i] = with_ones(kv_passed[i])
 
     def odd(backs):
         return [kv_odd.at[place.hop(back)] for back in backs]
@@ -263,7 +265,7 @@
         def replace(here, s):
             p = jnp.exp2(s - wide(top[here, :])).astype(BF16)
             p_new[here, :] = p
-            acc[here, :] += dot(p, kv_now[:, HDIM:])
+            acc[here, :] += dot(p, ones_beside(kv_now[:, HDIM:]))
 
         @pl.loop(0, n_ctx)
         def _(c):
@@ -403,7 +405,7 @@
     many = HEADS * rows
     once = 2 * many * rows * HDIM
     by_row, by_lane = (many, HDIM), (HDIM, many)
-    block, kv_ones = (rows, 2 * HDIM), (rows, 3 * HDIM)
+    block = (rows, 2 * HDIM)
     run = functools.partial(call, resident=(n_ctx + 1) * many * rows <= 6 * 2**20)
     def kernel(body, *args, **kwargs):
         return run(functools.partial(body, n_ctx), body.__name__, *args, **kwargs)
@@ -414,35 +416,36 @@
     later = [ctx < ctx ^ max(2 * i, 1) for i in range(pairs)]
 
     kv, = run(join, "join", [(block, BF16)], (keys, values), [], 1, away=(0, 1), copies=2)
+    near = lambda i: i & (i - 1) == 0
     prev = lax.ppermute(kv, axes, run_route(n_dp, n_ctx))
+    straight = {i: lax.ppermute(kv, axes, straight_route(n_dp, n_ctx, 2 * i)) for i in range(1, pairs) if not near(i)}
     facts, kv_own, q_s, q_t, do_r, start, level, p_own, acc = kernel(
-        prepare, [((8, HDIM), jnp.int32), (kv_ones, BF16), (by_row, BF16), (by_lane, BF16), (by_row, BF16),
+        prepare, [((8, HDIM), jnp.int32), (block, BF16), (by_row, BF16), (by_lane, BF16), (by_row, BF16),
                   ((rows, rows), jnp.int32), (by_row, F32), ((many, rows), BF16), ((many, 2 * HDIM), F32)],
         (lengths, queries, grad_out, kv),
         [pltpu.SMEM(lengths.shape, jnp.int32), pltpu.VMEM(queries.shape, BF16), pltpu.VMEM(queries.shape, BF16)], 2 * once,
         away=(0, 1, 2), copies=3)
-    ours = kv_own[:, :2 * HDIM]
-    sent = [jnp.where(after, ours, prev) for after in later]
-    got = [prev] + [swap(sent[i], 2 * i) for i in range(1, pairs)]
+    sent = [jnp.where(after, kv_own, prev) for after in later]
+    got = [prev] + [swap(sent[i], 2 * i) if near(i) else straight[i] for i in range(1, pairs)]
     passed = swap(jnp.stack(sent[:1] + got[1:]), 1)
     kv_even, p_even, acc = kernel(
-        attend_even, [((pairs,) + kv_ones, BF16), ((pairs, many, rows), BF16), ((many, 2 * HDIM), F32)],
+        attend_even, [((pairs,) + block, BF16), ((pairs, many, rows), BF16), ((many, 2 * HDIM), F32)],
         (facts, q_s, start, level, acc, *got), [], 2 * pairs * once)
-    attn_out, kv_odd, ds_odd, do_s, do_t, corr, g_passed, p_own, p_even = kernel(
+    attn_out, ds_odd, do_s, do_t, corr, g_passed, p_own, p_even = kernel(
         forward,
-        [(queries.shape, BF16), ((pairs,) + kv_ones, BF16), ((pairs, many, rows), BF16),
+        [(queries.shape, BF16), ((pairs, many, rows), BF16),
          (by_row, BF16), (by_lane, BF16), (by_row, F32), ((pairs,) + block, BF16), (p_own.shape, BF16), (p_even.shape, BF16)],
         (facts, q_s, q_t, do_r, start, level, acc, kv_own, kv_even, passed, p_own, p_even),
         [pltpu.VMEM(queries.shape, BF16), pltpu.VMEM((pairs, many, rows), BF16), pltpu.VMEM((many, 2 * HDIM), F32),
-         pltpu.VMEM(by_row, F32), pltpu.VMEM((many, rows), BF16), pltpu.VMEM(kv_ones, BF16)],
-        5 * pairs * once, aliases=((10, 7), (11, 8)), leaves=(0,), copies=2)
+         pltpu.VMEM(by_row, F32), pltpu.VMEM((many, rows), BF16), pltpu.VMEM(block, BF16)],
+        5 * pairs * once, aliases=((10, 6), (11, 7)), leaves=(0,), copies=2)
     partner = swap(g_passed, 1).astype(F32)
     shared = (facts, q_t, do_s, do_t, kv_even, p_even, corr)
     ds_even, g_direct = kernel(even, [((pairs - 1, many, rows), BF16), ((pairs - 1,) + block, F32)],
                                shared, [], 3 * (pairs - 1) * once)
     terms = [partner[0]] + [swap((g_direct[i - 1] + partner[i]).astype(BF16), 2 * i).astype(F32) for i in range(1, pairs)]
     grad_queries, g_own, g_prev = kernel(rest, [(queries.shape, BF16), (block, F32), (block, F32)],
-                                         shared + (kv_own, p_own, kv_odd, ds_odd, ds_even),
+                                         shared + (kv_own, p_own, passed, ds_odd, ds_even),
                                          [pltpu.VMEM(by_row, F32)], (n_ctx + 7) * once)
     own_total, prev_total = g_own, g_prev
     for after, term in zip(later, terms):

time: 46.9 us -> 60.5 us (1.29); the launches traced: 47.2 us -> 59.7 us
  local copies, waits for them, and re-layouts: 0 us -> 9.85 us
  starting transfers between devices: 15 us -> 20.7 us
  waiting for transfers between devices: 22.5 us -> 17.6 us
  other arithmetic: 0.49 us -> 1.67 us
  Pallas kernels: 8.41 us -> 9.07 us
    unnamed x0 -> x26, local copies, waits for them, and re-layouts: none -> 9.85 us
    ppermute x0 -> x1, starting transfers between devices: none -> 4.36 us  [shards(): lax.ppermute(kv, axes, straight_route(n_dp, n_ctx, 2 * i))]
    ppermute x1, waiting for transfers between devices: 10.4 us -> 8.01 us  [shards(): last = lax.ppermute(prev_total.astype(BF16), axes, back)]
    ppermute x8 -> x7, waiting for transfers between devices: 11.7 us -> 9.6 us  [swap(): return lax.ppermute(blocks, axes, flip_route(n_dp, n_ctx, flip))]
    ppermute x8 -> x7, starting transfers between devices: 8.82 us -> 10.1 us  [swap(): return lax.ppermute(blocks, axes, flip_route(n_dp, n_ctx, flip))]
    convert_element_type x1, other arithmetic: 0.08 us -> 1.27 us  [shards(): partner = swap(g_passed, 1).astype(F32)]
    pallas_call x7, Pallas kernels: 8.41 us -> 9.07 us  [call(): pl.pallas_call(body, out_shape=outs, in_specs=in_specs, out_specs=tuple(o...]
  transfers between devices with their start and end apart: 10 -> 10, of which waited for: 9 -> 6; matrix products, arithmetic and copies ran while one was open for 0% -> 0% of each run, Pallas kernels for 11% -> 8%
where the time goes in v2:
time: 60.5 us; the launch traced here: 59.7 us
  starting transfers between devices  20.7 us (34%)
  waiting for transfers between devices  17.6 us (29%)
  local copies, waits for them, and re-layouts  9.85 us (16%)
  Pallas kernels  9.07 us (15%)
  other arithmetic  1.67 us (3%)
  between operations  0.82 us (1%)
    ppermute x7, starting transfers between devices, swap(): return lax.ppermute(blocks, axes, flip_route(n_dp, n_ctx, flip))  10.1 us
    unnamed x26, local copies, waits for them, and re-layouts  9.85 us
    ppermute x7, waiting for transfers between devices, swap(): return lax.ppermute(blocks, axes, flip_route(n_dp, n_ctx, flip))  9.6 us
    pallas_call x7, Pallas kernels, call(): pl.pallas_call(body, out_shape=outs, in_specs=in_specs, out_specs=tuple(o...  9.07 us
    ppermute x1, waiting for transfers between devices, shards(): last = lax.ppermute(prev_total.astype(BF16), axes, back)  8.01 us
    ppermute x1, starting transfers between devices, shards(): prev = lax.ppermute(kv, axes, run_route(n_dp, n_ctx))  4.94 us
    ppermute x1, starting transfers between devices, shards(): lax.ppermute(kv, axes, straight_route(n_dp, n_ctx, 2 * i))  4.36 us
    ppermute x1, starting transfers between devices, shards(): last = lax.ppermute(prev_total.astype(BF16), axes, back)  1.29 us
  transfers between devices with their start and end apart: 10, of which 6 were waited for; matrix products, arithmetic and copies ran while one was open for 0% of the time, Pallas kernels for 8%

profile of v2, /device:TPU:0, one launch (start us, length us, event | category | flops | bytes accessed | tf_op | source)
XLA Modules:
  0.0 59.7 jit_solution(7977004172689640861)
XLA Ops:
  0.6 0.9 %join.1.kv_ref = bf16[256,256]{1,0:T(8,128)(2,1)S(1)} custom-call(bf16[256,128]{1,0:T(8,128)(2,1)} %keys.1, bf16[256,128]{1,0:T(8,128)(2,1)} %values.1), custom_call_target="tpu_custom_call" | custom-call | flops 1 | bytes 1048576 | tf_op jit(solution)/shard_map/join/pallas_call | solution.py:386
  1.5 4.9 %collective-permute-start = (bf16[256,256]{1,0:T(8,128)(2,1)S(1)}, bf16[256,256]{1,0:T(8,128)(2,1)S(1)}, u32[]{:S(2)}, u32[]{:S(2)}) collective-permute-start(bf16[256,256]{1,0:T(8,128)(2,1)S(1)} %join.1.kv_ref), channel_id=1, source_target_pairs={{0,8},{1,9},{2,10},{3,11},{4,12},{5,13},{6,14},{7,15},{8,16},{9,17... | collective-permute-start | bytes 393224 | tf_op jit(solution)/shard_map/ppermute | solution.py:420
  6.5 4.4 %collective-permute-start.3 = (bf16[256,256]{1,0:T(8,128)(2,1)S(1)}, bf16[256,256]{1,0:T(8,128)(2,1)S(1)}, u32[]{:S(2)}, u32[]{:S(2)}) collective-permute-start(bf16[256,256]{1,0:T(8,128)(2,1)S(1)} %join.1.kv_ref), channel_id=1, source_target_pairs={{0,6},{1,7},{2,4},{3,5},{4,10},{5,11},{6,8},{7,9},{8,14},{9,15},{1... | collective-permute-start | bytes 393224 | tf_op jit(solution)/shard_map/ppermute | solution.py:421
  10.9 2.3 %prepare.1 = (s32[8,128]{1,0:T(8,128)S(1)}, bf16[256,256]{1,0:T(8,128)(2,1)S(1)}, bf16[2048,128]{1,0:T(8,128)(2,1)S(1)}, bf16[128,2048]{1,0:T(8,128)(2,1)S(1)}, ...) custom-call(s32[16]{0:T(128)} %lengths_hbm.1, ...), custom_call_target="tpu_custom_call" | custom-call | flops 268435456 | bytes 1048576 | tf_op jit(solution)/shard_map/prepare/pallas_call | solution.py:386
  13.1 0.0 collective-permute-done.refs_0_
  13.2 1.6 %collective-permute-start.2 = (bf16[256,256]{1,0:T(8,128)(2,1)S(1)}, bf16[256,256]{1,0:T(8,128)(2,1)S(1)}, u32[]{:S(2)}, u32[]{:S(2)}) collective-permute-start(bf16[256,256]{1,0:T(8,128)(2,1)S(1)} %get-tuple-element.64), channel_id=1, source_target_pairs={{0,4},{1,5},{2,6},{3,7},{4,0},{5,1},{6,2},{7,3},{8,12},{9,13},{10,... | collective-permute-start | bytes 393224 | tf_op jit(solution)/shard_map/ppermute | solution.py:414
  14.8 0.5 collective-permute-start.1
  15.3 0.0 collective-permute-done.3.refs_3_
  15.3 2.9 %collective-permute-done.2.refs_2_ = bf16[256,256]{1,0:T(8,128)(2,1)S(1)} collective-permute-done((bf16[256,256]{1,0:T(8,128)(2,1)S(1)}, bf16[256,256]{1,0:T(8,128)(2,1)S(1)}, u32[]{:S(2)}, u32[]{:S(2)}) %collective-permute-start.2) | collective-permute-done | bytes 131104 | tf_op jit(solution)/shard_map/ppermute | solution.py:414
  18.2 1.5 %collective-permute-done.1.refs_1_ = bf16[256,256]{1,0:T(8,128)(2,1)S(1)} collective-permute-done((bf16[256,256]{1,0:T(8,128)(2,1)S(1)}, bf16[256,256]{1,0:T(8,128)(2,1)S(1)}, u32[]{:S(2)}, u32[]{:S(2)}) %collective-permute-start.1) | collective-permute-done | bytes 131104 | tf_op jit(solution)/shard_map/ppermute | solution.py:414
  19.7 0.1 pad_maximum_fusion
  19.8 0.1 collective-permute-start.4
  19.9 0.2 attend_even.1
  20.1 1.7 %collective-permute-done.4.kv_odd = bf16[4,256,256]{2,1,0:T(8,128)(2,1)S(1)} collective-permute-done((bf16[4,256,256]{2,1,0:T(8,128)(2,1)S(1)}, bf16[4,256,256]{2,1,0:T(8,128)(2,1)S(1)}, u32[]{:S(2)}, u32[]{:S(2)}) %collective-permute-start.4) | collective-permute-done | bytes 524320 | tf_op jit(solution)/shard_map/ppermute | solution.py:414
  21.8 0.0 copy-start.11
  21.8 2.6 %forward.1 = (bf16[256,1024]{1,0:T(8,128)(2,1)}, bf16[4,2048,256]{2,1,0:T(8,128)(2,1)S(1)}, bf16[2048,128]{1,0:T(8,128)(2,1)S(1)}, bf16[128,2048]{1,0:T(8,128)(2...) custom-call(s32[8,128]{1,0:T(8,128)S(1)} %get-tuple-element.31.facts, ...), custom_call_target="tpu_custom_call", output_to_operand_aliasing={{6}: (10, {}), {7}: (11, {})} | custom-call | flops 2684354560 | bytes 1048576 | tf_op jit(solution)/shard_map/forward/pallas_call | solution.py:386
  24.3 0.0 copy-done.11
  24.4 0.0 copy-start
  24.4 2.0 %copy-done = bf16[4,2048,256]{2,1,0:T(8,128)(2,1)} copy-done((bf16[4,2048,256]{2,1,0:T(8,128)(2,1)}, bf16[4,2048,256]{2,1,0:T(8,128)(2,1)S(1)}, u32[]{:S(2)}) %copy-start) | copy-done | bytes 4194328
  26.3 0.0 copy-start.3
  26.3 2.0 %copy-done.3 = bf16[4,2048,256]{2,1,0:T(8,128)(2,1)} copy-done((bf16[4,2048,256]{2,1,0:T(8,128)(2,1)}, bf16[4,2048,256]{2,1,0:T(8,128)(2,1)S(1)}, u32[]{:S(2)}) %copy-start.3) | copy-done | bytes 4194328
  28.3 0.0 copy-start.5
  28.3 0.8 %copy-done.5 = bf16[2048,128]{1,0:T(8,128)(2,1)} copy-done((bf16[2048,128]{1,0:T(8,128)(2,1)}, bf16[2048,128]{1,0:T(8,128)(2,1)S(1)}, u32[]{:S(2)}) %copy-start.5) | copy-done | bytes 524312
  29.1 0.0 copy-start.8
  29.1 0.8 %copy-done.8 = bf16[128,2048]{1,0:T(8,128)(2,1)} copy-done((bf16[128,2048]{1,0:T(8,128)(2,1)}, bf16[128,2048]{1,0:T(8,128)(2,1)S(1)}, u32[]{:S(2)}) %copy-start.8) | copy-done | bytes 524312
  29.9 1.6 %collective-permute-start.5 = (bf16[4,256,256]{2,1,0:T(8,128)(2,1)}, bf16[4,256,256]{2,1,0:T(8,128)(2,1)}, u32[]{:S(2)}, u32[]{:S(2)}) collective-permute-start(bf16[4,256,256]{2,1,0:T(8,128)(2,1)} %get-tuple-element.53), channel_id=1, source_target_pairs={{0,1},{1,0},{2,3},{3,2},{4,5},{5,4},{6,7},{7,6},{8,9},{9,8},{10,11... | collective-permute-start | bytes 1572872 | tf_op jit(solution)/shard_map/ppermute | solution.py:414
  31.5 0.0 copy-start.1
  31.5 2.2 %copy-done.1 = bf16[4,2048,256]{2,1,0:T(8,128)(2,1)S(1)} copy-done((bf16[4,2048,256]{2,1,0:T(8,128)(2,1)S(1)}, bf16[4,2048,256]{2,1,0:T(8,128)(2,1)}, u32[]{:S(2)}) %copy-start.1) | copy-done | bytes 4194328
  33.7 0.0 copy-start.6
  33.7 1.0 %copy-done.6 = bf16[2048,128]{1,0:T(8,128)(2,1)S(1)} copy-done((bf16[2048,128]{1,0:T(8,128)(2,1)S(1)}, bf16[2048,128]{1,0:T(8,128)(2,1)}, u32[]{:S(2)}) %copy-start.6) | copy-done | bytes 524312
  34.7 0.0 copy-start.9
  34.7 1.0 %copy-done.9 = bf16[128,2048]{1,0:T(8,128)(2,1)S(1)} copy-done((bf16[128,2048]{1,0:T(8,128)(2,1)S(1)}, bf16[128,2048]{1,0:T(8,128)(2,1)}, u32[]{:S(2)}) %copy-start.9) | copy-done | bytes 524312
  35.8 0.0 copy-start.2
  35.8 0.0 copy-start.4
  35.8 0.0 copy-start.7
  35.8 0.0 copy-start.10
  35.8 0.0 copy-start.12
  35.8 0.1 even.1
  35.9 0.0 collective-permute-done.5
  35.9 1.3 %convert_element_type.33 = f32[4,256,256]{2,1,0:T(8,128)S(1)} convert(bf16[4,256,256]{2,1,0:T(8,128)(2,1)} %collective-permute-done.5) | non-fusion elementwise | flops 262144 | bytes 1572864 | tf_op jit(solution)/shard_map/convert_element_type | solution.py:442
  37.2 0.1 fusion.12
  37.3 5.7 %collective-permute-start.8 = (bf16[256,256]{1,0:T(8,128)(2,1)S(1)}, bf16[256,256]{1,0:T(8,128)(2,1)S(1)}, u32[]{:S(2)}, u32[]{:S(2)}) collective-permute-start(bf16[256,256]{1,0:T(8,128)(2,1)S(1)} %get-tuple-element.58), channel_id=1, source_target_pairs={{0,6},{1,7},{2,4},{3,5},{4,2},{5,3},{6,0},{7,1},{8,14},{9,15},{10,... | collective-permute-start | bytes 393224 | tf_op jit(solution)/shard_map/ppermute | solution.py:414
  43.1 0.0 collective-permute-start.7
  43.1 0.6 %collective-permute-start.6 = (bf16[256,256]{1,0:T(8,128)(2,1)S(1)}, bf16[256,256]{1,0:T(8,128)(2,1)S(1)}, u32[]{:S(2)}, u32[]{:S(2)}) collective-permute-start(bf16[256,256]{1,0:T(8,128)(2,1)S(1)} %get-tuple-element.60), channel_id=1, source_target_pairs={{0,2},{1,3},{2,0},{3,1},{4,6},{5,7},{6,4},{7,5},{8,10},{9,11},{10,... | collective-permute-start | bytes 393224 | tf_op jit(solution)/shard_map/ppermute | solution.py:414
  43.7 0.0 copy-done.2
  43.7 0.0 copy-done.4
  43.7 0.0 copy-done.7
  43.7 0.0 copy-done.10
  43.7 0.0 copy-done.12
  43.7 2.3 %rest.1 = (bf16[256,1024]{1,0:T(8,128)(2,1)}, f32[256,256]{1,0:T(8,128)S(1)}, f32[256,256]{1,0:T(8,128)S(1)}) custom-call(s32[8,128]{1,0:T(8,128)S(1)} %get-tuple-element.31.facts, bf16[128,2048]{1,0:T(8,128)(2,1)S(1)} %get-tuple-element.33.q_t, bf16[2048,128]{1,0:T(8,128)(2,1)S(1)} %copy-done.7, bf16[128,2048]{1,0:T(8,128)(2,1)S(1)} %copy-done.10, ...), custom_call_target="tpu_custom_call" | custom-call | flops 2013265920 | bytes 1048576 | tf_op jit(solution)/shard_map/rest/pallas_call | solution.py:386
  46.1 0.9 %collective-permute-done.8 = bf16[256,256]{1,0:T(8,128)(2,1)S(1)} collective-permute-done((bf16[256,256]{1,0:T(8,128)(2,1)S(1)}, bf16[256,256]{1,0:T(8,128)(2,1)S(1)}, u32[]{:S(2)}, u32[]{:S(2)}) %collective-permute-start.8) | collective-permute-done | bytes 131104 | tf_op jit(solution)/shard_map/ppermute | solution.py:414
  47.0 2.5 %collective-permute-done.7 = bf16[256,256]{1,0:T(8,128)(2,1)S(1)} collective-permute-done((bf16[256,256]{1,0:T(8,128)(2,1)S(1)}, bf16[256,256]{1,0:T(8,128)(2,1)S(1)}, u32[]{:S(2)}, u32[]{:S(2)}) %collective-permute-start.7) | collective-permute-done | bytes 131104 | tf_op jit(solution)/shard_map/ppermute | solution.py:414
  49.5 0.0 collective-permute-done.6
  49.5 0.2 fusion.6
  49.7 1.3 %collective-permute-start.9 = (bf16[256,256]{1,0:T(8,128)(2,1)S(1)}, bf16[256,256]{1,0:T(8,128)(2,1)S(1)}, u32[]{:S(2)}, u32[]{:S(2)}) collective-permute-start(bf16[256,256]{1,0:T(8,128)(2,1)S(1)} %get-tuple-element.61), channel_id=1, source_target_pairs={{8,0},{9,1},{10,2},{11,3},{12,4},{13,5},{14,6},{15,7},{16,8},{17,9... | collective-permute-start | bytes 393224 | tf_op jit(solution)/shard_map/ppermute | solution.py:455
  51.0 8.0 %collective-permute-done.9.last = bf16[256,256]{1,0:T(8,128)(2,1)S(1)} collective-permute-done((bf16[256,256]{1,0:T(8,128)(2,1)S(1)}, bf16[256,256]{1,0:T(8,128)(2,1)S(1)}, u32[]{:S(2)}, u32[]{:S(2)}) %collective-permute-start.9) | collective-permute-done | bytes 131104 | tf_op jit(solution)/shard_map/ppermute | solution.py:455
  59.0 0.7 %finish.1 = (bf16[256,128]{1,0:T(8,128)(2,1)}, bf16[256,128]{1,0:T(8,128)(2,1)}) custom-call(f32[256,256]{1,0:T(8,128)S(1)} %get-tuple-element.62.total, bf16[256,256]{1,0:T(8,128)(2,1)S(1)} %collective-permute-done.9.last), custom_call_target="tpu_custom_call" | custom-call | flops 1 | bytes 1048576 | tf_op jit(solution)/shard_map/finish/pallas_call | solution.py:386
  (1 shorter events, 0.0 us)
Async XLA Ops:
  1.5 11.6 %collective-permute-start = (bf16[256,256]{1,0:T(8,128)(2,1)S(1)}, bf16[256,256]{1,0:T(8,128)(2,1)S(1)}, u32[]{:S(2)}, u32[]{:S(2)}) collective-permute-start(bf16[256,256]{1,0:T(8,128)(2,1)S(1)} %join.1.kv_ref), channel_id=1, source_target_pairs={{0,8},{1,9},{2,10},{3,11},{4,12},{5,13},{6,14},{7,15},{8,16},{9,17... | collective-permute-start | bytes 393224 | tf_op jit(solution)/shard_map/ppermute | solution.py:420
  6.5 8.8 %collective-permute-start.3 = (bf16[256,256]{1,0:T(8,128)(2,1)S(1)}, bf16[256,256]{1,0:T(8,128)(2,1)S(1)}, u32[]{:S(2)}, u32[]{:S(2)}) collective-permute-start(bf16[256,256]{1,0:T(8,128)(2,1)S(1)} %join.1.kv_ref), channel_id=1, source_target_pairs={{0,6},{1,7},{2,4},{3,5},{4,10},{5,11},{6,8},{7,9},{8,14},{9,15},{1... | collective-permute-start | bytes 393224 | tf_op jit(solution)/shard_map/ppermute | solution.py:421
  13.2 5.0 %collective-permute-start.2 = (bf16[256,256]{1,0:T(8,128)(2,1)S(1)}, bf16[256,256]{1,0:T(8,128)(2,1)S(1)}, u32[]{:S(2)}, u32[]{:S(2)}) collective-permute-start(bf16[256,256]{1,0:T(8,128)(2,1)S(1)} %get-tuple-element.64), channel_id=1, source_target_pairs={{0,4},{1,5},{2,6},{3,7},{4,0},{5,1},{6,2},{7,3},{8,12},{9,13},{10,... | collective-permute-start | bytes 393224 | tf_op jit(solution)/shard_map/ppermute | solution.py:414
  14.8 5.0 %collective-permute-start.1 = (bf16[256,256]{1,0:T(8,128)(2,1)S(1)}, bf16[256,256]{1,0:T(8,128)(2,1)S(1)}, u32[]{:S(2)}, u32[]{:S(2)}) collective-permute-start(bf16[256,256]{1,0:T(8,128)(2,1)S(1)} %get-tuple-element.65), channel_id=1, source_target_pairs={{0,2},{1,3},{2,0},{3,1},{4,6},{5,7},{6,4},{7,5},{8,10},{9,11},{10,... | collective-permute-start | bytes 393224 | tf_op jit(solution)/shard_map/ppermute | solution.py:414
  19.8 2.0 %collective-permute-start.4 = (bf16[4,256,256]{2,1,0:T(8,128)(2,1)S(1)}, bf16[4,256,256]{2,1,0:T(8,128)(2,1)S(1)}, u32[]{:S(2)}, u32[]{:S(2)}) collective-permute-start(bf16[4,256,256]{2,1,0:T(8,128)(2,1)S(1)} %pad_maximum_fusion), channel_id=1, source_target_pairs={{0,1},{1,0},{2,3},{3,2},{4,5},{5,4},{6,7},{7,6},{8,9},{9,8},{10,11... | collective-permute-start | bytes 1572872 | tf_op jit(solution)/shard_map/ppermute | solution.py:414
  21.8 2.6 %copy-start.11 = (bf16[4,256,256]{2,1,0:T(8,128)(2,1)}, bf16[4,256,256]{2,1,0:T(8,128)(2,1)S(1)}, u32[]{:S(2)}) copy-start(bf16[4,256,256]{2,1,0:T(8,128)(2,1)S(1)} %collective-permute-done.4.kv_odd) | copy-start | bytes 1572868
  24.4 2.0 %copy-start = (bf16[4,2048,256]{2,1,0:T(8,128)(2,1)}, bf16[4,2048,256]{2,1,0:T(8,128)(2,1)S(1)}, u32[]{:S(2)}) copy-start(bf16[4,2048,256]{2,1,0:T(8,128)(2,1)S(1)} %get-tuple-element.46.p_even) | copy-start | bytes 12582916
  26.3 2.0 %copy-start.3 = (bf16[4,2048,256]{2,1,0:T(8,128)(2,1)}, bf16[4,2048,256]{2,1,0:T(8,128)(2,1)S(1)}, u32[]{:S(2)}) copy-start(bf16[4,2048,256]{2,1,0:T(8,128)(2,1)S(1)} %get-tuple-element.49.ds_odd) | copy-start | bytes 12582916
  28.3 0.8 %copy-start.5 = (bf16[2048,128]{1,0:T(8,128)(2,1)}, bf16[2048,128]{1,0:T(8,128)(2,1)S(1)}, u32[]{:S(2)}) copy-start(bf16[2048,128]{1,0:T(8,128)(2,1)S(1)} %get-tuple-element.44.do_s) | copy-start | bytes 1572868
  29.1 0.8 %copy-start.8 = (bf16[128,2048]{1,0:T(8,128)(2,1)}, bf16[128,2048]{1,0:T(8,128)(2,1)S(1)}, u32[]{:S(2)}) copy-start(bf16[128,2048]{1,0:T(8,128)(2,1)S(1)} %get-tuple-element.45.do_t) | copy-start | bytes 1572868
  29.9 6.0 %collective-permute-start.5 = (bf16[4,256,256]{2,1,0:T(8,128)(2,1)}, bf16[4,256,256]{2,1,0:T(8,128)(2,1)}, u32[]{:S(2)}, u32[]{:S(2)}) collective-permute-start(bf16[4,256,256]{2,1,0:T(8,128)(2,1)} %get-tuple-element.53), channel_id=1, source_target_pairs={{0,1},{1,0},{2,3},{3,2},{4,5},{5,4},{6,7},{7,6},{8,9},{9,8},{10,11... | collective-permute-start | bytes 1572872 | tf_op jit(solution)/shard_map/ppermute | solution.py:414
  31.5 2.2 %copy-start.1 = (bf16[4,2048,256]{2,1,0:T(8,128)(2,1)S(1)}, bf16[4,2048,256]{2,1,0:T(8,128)(2,1)}, u32[]{:S(2)}) copy-start(bf16[4,2048,256]{2,1,0:T(8,128)(2,1)} %copy-done) | copy-start | bytes 12582916
  33.7 1.0 %copy-start.6 = (bf16[2048,128]{1,0:T(8,128)(2,1)S(1)}, bf16[2048,128]{1,0:T(8,128)(2,1)}, u32[]{:S(2)}) copy-start(bf16[2048,128]{1,0:T(8,128)(2,1)} %copy-done.5) | copy-start | bytes 1572868
  34.7 1.0 %copy-start.9 = (bf16[128,2048]{1,0:T(8,128)(2,1)S(1)}, bf16[128,2048]{1,0:T(8,128)(2,1)}, u32[]{:S(2)}) copy-start(bf16[128,2048]{1,0:T(8,128)(2,1)} %copy-done.8) | copy-start | bytes 1572868
  35.8 8.0 %copy-start.2 = (bf16[4,2048,256]{2,1,0:T(8,128)(2,1)S(1)}, bf16[4,2048,256]{2,1,0:T(8,128)(2,1)}, u32[]{:S(2)}) copy-start(bf16[4,2048,256]{2,1,0:T(8,128)(2,1)} %copy-done) | copy-start | bytes 12582916
  35.8 8.0 %copy-start.4 = (bf16[4,2048,256]{2,1,0:T(8,128)(2,1)S(1)}, bf16[4,2048,256]{2,1,0:T(8,128)(2,1)}, u32[]{:S(2)}) copy-start(bf16[4,2048,256]{2,1,0:T(8,128)(2,1)} %copy-done.3) | copy-start | bytes 12582916
  35.8 8.0 %copy-start.7 = (bf16[2048,128]{1,0:T(8,128)(2,1)S(1)}, bf16[2048,128]{1,0:T(8,128)(2,1)}, u32[]{:S(2)}) copy-start(bf16[2048,128]{1,0:T(8,128)(2,1)} %copy-done.5) | copy-start | bytes 1572868
  35.8 8.0 %copy-start.10 = (bf16[128,2048]{1,0:T(8,128)(2,1)S(1)}, bf16[128,2048]{1,0:T(8,128)(2,1)}, u32[]{:S(2)}) copy-start(bf16[128,2048]{1,0:T(8,128)(2,1)} %copy-done.8) | copy-start | bytes 1572868
  35.8 8.0 %copy-start.12 = (bf16[4,256,256]{2,1,0:T(8,128)(2,1)S(1)}, bf16[4,256,256]{2,1,0:T(8,128)(2,1)}, u32[]{:S(2)}) copy-start(bf16[4,256,256]{2,1,0:T(8,128)(2,1)} %copy-done.11) | copy-start | bytes 1572868
  37.3 9.6 %collective-permute-start.8 = (bf16[256,256]{1,0:T(8,128)(2,1)S(1)}, bf16[256,256]{1,0:T(8,128)(2,1)S(1)}, u32[]{:S(2)}, u32[]{:S(2)}) collective-permute-start(bf16[256,256]{1,0:T(8,128)(2,1)S(1)} %get-tuple-element.58), channel_id=1, source_target_pairs={{0,6},{1,7},{2,4},{3,5},{4,2},{5,3},{6,0},{7,1},{8,14},{9,15},{10,... | collective-permute-start | bytes 393224 | tf_op jit(solution)/shard_map/ppermute | solution.py:414
  43.1 6.5 %collective-permute-start.7 = (bf16[256,256]{1,0:T(8,128)(2,1)S(1)}, bf16[256,256]{1,0:T(8,128)(2,1)S(1)}, u32[]{:S(2)}, u32[]{:S(2)}) collective-permute-start(bf16[256,256]{1,0:T(8,128)(2,1)S(1)} %get-tuple-element.59), channel_id=1, source_target_pairs={{0,4},{1,5},{2,6},{3,7},{4,0},{5,1},{6,2},{7,3},{8,12},{9,13},{10,... | collective-permute-start | bytes 393224 | tf_op jit(solution)/shard_map/ppermute | solution.py:414
  43.1 6.5 %collective-permute-start.6 = (bf16[256,256]{1,0:T(8,128)(2,1)S(1)}, bf16[256,256]{1,0:T(8,128)(2,1)S(1)}, u32[]{:S(2)}, u32[]{:S(2)}) collective-permute-start(bf16[256,256]{1,0:T(8,128)(2,1)S(1)} %get-tuple-element.60), channel_id=1, source_target_pairs={{0,2},{1,3},{2,0},{3,1},{4,6},{5,7},{6,4},{7,5},{8,10},{9,11},{10,... | collective-permute-start | bytes 393224 | tf_op jit(solution)/shard_map/ppermute | solution.py:414
  49.7 9.3 %collective-permute-start.9 = (bf16[256,256]{1,0:T(8,128)(2,1)S(1)}, bf16[256,256]{1,0:T(8,128)(2,1)S(1)}, u32[]{:S(2)}, u32[]{:S(2)}) collective-permute-start(bf16[256,256]{1,0:T(8,128)(2,1)S(1)} %get-tuple-element.61), channel_id=1, source_target_pairs={{8,0},{9,1},{10,2},{11,3},{12,4},{13,5},{14,6},{15,7},{16,8},{17,9... | collective-permute-start | bytes 393224 | tf_op jit(solution)/shard_map/ppermute | solution.py:455

commit v3 on v2

--- a/solution.py
+++ b/solution.py
@@ -201,7 +201,7 @@
 
 
 def forward(n_ctx, facts, q_s, q_t, do_r, start, level, acc_in, kv_own, kv_even, kv_odd, p_own_in, p_even_in,
-            o_hbm, ds_odd, do_s, do_t, corr, g_passed, p_own, p_even, o_ref, p_odd, acc, top, p_new, kv_now, sems):
+            o_hbm, k_odd, ds_odd, do_s, do_t, corr, g_passed, p_own, p_even, o_ref, p_odd, acc, top, p_new, kv_now, sems):
     rows = o_ref.shape[0]
     size = rows // n_ctx
     place = Place(n_ctx, rows, facts)
@@ -209,6 +209,9 @@
     everything = HEADS * rows
     odd_backs = range(1, n_ctx, 2)
     del p_own_in, p_even_in
+
+    for i in range(pairs):
+        k_odd[i] = kv_odd[i, :, :HDIM]
 
     def odd(backs):
         return [kv_odd.at[place.hop(back)] for back in backs]
@@ -326,7 +329,7 @@
         g_direct[place.hop(2 * i + 2) - 1] = jnp.zeros((rows, 2 * HDIM), F32)
 
 
-def rest(n_ctx, facts, q_t, do_s, do_t, kv_even, p_even, corr, kv_own, p_own, kv_odd, ds_odd, ds_even,
+def rest(n_ctx, facts, q_t, do_s, do_t, kv_even, p_even, corr, kv_own, p_own, k_odd, ds_odd, ds_even,
          dq_ref, g_own, g_prev, dq_acc):
     rows = kv_own.shape[0]
     place = Place(n_ctx, rows, facts)
@@ -339,7 +342,7 @@
                                 side_by_side([kv[place.hop(back), :, :HDIM] for back in backs], 0))
 
     def add_odd(backs, many):
-        add(backs, many, lambda back: ds_odd.at[lax.div(back, 2)], kv_odd)
+        add(backs, many, lambda back: ds_odd.at[lax.div(back, 2)], k_odd)
 
     def add_even(backs, many):
         add(backs, many, lambda back: ds_even.at[lax.div(back, 2) - 1], kv_even)
@@ -368,11 +371,12 @@
     return sum(math.prod(array.shape) * jnp.dtype(array.dtype).itemsize for array in arrays)
 
 
-def call(body, name, outs, args, scratch, flops, resident, aliases=(), away=(), leaves=(), copies=0):
+def call(body, name, outs, args, scratch, flops, resident, aliases=(), away=(), leaves=(), final=(), copies=0):
     vmem = pl.BlockSpec(memory_space=pltpu.VMEM)
     anywhere = pl.BlockSpec(memory_space=pl.ANY)
     hbm = pl.BlockSpec(memory_space=pltpu.HBM)
-    outs = tuple(jax.ShapeDtypeStruct(shape, dtype) for shape, dtype in outs)
+    outs = tuple(jax.ShapeDtypeStruct(shape, dtype) if i in final or not resident else pltpu.VMEM(shape, dtype)
+                 for i, (shape, dtype) in enumerate(outs))
     held = size_of(scratch) + 8 * 2**20
     if not resident:
         held = min(held + size_of(outs) + size_of(args), 62 * 2**20)
@@ -431,29 +435,29 @@
     kv_even, p_even, acc = kernel(
         attend_even, [((pairs,) + block, BF16), ((pairs, many, rows), BF16), ((many, 2 * HDIM), F32)],
         (facts, q_s, start, level, acc, *got), [], 2 * pairs * once)
-    attn_out, ds_odd, do_s, do_t, corr, g_passed, p_own, p_even = kernel(
+    attn_out, k_odd, ds_odd, do_s, do_t, corr, g_passed, p_own, p_even = kernel(
         forward,
-        [(queries.shape, BF16), ((pairs, many, rows), BF16),
+        [(queries.shape, BF16), ((pairs, rows, HDIM), BF16), ((pairs, many, rows), BF16),
          (by_row, BF16), (by_lane, BF16), (by_row, F32), ((pairs,) + block, BF16), (p_own.shape, BF16), (p_even.shape, BF16)],
         (facts, q_s, q_t, do_r, start, level, acc, kv_own, kv_even, passed, p_own, p_even),
         [pltpu.VMEM(queries.shape, BF16), pltpu.VMEM((pairs, many, rows), BF16), pltpu.VMEM((many, 2 * HDIM), F32),
          pltpu.VMEM(by_row, F32), pltpu.VMEM((many, rows), BF16), pltpu.VMEM(block, BF16)],
-        5 * pairs * once, aliases=((10, 6), (11, 7)), leaves=(0,), copies=2)
+        5 * pairs * once, aliases=((10, 7), (11, 8)), leaves=(0,), final=(0,), copies=2)
     partner = swap(g_passed, 1).astype(F32)
     shared = (facts, q_t, do_s, do_t, kv_even, p_even, corr)
     ds_even, g_direct = kernel(even, [((pairs - 1, many, rows), BF16), ((pairs - 1,) + block, F32)],
                                shared, [], 3 * (pairs - 1) * once)
     terms = [partner[0]] + [swap((g_direct[i - 1] + partner[i]).astype(BF16), 2 * i).astype(F32) for i in range(1, pairs)]
     grad_queries, g_own, g_prev = kernel(rest, [(queries.shape, BF16), (block, F32), (block, F32)],
-                                         shared + (kv_own, p_own, passed, ds_odd, ds_even),
-                                         [pltpu.VMEM(by_row, F32)], (n_ctx + 7) * once)
+                                         shared + (kv_own, p_own, k_odd, ds_odd, ds_even),
+                                         [pltpu.VMEM(by_row, F32)], (n_ctx + 7) * once, final=(0,))
     own_total, prev_total = g_own, g_prev
     for after, term in zip(later, terms):
         own_total = own_total + jnp.where(after, term, 0.0)
         prev_total = prev_total + jnp.where(after, 0.0, term)
     back = [(b, a) for a, b in run_route(n_dp, n_ctx)]
     last = lax.ppermute(prev_total.astype(BF16), axes, back)
-    grad_keys, grad_values = run(finish, "finish", [(keys.shape, BF16), (values.shape, BF16)], (own_total, last), [], 1)
+    grad_keys, grad_values = run(finish, "finish", [(keys.shape, BF16), (values.shape, BF16)], (own_total, last), [], 1, final=(0, 1))
     return (attn_out, grad_queries, grad_keys, grad_values)
 
 

time: 60.5 us -> 60.8 us (level)
  starting transfers between devices: 20.7 us -> 19.8 us
  waiting for transfers between devices: 17.6 us -> 18.5 us
    ppermute x7, starting transfers between devices: 10.1 us -> 9.24 us  [swap(): return lax.ppermute(blocks, axes, flip_route(n_dp, n_ctx, flip))]
    unnamed x26 -> x22, local copies, waits for them, and re-layouts: 9.85 us -> 9.92 us
  transfers between devices with their start and end apart: 10 -> 10, of which waited for: 6 -> 7; matrix products, arithmetic and copies ran while one was open for 0% -> 0% of each run, Pallas kernels for 8% -> 8%
where the time goes in v3:
time: 60.8 us; the launch traced here: 59.9 us
  starting transfers between devices  19.8 us (33%)
  waiting for transfers between devices  18.5 us (30%)
  local copies, waits for them, and re-layouts  9.92 us (16%)
  Pallas kernels  9.11 us (15%)
  other arithmetic  1.67 us (3%)
  between operations  0.8 us (1%)
    ppermute x7, waiting for transfers between devices, swap(): return lax.ppermute(blocks, axes, flip_route(n_dp, n_ctx, flip))  9.97 us
    unnamed x22, local copies, waits for them, and re-layouts  9.92 us
    ppermute x7, starting transfers between devices, swap(): return lax.ppermute(blocks, axes, flip_route(n_dp, n_ctx, flip))  9.24 us
    pallas_call x7, Pallas kernels, call(): pl.pallas_call(body, out_shape=outs, in_specs=in_specs, out_specs=tuple(o...  9.11 us
    ppermute x1, waiting for transfers between devices, shards(): last = lax.ppermute(prev_total.astype(BF16), axes, back)  8.56 us
    ppermute x1, starting transfers between devices, shards(): prev = lax.ppermute(kv, axes, run_route(n_dp, n_ctx))  4.94 us
    ppermute x1, starting transfers between devices, shards(): lax.ppermute(kv, axes, straight_route(n_dp, n_ctx, 2 * i))  4.36 us
    ppermute x1, starting transfers between devices, shards(): last = lax.ppermute(prev_total.astype(BF16), axes, back)  1.29 us
  transfers between devices with their start and end apart: 10, of which 7 were waited for; matrix products, arithmetic and copies ran while one was open for 0% of the time, Pallas kernels for 8%

profile of v3, /device:TPU:0, one launch (start us, length us, event | category | flops | bytes accessed | tf_op | source)
XLA Modules:
  0.0 59.9 jit_solution(7027302066399141691)
XLA Ops:
  0.6 0.9 %join.1.kv_ref = bf16[256,256]{1,0:T(8,128)(2,1)S(1)} custom-call(bf16[256,128]{1,0:T(8,128)(2,1)} %keys.1, bf16[256,128]{1,0:T(8,128)(2,1)} %values.1), custom_call_target="tpu_custom_call" | custom-call | flops 1 | bytes 1048576 | tf_op jit(solution)/shard_map/join/pallas_call | solution.py:390
  1.5 4.9 %collective-permute-start = (bf16[256,256]{1,0:T(8,128)(2,1)S(1)}, bf16[256,256]{1,0:T(8,128)(2,1)S(1)}, u32[]{:S(2)}, u32[]{:S(2)}) collective-permute-start(bf16[256,256]{1,0:T(8,128)(2,1)S(1)} %join.1.kv_ref), channel_id=1, source_target_pairs={{0,8},{1,9},{2,10},{3,11},{4,12},{5,13},{6,14},{7,15},{8,16},{9,17... | collective-permute-start | bytes 393224 | tf_op jit(solution)/shard_map/ppermute | solution.py:424
  6.5 4.4 %collective-permute-start.3 = (bf16[256,256]{1,0:T(8,128)(2,1)S(1)}, bf16[256,256]{1,0:T(8,128)(2,1)S(1)}, u32[]{:S(2)}, u32[]{:S(2)}) collective-permute-start(bf16[256,256]{1,0:T(8,128)(2,1)S(1)} %join.1.kv_ref), channel_id=1, source_target_pairs={{0,6},{1,7},{2,4},{3,5},{4,10},{5,11},{6,8},{7,9},{8,14},{9,15},{1... | collective-permute-start | bytes 393224 | tf_op jit(solution)/shard_map/ppermute | solution.py:425
  10.9 2.3 %prepare.1 = (s32[8,128]{1,0:T(8,128)S(1)}, bf16[256,256]{1,0:T(8,128)(2,1)S(1)}, bf16[2048,128]{1,0:T(8,128)(2,1)S(1)}, bf16[128,2048]{1,0:T(8,128)(2,1)S(1)}, ...) custom-call(s32[16]{0:T(128)} %lengths_hbm.1, ...), custom_call_target="tpu_custom_call" | custom-call | flops 268435456 | bytes 1048576 | tf_op jit(solution)/shard_map/prepare/pallas_call | solution.py:390
  13.1 0.0 collective-permute-done.refs_0_
  13.2 1.6 %collective-permute-start.2 = (bf16[256,256]{1,0:T(8,128)(2,1)S(1)}, bf16[256,256]{1,0:T(8,128)(2,1)S(1)}, u32[]{:S(2)}, u32[]{:S(2)}) collective-permute-start(bf16[256,256]{1,0:T(8,128)(2,1)S(1)} %get-tuple-element.66), channel_id=1, source_target_pairs={{0,4},{1,5},{2,6},{3,7},{4,0},{5,1},{6,2},{7,3},{8,12},{9,13},{10,... | collective-permute-start | bytes 393224 | tf_op jit(solution)/shard_map/ppermute | solution.py:418
  14.8 0.5 collective-permute-start.1
  15.3 0.0 collective-permute-done.3.refs_3_
  15.3 2.9 %collective-permute-done.2.refs_2_ = bf16[256,256]{1,0:T(8,128)(2,1)S(1)} collective-permute-done((bf16[256,256]{1,0:T(8,128)(2,1)S(1)}, bf16[256,256]{1,0:T(8,128)(2,1)S(1)}, u32[]{:S(2)}, u32[]{:S(2)}) %collective-permute-start.2) | collective-permute-done | bytes 131104 | tf_op jit(solution)/shard_map/ppermute | solution.py:418
  18.2 1.5 %collective-permute-done.1.refs_1_ = bf16[256,256]{1,0:T(8,128)(2,1)S(1)} collective-permute-done((bf16[256,256]{1,0:T(8,128)(2,1)S(1)}, bf16[256,256]{1,0:T(8,128)(2,1)S(1)}, u32[]{:S(2)}, u32[]{:S(2)}) %collective-permute-start.1) | collective-permute-done | bytes 131104 | tf_op jit(solution)/shard_map/ppermute | solution.py:418
  19.7 0.1 pad_maximum_fusion
  19.8 0.1 collective-permute-start.4
  19.9 0.2 attend_even.1
  20.1 1.7 %collective-permute-done.4.kv_odd = bf16[4,256,256]{2,1,0:T(8,128)(2,1)S(1)} collective-permute-done((bf16[4,256,256]{2,1,0:T(8,128)(2,1)S(1)}, bf16[4,256,256]{2,1,0:T(8,128)(2,1)S(1)}, u32[]{:S(2)}, u32[]{:S(2)}) %collective-permute-start.4) | collective-permute-done | bytes 524320 | tf_op jit(solution)/shard_map/ppermute | solution.py:418
  21.8 2.6 %forward.1 = (bf16[256,1024]{1,0:T(8,128)(2,1)}, bf16[4,256,128]{2,1,0:T(8,128)(2,1)S(1)}, bf16[4,2048,256]{2,1,0:T(8,128)(2,1)S(1)}, bf16[2048,128]{1,0:T(8,128...) custom-call(s32[8,128]{1,0:T(8,128)S(1)} %get-tuple-element.32.facts, ...), custom_call_target="tpu_custom_call", output_to_operand_aliasing={{7}: (10, {}), {8}: (11, {})} | custom-call | flops 2684354560 | bytes 1048576 | tf_op jit(solution)/shard_map/forward/pallas_call | solution.py:390
  24.4 0.0 copy-start
  24.4 1.9 %copy-done = bf16[4,2048,256]{2,1,0:T(8,128)(2,1)} copy-done((bf16[4,2048,256]{2,1,0:T(8,128)(2,1)}, bf16[4,2048,256]{2,1,0:T(8,128)(2,1)S(1)}, u32[]{:S(2)}) %copy-start) | copy-done | bytes 4194328
  26.3 0.0 copy-start.3
  26.3 2.0 %copy-done.3 = bf16[4,2048,256]{2,1,0:T(8,128)(2,1)} copy-done((bf16[4,2048,256]{2,1,0:T(8,128)(2,1)}, bf16[4,2048,256]{2,1,0:T(8,128)(2,1)S(1)}, u32[]{:S(2)}) %copy-start.3) | copy-done | bytes 4194328
  28.4 0.0 copy-start.5
  28.4 0.9 %copy-done.5 = bf16[2048,128]{1,0:T(8,128)(2,1)} copy-done((bf16[2048,128]{1,0:T(8,128)(2,1)}, bf16[2048,128]{1,0:T(8,128)(2,1)S(1)}, u32[]{:S(2)}) %copy-start.5) | copy-done | bytes 524312
  29.2 0.0 copy-start.8
  29.2 0.8 %copy-done.8 = bf16[128,2048]{1,0:T(8,128)(2,1)} copy-done((bf16[128,2048]{1,0:T(8,128)(2,1)}, bf16[128,2048]{1,0:T(8,128)(2,1)S(1)}, u32[]{:S(2)}) %copy-start.8) | copy-done | bytes 524312
  30.0 1.4 %collective-permute-start.5 = (bf16[4,256,256]{2,1,0:T(8,128)(2,1)}, bf16[4,256,256]{2,1,0:T(8,128)(2,1)}, u32[]{:S(2)}, u32[]{:S(2)}) collective-permute-start(bf16[4,256,256]{2,1,0:T(8,128)(2,1)} %get-tuple-element.55), channel_id=1, source_target_pairs={{0,1},{1,0},{2,3},{3,2},{4,5},{5,4},{6,7},{7,6},{8,9},{9,8},{10,11... | collective-permute-start | bytes 1572872 | tf_op jit(solution)/shard_map/ppermute | solution.py:418
  31.4 0.0 copy-start.1
  31.5 2.2 %copy-done.1 = bf16[4,2048,256]{2,1,0:T(8,128)(2,1)S(1)} copy-done((bf16[4,2048,256]{2,1,0:T(8,128)(2,1)S(1)}, bf16[4,2048,256]{2,1,0:T(8,128)(2,1)}, u32[]{:S(2)}) %copy-start.1) | copy-done | bytes 4194328
  33.6 0.0 copy-start.6
  33.6 1.0 %copy-done.6 = bf16[2048,128]{1,0:T(8,128)(2,1)S(1)} copy-done((bf16[2048,128]{1,0:T(8,128)(2,1)S(1)}, bf16[2048,128]{1,0:T(8,128)(2,1)}, u32[]{:S(2)}) %copy-start.6) | copy-done | bytes 524312
  34.7 0.0 copy-start.9
  34.7 1.0 %copy-done.9 = bf16[128,2048]{1,0:T(8,128)(2,1)S(1)} copy-done((bf16[128,2048]{1,0:T(8,128)(2,1)S(1)}, bf16[128,2048]{1,0:T(8,128)(2,1)}, u32[]{:S(2)}) %copy-start.9) | copy-done | bytes 524312
  35.7 0.0 copy-start.2
  35.7 0.0 copy-start.4
  35.7 0.0 copy-start.7
  35.7 0.0 copy-start.10
  35.7 0.1 even.1
  35.9 0.0 collective-permute-done.5
  35.9 1.3 %convert_element_type.33 = f32[4,256,256]{2,1,0:T(8,128)S(1)} convert(bf16[4,256,256]{2,1,0:T(8,128)(2,1)} %collective-permute-done.5) | non-fusion elementwise | flops 262144 | bytes 1572864 | tf_op jit(solution)/shard_map/convert_element_type | solution.py:446
  37.2 0.1 fusion.12
  37.3 5.0 %collective-permute-start.8 = (bf16[256,256]{1,0:T(8,128)(2,1)S(1)}, bf16[256,256]{1,0:T(8,128)(2,1)S(1)}, u32[]{:S(2)}, u32[]{:S(2)}) collective-permute-start(bf16[256,256]{1,0:T(8,128)(2,1)S(1)} %get-tuple-element.60), channel_id=1, source_target_pairs={{0,6},{1,7},{2,4},{3,5},{4,2},{5,3},{6,0},{7,1},{8,14},{9,15},{10,... | collective-permute-start | bytes 393224 | tf_op jit(solution)/shard_map/ppermute | solution.py:418
  42.3 0.0 collective-permute-start.7
  42.3 0.6 %collective-permute-start.6 = (bf16[256,256]{1,0:T(8,128)(2,1)S(1)}, bf16[256,256]{1,0:T(8,128)(2,1)S(1)}, u32[]{:S(2)}, u32[]{:S(2)}) collective-permute-start(bf16[256,256]{1,0:T(8,128)(2,1)S(1)} %get-tuple-element.62), channel_id=1, source_target_pairs={{0,2},{1,3},{2,0},{3,1},{4,6},{5,7},{6,4},{7,5},{8,10},{9,11},{10,... | collective-permute-start | bytes 393224 | tf_op jit(solution)/shard_map/ppermute | solution.py:418
  42.9 0.0 copy-done.2
  43.0 0.0 copy-done.4
  43.0 0.0 copy-done.7
  43.0 0.0 copy-done.10
  43.0 2.3 %rest.1 = (bf16[256,1024]{1,0:T(8,128)(2,1)}, f32[256,256]{1,0:T(8,128)S(1)}, f32[256,256]{1,0:T(8,128)S(1)}) custom-call(s32[8,128]{1,0:T(8,128)S(1)} %get-tuple-element.32.facts, bf16[128,2048]{1,0:T(8,128)(2,1)S(1)} %get-tuple-element.34.q_t, bf16[2048,128]{1,0:T(8,128)(2,1)S(1)} %copy-done.7, bf16[128,2048]{1,0:T(8,128)(2,1)S(1)} %copy-done.10, ...), custom_call_target="tpu_custom_call" | custom-call | flops 2013265920 | bytes 1048576 | tf_op jit(solution)/shard_map/rest/pallas_call | solution.py:390
  45.3 0.5 collective-permute-done.8
  45.8 1.7 %collective-permute-done.7 = bf16[256,256]{1,0:T(8,128)(2,1)S(1)} collective-permute-done((bf16[256,256]{1,0:T(8,128)(2,1)S(1)}, bf16[256,256]{1,0:T(8,128)(2,1)S(1)}, u32[]{:S(2)}, u32[]{:S(2)}) %collective-permute-start.7) | collective-permute-done | bytes 131104 | tf_op jit(solution)/shard_map/ppermute | solution.py:418
  47.5 1.7 %collective-permute-done.6 = bf16[256,256]{1,0:T(8,128)(2,1)S(1)} collective-permute-done((bf16[256,256]{1,0:T(8,128)(2,1)S(1)}, bf16[256,256]{1,0:T(8,128)(2,1)S(1)}, u32[]{:S(2)}, u32[]{:S(2)}) %collective-permute-start.6) | collective-permute-done | bytes 131104 | tf_op jit(solution)/shard_map/ppermute | solution.py:418
  49.1 0.2 fusion.6
  49.3 1.3 %collective-permute-start.9 = (bf16[256,256]{1,0:T(8,128)(2,1)S(1)}, bf16[256,256]{1,0:T(8,128)(2,1)S(1)}, u32[]{:S(2)}, u32[]{:S(2)}) collective-permute-start(bf16[256,256]{1,0:T(8,128)(2,1)S(1)} %get-tuple-element.63), channel_id=1, source_target_pairs={{8,0},{9,1},{10,2},{11,3},{12,4},{13,5},{14,6},{15,7},{16,8},{17,9... | collective-permute-start | bytes 393224 | tf_op jit(solution)/shard_map/ppermute | solution.py:459
  50.6 8.6 %collective-permute-done.9.last = bf16[256,256]{1,0:T(8,128)(2,1)S(1)} collective-permute-done((bf16[256,256]{1,0:T(8,128)(2,1)S(1)}, bf16[256,256]{1,0:T(8,128)(2,1)S(1)}, u32[]{:S(2)}, u32[]{:S(2)}) %collective-permute-start.9) | collective-permute-done | bytes 131104 | tf_op jit(solution)/shard_map/ppermute | solution.py:459
  59.2 0.7 %finish.1 = (bf16[256,128]{1,0:T(8,128)(2,1)}, bf16[256,128]{1,0:T(8,128)(2,1)}) custom-call(f32[256,256]{1,0:T(8,128)S(1)} %get-tuple-element.64.total, bf16[256,256]{1,0:T(8,128)(2,1)S(1)} %collective-permute-done.9.last), custom_call_target="tpu_custom_call" | custom-call | flops 1 | bytes 1048576 | tf_op jit(solution)/shard_map/finish/pallas_call | solution.py:390
  (1 shorter events, 0.0 us)
Async XLA Ops:
  1.5 11.6 %collective-permute-start = (bf16[256,256]{1,0:T(8,128)(2,1)S(1)}, bf16[256,256]{1,0:T(8,128)(2,1)S(1)}, u32[]{:S(2)}, u32[]{:S(2)}) collective-permute-start(bf16[256,256]{1,0:T(8,128)(2,1)S(1)} %join.1.kv_ref), channel_id=1, source_target_pairs={{0,8},{1,9},{2,10},{3,11},{4,12},{5,13},{6,14},{7,15},{8,16},{9,17... | collective-permute-start | bytes 393224 | tf_op jit(solution)/shard_map/ppermute | solution.py:424
  6.5 8.8 %collective-permute-start.3 = (bf16[256,256]{1,0:T(8,128)(2,1)S(1)}, bf16[256,256]{1,0:T(8,128)(2,1)S(1)}, u32[]{:S(2)}, u32[]{:S(2)}) collective-permute-start(bf16[256,256]{1,0:T(8,128)(2,1)S(1)} %join.1.kv_ref), channel_id=1, source_target_pairs={{0,6},{1,7},{2,4},{3,5},{4,10},{5,11},{6,8},{7,9},{8,14},{9,15},{1... | collective-permute-start | bytes 393224 | tf_op jit(solution)/shard_map/ppermute | solution.py:425
  13.2 5.0 %collective-permute-start.2 = (bf16[256,256]{1,0:T(8,128)(2,1)S(1)}, bf16[256,256]{1,0:T(8,128)(2,1)S(1)}, u32[]{:S(2)}, u32[]{:S(2)}) collective-permute-start(bf16[256,256]{1,0:T(8,128)(2,1)S(1)} %get-tuple-element.66), channel_id=1, source_target_pairs={{0,4},{1,5},{2,6},{3,7},{4,0},{5,1},{6,2},{7,3},{8,12},{9,13},{10,... | collective-permute-start | bytes 393224 | tf_op jit(solution)/shard_map/ppermute | solution.py:418
  14.8 5.0 %collective-permute-start.1 = (bf16[256,256]{1,0:T(8,128)(2,1)S(1)}, bf16[256,256]{1,0:T(8,128)(2,1)S(1)}, u32[]{:S(2)}, u32[]{:S(2)}) collective-permute-start(bf16[256,256]{1,0:T(8,128)(2,1)S(1)} %get-tuple-element.67), channel_id=1, source_target_pairs={{0,2},{1,3},{2,0},{3,1},{4,6},{5,7},{6,4},{7,5},{8,10},{9,11},{10,... | collective-permute-start | bytes 393224 | tf_op jit(solution)/shard_map/ppermute | solution.py:418
  19.8 2.0 %collective-permute-start.4 = (bf16[4,256,256]{2,1,0:T(8,128)(2,1)S(1)}, bf16[4,256,256]{2,1,0:T(8,128)(2,1)S(1)}, u32[]{:S(2)}, u32[]{:S(2)}) collective-permute-start(bf16[4,256,256]{2,1,0:T(8,128)(2,1)S(1)} %pad_maximum_fusion), channel_id=1, source_target_pairs={{0,1},{1,0},{2,3},{3,2},{4,5},{5,4},{6,7},{7,6},{8,9},{9,8},{10,11... | collective-permute-start | bytes 1572872 | tf_op jit(solution)/shard_map/ppermute | solution.py:418
  24.4 2.0 %copy-start = (bf16[4,2048,256]{2,1,0:T(8,128)(2,1)}, bf16[4,2048,256]{2,1,0:T(8,128)(2,1)S(1)}, u32[]{:S(2)}) copy-start(bf16[4,2048,256]{2,1,0:T(8,128)(2,1)S(1)} %get-tuple-element.47.p_even) | copy-start | bytes 12582916
  26.3 2.0 %copy-start.3 = (bf16[4,2048,256]{2,1,0:T(8,128)(2,1)}, bf16[4,2048,256]{2,1,0:T(8,128)(2,1)S(1)}, u32[]{:S(2)}) copy-start(bf16[4,2048,256]{2,1,0:T(8,128)(2,1)S(1)} %get-tuple-element.51.ds_odd) | copy-start | bytes 12582916
  28.4 0.9 %copy-start.5 = (bf16[2048,128]{1,0:T(8,128)(2,1)}, bf16[2048,128]{1,0:T(8,128)(2,1)S(1)}, u32[]{:S(2)}) copy-start(bf16[2048,128]{1,0:T(8,128)(2,1)S(1)} %get-tuple-element.45.do_s) | copy-start | bytes 1572868
  29.2 0.8 %copy-start.8 = (bf16[128,2048]{1,0:T(8,128)(2,1)}, bf16[128,2048]{1,0:T(8,128)(2,1)S(1)}, u32[]{:S(2)}) copy-start(bf16[128,2048]{1,0:T(8,128)(2,1)S(1)} %get-tuple-element.46.do_t) | copy-start | bytes 1572868
  30.0 5.9 %collective-permute-start.5 = (bf16[4,256,256]{2,1,0:T(8,128)(2,1)}, bf16[4,256,256]{2,1,0:T(8,128)(2,1)}, u32[]{:S(2)}, u32[]{:S(2)}) collective-permute-start(bf16[4,256,256]{2,1,0:T(8,128)(2,1)} %get-tuple-element.55), channel_id=1, source_target_pairs={{0,1},{1,0},{2,3},{3,2},{4,5},{5,4},{6,7},{7,6},{8,9},{9,8},{10,11... | collective-permute-start | bytes 1572872 | tf_op jit(solution)/shard_map/ppermute | solution.py:418
  31.4 2.2 %copy-start.1 = (bf16[4,2048,256]{2,1,0:T(8,128)(2,1)S(1)}, bf16[4,2048,256]{2,1,0:T(8,128)(2,1)}, u32[]{:S(2)}) copy-start(bf16[4,2048,256]{2,1,0:T(8,128)(2,1)} %copy-done) | copy-start | bytes 12582916
  33.6 1.0 %copy-start.6 = (bf16[2048,128]{1,0:T(8,128)(2,1)S(1)}, bf16[2048,128]{1,0:T(8,128)(2,1)}, u32[]{:S(2)}) copy-start(bf16[2048,128]{1,0:T(8,128)(2,1)} %copy-done.5) | copy-start | bytes 1572868
  34.7 1.0 %copy-start.9 = (bf16[128,2048]{1,0:T(8,128)(2,1)S(1)}, bf16[128,2048]{1,0:T(8,128)(2,1)}, u32[]{:S(2)}) copy-start(bf16[128,2048]{1,0:T(8,128)(2,1)} %copy-done.8) | copy-start | bytes 1572868
  35.7 7.2 %copy-start.2 = (bf16[4,2048,256]{2,1,0:T(8,128)(2,1)S(1)}, bf16[4,2048,256]{2,1,0:T(8,128)(2,1)}, u32[]{:S(2)}) copy-start(bf16[4,2048,256]{2,1,0:T(8,128)(2,1)} %copy-done) | copy-start | bytes 12582916
  35.7 7.2 %copy-start.4 = (bf16[4,2048,256]{2,1,0:T(8,128)(2,1)S(1)}, bf16[4,2048,256]{2,1,0:T(8,128)(2,1)}, u32[]{:S(2)}) copy-start(bf16[4,2048,256]{2,1,0:T(8,128)(2,1)} %copy-done.3) | copy-start | bytes 12582916
  35.7 7.2 %copy-start.7 = (bf16[2048,128]{1,0:T(8,128)(2,1)S(1)}, bf16[2048,128]{1,0:T(8,128)(2,1)}, u32[]{:S(2)}) copy-start(bf16[2048,128]{1,0:T(8,128)(2,1)} %copy-done.5) | copy-start | bytes 1572868
  35.7 7.2 %copy-start.10 = (bf16[128,2048]{1,0:T(8,128)(2,1)S(1)}, bf16[128,2048]{1,0:T(8,128)(2,1)}, u32[]{:S(2)}) copy-start(bf16[128,2048]{1,0:T(8,128)(2,1)} %copy-done.8) | copy-start | bytes 1572868
  37.3 8.5 %collective-permute-start.8 = (bf16[256,256]{1,0:T(8,128)(2,1)S(1)}, bf16[256,256]{1,0:T(8,128)(2,1)S(1)}, u32[]{:S(2)}, u32[]{:S(2)}) collective-permute-start(bf16[256,256]{1,0:T(8,128)(2,1)S(1)} %get-tuple-element.60), channel_id=1, source_target_pairs={{0,6},{1,7},{2,4},{3,5},{4,2},{5,3},{6,0},{7,1},{8,14},{9,15},{10,... | collective-permute-start | bytes 393224 | tf_op jit(solution)/shard_map/ppermute | solution.py:418
  42.3 5.2 %collective-permute-start.7 = (bf16[256,256]{1,0:T(8,128)(2,1)S(1)}, bf16[256,256]{1,0:T(8,128)(2,1)S(1)}, u32[]{:S(2)}, u32[]{:S(2)}) collective-permute-start(bf16[256,256]{1,0:T(8,128)(2,1)S(1)} %get-tuple-element.61), channel_id=1, source_target_pairs={{0,4},{1,5},{2,6},{3,7},{4,0},{5,1},{6,2},{7,3},{8,12},{9,13},{10,... | collective-permute-start | bytes 393224 | tf_op jit(solution)/shard_map/ppermute | solution.py:418
  42.3 6.8 %collective-permute-start.6 = (bf16[256,256]{1,0:T(8,128)(2,1)S(1)}, bf16[256,256]{1,0:T(8,128)(2,1)S(1)}, u32[]{:S(2)}, u32[]{:S(2)}) collective-permute-start(bf16[256,256]{1,0:T(8,128)(2,1)S(1)} %get-tuple-element.62), channel_id=1, source_target_pairs={{0,2},{1,3},{2,0},{3,1},{4,6},{5,7},{6,4},{7,5},{8,10},{9,11},{10,... | collective-permute-start | bytes 393224 | tf_op jit(solution)/shard_map/ppermute | solution.py:418
  49.3 9.9 %collective-permute-start.9 = (bf16[256,256]{1,0:T(8,128)(2,1)S(1)}, bf16[256,256]{1,0:T(8,128)(2,1)S(1)}, u32[]{:S(2)}, u32[]{:S(2)}) collective-permute-start(bf16[256,256]{1,0:T(8,128)(2,1)S(1)} %get-tuple-element.63), channel_id=1, source_target_pairs={{8,0},{9,1},{10,2},{11,3},{12,4},{13,5},{14,6},{15,7},{16,8},{17,9... | collective-permute-start | bytes 393224 | tf_op jit(solution)/shard_map/ppermute | solution.py:459

commit v4 on v3

--- a/solution.py
+++ b/solution.py
@@ -101,8 +101,9 @@
     return copies
 
 
-def join(keys, values, kv, sems):
-    for copy in fetch([(keys, kv.at[:, pl.ds(0, HDIM)]), (values, kv.at[:, pl.ds(HDIM, HDIM)])], sems):
+def join(keys, values, *refs):
+    *joined, sems = refs
+    for copy in fetch([(source, kv.at[:, pl.ds(lane, HDIM)]) for kv in joined for source, lane in ((keys, 0), (values, HDIM))], sems):
         copy.wait()
 
 
@@ -371,12 +372,11 @@
     return sum(math.prod(array.shape) * jnp.dtype(array.dtype).itemsize for array in arrays)
 
 
-def call(body, name, outs, args, scratch, flops, resident, aliases=(), away=(), leaves=(), final=(), copies=0):
+def call(body, name, outs, args, scratch, flops, resident, aliases=(), away=(), leaves=(), copies=0):
     vmem = pl.BlockSpec(memory_space=pltpu.VMEM)
     anywhere = pl.BlockSpec(memory_space=pl.ANY)
     hbm = pl.BlockSpec(memory_space=pltpu.HBM)
-    outs = tuple(jax.ShapeDtypeStruct(shape, dtype) if i in final or not resident else pltpu.VMEM(shape, dtype)
-                 for i, (shape, dtype) in enumerate(outs))
+    outs = tuple(jax.ShapeDtypeStruct(shape, dtype) for shape, dtype in outs)
     held = size_of(scratch) + 8 * 2**20
     if not resident:
         held = min(held + size_of(outs) + size_of(args), 62 * 2**20)
@@ -419,10 +419,10 @@
 
     later = [ctx < ctx ^ max(2 * i, 1) for i in range(pairs)]
 
-    kv, = run(join, "join", [(block, BF16)], (keys, values), [], 1, away=(0, 1), copies=2)
+    kv, kv_again = run(join, "join", [(block, BF16)] * 2, (keys, values), [], 1, away=(0, 1), copies=4)
     near = lambda i: i & (i - 1) == 0
     prev = lax.ppermute(kv, axes, run_route(n_dp, n_ctx))
-    straight = {i: lax.ppermute(kv, axes, straight_route(n_dp, n_ctx, 2 * i)) for i in range(1, pairs) if not near(i)}
+    straight = {i: lax.ppermute(kv_again, axes, straight_route(n_dp, n_ctx, 2 * i)) for i in range(1, pairs) if not near(i)}
     facts, kv_own, q_s, q_t, do_r, start, level, p_own, acc = kernel(
         prepare, [((8, HDIM), jnp.int32), (block, BF16), (by_row, BF16), (by_lane, BF16), (by_row, BF16),
                   ((rows, rows), jnp.int32), (by_row, F32), ((many, rows), BF16), ((many, 2 * HDIM), F32)],
@@ -442,7 +442,7 @@
         (facts, q_s, q_t, do_r, start, level, acc, kv_own, kv_even, passed, p_own, p_even),
         [pltpu.VMEM(queries.shape, BF16), pltpu.VMEM((pairs, many, rows), BF16), pltpu.VMEM((many, 2 * HDIM), F32),
          pltpu.VMEM(by_row, F32), pltpu.VMEM((many, rows), BF16), pltpu.VMEM(block, BF16)],
-        5 * pairs * once, aliases=((10, 7), (11, 8)), leaves=(0,), final=(0,), copies=2)
+        5 * pairs * once, aliases=((10, 7), (11, 8)), leaves=(0,), copies=2)
     partner = swap(g_passed, 1).astype(F32)
     shared = (facts, q_t, do_s, do_t, kv_even, p_even, corr)
     ds_even, g_direct = kernel(even, [((pairs - 1, many, rows), BF16), ((pairs - 1,) + block, F32)],
@@ -450,14 +450,14 @@
     terms = [partner[0]] + [swap((g_direct[i - 1] + partner[i]).astype(BF16), 2 * i).astype(F32) for i in range(1, pairs)]
     grad_queries, g_own, g_prev = kernel(rest, [(queries.shape, BF16), (block, F32), (block, F32)],
                                          shared + (kv_own, p_own, k_odd, ds_odd, ds_even),
-                                         [pltpu.VMEM(by_row, F32)], (n_ctx + 7) * once, final=(0,))
+                                         [pltpu.VMEM(by_row, F32)], (n_ctx + 7) * once)
     own_total, prev_total = g_own, g_prev
     for after, term in zip(later, terms):
         own_total = own_total + jnp.where(after, term, 0.0)
         prev_total = prev_total + jnp.where(after, 0.0, term)
     back = [(b, a) for a, b in run_route(n_dp, n_ctx)]
     last = lax.ppermute(prev_total.astype(BF16), axes, back)
-    grad_keys, grad_values = run(finish, "finish", [(keys.shape, BF16), (values.shape, BF16)], (own_total, last), [], 1, final=(0, 1))
+    grad_keys, grad_values = run(finish, "finish", [(keys.shape, BF16), (values.shape, BF16)], (own_total, last), [], 1)
     return (attn_out, grad_queries, grad_keys, grad_values)
 
 

time: 60.8 us -> 59.5 us (0.979)
  starting transfers between devices: 19.8 us -> 18.9 us
    ppermute x7, waiting for transfers between devices: 9.97 us -> 8.77 us  [swap(): return lax.ppermute(blocks, axes, flip_route(n_dp, n_ctx, flip))]
    ppermute x7, starting transfers between devices: 9.24 us -> 8.27 us  [swap(): return lax.ppermute(blocks, axes, flip_route(n_dp, n_ctx, flip))]
  transfers between devices with their start and end apart: 10 -> 10, of which waited for: 7 -> 6; matrix products, arithmetic and copies ran while one was open for 0% -> 0% of each run, Pallas kernels for 8% -> 8%
where the time goes in v4:
time: 59.5 us; the launch traced here: 58.3 us
  starting transfers between devices  18.9 us (32%)
  waiting for transfers between devices  17.9 us (30%)
  local copies, waits for them, and re-layouts  9.93 us (17%)
  Pallas kernels  9.19 us (15%)
  other arithmetic  1.67 us (3%)
  between operations  0.81 us (1%)
    unnamed x22, local copies, waits for them, and re-layouts  9.93 us
    pallas_call x7, Pallas kernels, call(): pl.pallas_call(body, out_shape=outs, in_specs=in_specs, out_specs=tuple(o...  9.19 us
    ppermute x1, waiting for transfers between devices, shards(): last = lax.ppermute(prev_total.astype(BF16), axes, back)  9.12 us
    ppermute x7, waiting for transfers between devices, swap(): return lax.ppermute(blocks, axes, flip_route(n_dp, n_ctx, flip))  8.77 us
    ppermute x7, starting transfers between devices, swap(): return lax.ppermute(blocks, axes, flip_route(n_dp, n_ctx, flip))  8.27 us
    ppermute x1, starting transfers between devices, shards(): prev = lax.ppermute(kv, axes, run_route(n_dp, n_ctx))  4.94 us
    ppermute x1, starting transfers between devices, shards(): lax.ppermute(kv_again, axes, straight_route(n_dp, n_ctx, 2 * i))  4.36 us
    ppermute x1, starting transfers between devices, shards(): last = lax.ppermute(prev_total.astype(BF16), axes, back)  1.29 us
  transfers between devices with their start and end apart: 10, of which 6 were waited for; matrix products, arithmetic and copies ran while one was open for 0% of the time, Pallas kernels for 8%

profile of v4, /device:TPU:0, one launch (start us, length us, event | category | flops | bytes accessed | tf_op | source)
XLA Modules:
  0.0 58.3 jit_solution(16443518561183353289)
XLA Ops:
  0.6 1.0 %join.1 = (bf16[256,256]{1,0:T(8,128)(2,1)S(1)}, bf16[256,256]{1,0:T(8,128)(2,1)S(1)}) custom-call(bf16[256,128]{1,0:T(8,128)(2,1)} %keys.1, bf16[256,128]{1,0:T(8,128)(2,1)} %values.1), custom_call_target="tpu_custom_call" | custom-call | flops 1 | bytes 1048576 | tf_op jit(solution)/shard_map/join/pallas_call | solution.py:390
  1.6 4.9 %collective-permute-start = (bf16[256,256]{1,0:T(8,128)(2,1)S(1)}, bf16[256,256]{1,0:T(8,128)(2,1)S(1)}, u32[]{:S(2)}, u32[]{:S(2)}) collective-permute-start(bf16[256,256]{1,0:T(8,128)(2,1)S(1)} %get-tuple-element.34.kv_ref), channel_id=1, source_target_pairs={{0,8},{1,9},{2,10},{3,11},{4,12},{5,13},{6,14},{7,15},{8,16},{9,17... | collective-permute-start | bytes 393224 | tf_op jit(solution)/shard_map/ppermute | solution.py:424
  6.6 4.4 %collective-permute-start.3 = (bf16[256,256]{1,0:T(8,128)(2,1)S(1)}, bf16[256,256]{1,0:T(8,128)(2,1)S(1)}, u32[]{:S(2)}, u32[]{:S(2)}) collective-permute-start(bf16[256,256]{1,0:T(8,128)(2,1)S(1)} %get-tuple-element.43), channel_id=1, source_target_pairs={{0,6},{1,7},{2,4},{3,5},{4,10},{5,11},{6,8},{7,9},{8,14},{9,15},{1... | collective-permute-start | bytes 393224 | tf_op jit(solution)/shard_map/ppermute | solution.py:425
  10.9 2.3 %prepare.1 = (s32[8,128]{1,0:T(8,128)S(1)}, bf16[256,256]{1,0:T(8,128)(2,1)S(1)}, bf16[2048,128]{1,0:T(8,128)(2,1)S(1)}, bf16[128,2048]{1,0:T(8,128)(2,1)S(1)}, ...) custom-call(s32[16]{0:T(128)} %lengths_hbm.1, ...), custom_call_target="tpu_custom_call" | custom-call | flops 268435456 | bytes 1048576 | tf_op jit(solution)/shard_map/prepare/pallas_call | solution.py:390
  13.2 0.0 collective-permute-done.refs_0_
  13.3 1.6 %collective-permute-start.2 = (bf16[256,256]{1,0:T(8,128)(2,1)S(1)}, bf16[256,256]{1,0:T(8,128)(2,1)S(1)}, u32[]{:S(2)}, u32[]{:S(2)}) collective-permute-start(bf16[256,256]{1,0:T(8,128)(2,1)S(1)} %get-tuple-element.70), channel_id=1, source_target_pairs={{0,4},{1,5},{2,6},{3,7},{4,0},{5,1},{6,2},{7,3},{8,12},{9,13},{10,... | collective-permute-start | bytes 393224 | tf_op jit(solution)/shard_map/ppermute | solution.py:418
  14.8 0.5 collective-permute-start.1
  15.4 0.0 collective-permute-done.3.refs_3_
  15.4 2.9 %collective-permute-done.2.refs_2_ = bf16[256,256]{1,0:T(8,128)(2,1)S(1)} collective-permute-done((bf16[256,256]{1,0:T(8,128)(2,1)S(1)}, bf16[256,256]{1,0:T(8,128)(2,1)S(1)}, u32[]{:S(2)}, u32[]{:S(2)}) %collective-permute-start.2) | collective-permute-done | bytes 131104 | tf_op jit(solution)/shard_map/ppermute | solution.py:418
  18.3 1.5 %collective-permute-done.1.refs_1_ = bf16[256,256]{1,0:T(8,128)(2,1)S(1)} collective-permute-done((bf16[256,256]{1,0:T(8,128)(2,1)S(1)}, bf16[256,256]{1,0:T(8,128)(2,1)S(1)}, u32[]{:S(2)}, u32[]{:S(2)}) %collective-permute-start.1) | collective-permute-done | bytes 131104 | tf_op jit(solution)/shard_map/ppermute | solution.py:418
  19.8 0.1 pad_maximum_fusion
  19.9 0.1 collective-permute-start.4
  20.0 0.2 attend_even.1
  20.2 1.7 %collective-permute-done.4.kv_odd = bf16[4,256,256]{2,1,0:T(8,128)(2,1)S(1)} collective-permute-done((bf16[4,256,256]{2,1,0:T(8,128)(2,1)S(1)}, bf16[4,256,256]{2,1,0:T(8,128)(2,1)S(1)}, u32[]{:S(2)}, u32[]{:S(2)}) %collective-permute-start.4) | collective-permute-done | bytes 524320 | tf_op jit(solution)/shard_map/ppermute | solution.py:418
  21.8 2.6 %forward.1 = (bf16[256,1024]{1,0:T(8,128)(2,1)}, bf16[4,256,128]{2,1,0:T(8,128)(2,1)S(1)}, bf16[4,2048,256]{2,1,0:T(8,128)(2,1)S(1)}, bf16[2048,128]{1,0:T(8,128...) custom-call(s32[8,128]{1,0:T(8,128)S(1)} %get-tuple-element.35.facts, ...), custom_call_target="tpu_custom_call", output_to_operand_aliasing={{7}: (10, {}), {8}: (11, {})} | custom-call | flops 2684354560 | bytes 1048576 | tf_op jit(solution)/shard_map/forward/pallas_call | solution.py:390
  24.5 0.0 copy-start
  24.5 1.9 %copy-done = bf16[4,2048,256]{2,1,0:T(8,128)(2,1)} copy-done((bf16[4,2048,256]{2,1,0:T(8,128)(2,1)}, bf16[4,2048,256]{2,1,0:T(8,128)(2,1)S(1)}, u32[]{:S(2)}) %copy-start) | copy-done | bytes 4194328
  26.4 0.0 copy-start.3
  26.4 2.0 %copy-done.3 = bf16[4,2048,256]{2,1,0:T(8,128)(2,1)} copy-done((bf16[4,2048,256]{2,1,0:T(8,128)(2,1)}, bf16[4,2048,256]{2,1,0:T(8,128)(2,1)S(1)}, u32[]{:S(2)}) %copy-start.3) | copy-done | bytes 4194328
  28.4 0.0 copy-start.5
  28.4 0.9 %copy-done.5 = bf16[2048,128]{1,0:T(8,128)(2,1)} copy-done((bf16[2048,128]{1,0:T(8,128)(2,1)}, bf16[2048,128]{1,0:T(8,128)(2,1)S(1)}, u32[]{:S(2)}) %copy-start.5) | copy-done | bytes 524312
  29.3 0.0 copy-start.8
  29.3 0.8 %copy-done.8 = bf16[128,2048]{1,0:T(8,128)(2,1)} copy-done((bf16[128,2048]{1,0:T(8,128)(2,1)}, bf16[128,2048]{1,0:T(8,128)(2,1)S(1)}, u32[]{:S(2)}) %copy-start.8) | copy-done | bytes 524312
  30.1 1.6 %collective-permute-start.5 = (bf16[4,256,256]{2,1,0:T(8,128)(2,1)}, bf16[4,256,256]{2,1,0:T(8,128)(2,1)}, u32[]{:S(2)}, u32[]{:S(2)}) collective-permute-start(bf16[4,256,256]{2,1,0:T(8,128)(2,1)} %get-tuple-element.59), channel_id=1, source_target_pairs={{0,1},{1,0},{2,3},{3,2},{4,5},{5,4},{6,7},{7,6},{8,9},{9,8},{10,11... | collective-permute-start | bytes 1572872 | tf_op jit(solution)/shard_map/ppermute | solution.py:418
  31.7 0.0 copy-start.1
  31.7 2.2 %copy-done.1 = bf16[4,2048,256]{2,1,0:T(8,128)(2,1)S(1)} copy-done((bf16[4,2048,256]{2,1,0:T(8,128)(2,1)S(1)}, bf16[4,2048,256]{2,1,0:T(8,128)(2,1)}, u32[]{:S(2)}) %copy-start.1) | copy-done | bytes 4194328
  33.9 0.0 copy-start.6
  33.9 1.0 %copy-done.6 = bf16[2048,128]{1,0:T(8,128)(2,1)S(1)} copy-done((bf16[2048,128]{1,0:T(8,128)(2,1)S(1)}, bf16[2048,128]{1,0:T(8,128)(2,1)}, u32[]{:S(2)}) %copy-start.6) | copy-done | bytes 524312
  34.9 0.0 copy-start.9
  34.9 1.0 %copy-done.9 = bf16[128,2048]{1,0:T(8,128)(2,1)S(1)} copy-done((bf16[128,2048]{1,0:T(8,128)(2,1)S(1)}, bf16[128,2048]{1,0:T(8,128)(2,1)}, u32[]{:S(2)}) %copy-start.9) | copy-done | bytes 524312
  36.0 0.0 copy-start.2
  36.0 0.0 copy-start.4
  36.0 0.0 copy-start.7
  36.0 0.0 copy-start.10
  36.0 0.1 even.1
  36.1 0.0 collective-permute-done.5
  36.1 1.3 %convert_element_type.33 = f32[4,256,256]{2,1,0:T(8,128)S(1)} convert(bf16[4,256,256]{2,1,0:T(8,128)(2,1)} %collective-permute-done.5) | non-fusion elementwise | flops 262144 | bytes 1572864 | tf_op jit(solution)/shard_map/convert_element_type | solution.py:446
  37.4 0.1 fusion.12
  37.5 3.0 %collective-permute-start.8 = (bf16[256,256]{1,0:T(8,128)(2,1)S(1)}, bf16[256,256]{1,0:T(8,128)(2,1)S(1)}, u32[]{:S(2)}, u32[]{:S(2)}) collective-permute-start(bf16[256,256]{1,0:T(8,128)(2,1)S(1)} %get-tuple-element.64), channel_id=1, source_target_pairs={{0,6},{1,7},{2,4},{3,5},{4,2},{5,3},{6,0},{7,1},{8,14},{9,15},{10,... | collective-permute-start | bytes 393224 | tf_op jit(solution)/shard_map/ppermute | solution.py:418
  40.5 1.5 %collective-permute-start.7 = (bf16[256,256]{1,0:T(8,128)(2,1)S(1)}, bf16[256,256]{1,0:T(8,128)(2,1)S(1)}, u32[]{:S(2)}, u32[]{:S(2)}) collective-permute-start(bf16[256,256]{1,0:T(8,128)(2,1)S(1)} %get-tuple-element.65), channel_id=1, source_target_pairs={{0,4},{1,5},{2,6},{3,7},{4,0},{5,1},{6,2},{7,3},{8,12},{9,13},{10,... | collective-permute-start | bytes 393224 | tf_op jit(solution)/shard_map/ppermute | solution.py:418
  42.1 0.0 collective-permute-start.6
  42.1 0.0 copy-done.2
  42.1 0.0 copy-done.4
  42.1 0.0 copy-done.7
  42.1 0.0 copy-done.10
  42.1 2.3 %rest.1 = (bf16[256,1024]{1,0:T(8,128)(2,1)}, f32[256,256]{1,0:T(8,128)S(1)}, f32[256,256]{1,0:T(8,128)S(1)}) custom-call(s32[8,128]{1,0:T(8,128)S(1)} %get-tuple-element.35.facts, bf16[128,2048]{1,0:T(8,128)(2,1)S(1)} %get-tuple-element.37.q_t, bf16[2048,128]{1,0:T(8,128)(2,1)S(1)} %copy-done.7, bf16[128,2048]{1,0:T(8,128)(2,1)S(1)} %copy-done.10, ...), custom_call_target="tpu_custom_call" | custom-call | flops 2013265920 | bytes 1048576 | tf_op jit(solution)/shard_map/rest/pallas_call | solution.py:390
  44.4 0.0 collective-permute-done.8
  44.5 2.5 %collective-permute-done.7 = bf16[256,256]{1,0:T(8,128)(2,1)S(1)} collective-permute-done((bf16[256,256]{1,0:T(8,128)(2,1)S(1)}, bf16[256,256]{1,0:T(8,128)(2,1)S(1)}, u32[]{:S(2)}, u32[]{:S(2)}) %collective-permute-start.7) | collective-permute-done | bytes 131104 | tf_op jit(solution)/shard_map/ppermute | solution.py:418
  47.0 0.1 collective-permute-done.6
  47.1 0.2 fusion.6
  47.2 1.3 %collective-permute-start.9 = (bf16[256,256]{1,0:T(8,128)(2,1)S(1)}, bf16[256,256]{1,0:T(8,128)(2,1)S(1)}, u32[]{:S(2)}, u32[]{:S(2)}) collective-permute-start(bf16[256,256]{1,0:T(8,128)(2,1)S(1)} %get-tuple-element.67), channel_id=1, source_target_pairs={{8,0},{9,1},{10,2},{11,3},{12,4},{13,5},{14,6},{15,7},{16,8},{17,9... | collective-permute-start | bytes 393224 | tf_op jit(solution)/shard_map/ppermute | solution.py:459
  48.5 9.1 %collective-permute-done.9.last = bf16[256,256]{1,0:T(8,128)(2,1)S(1)} collective-permute-done((bf16[256,256]{1,0:T(8,128)(2,1)S(1)}, bf16[256,256]{1,0:T(8,128)(2,1)S(1)}, u32[]{:S(2)}, u32[]{:S(2)}) %collective-permute-start.9) | collective-permute-done | bytes 131104 | tf_op jit(solution)/shard_map/ppermute | solution.py:459
  57.7 0.7 %finish.1 = (bf16[256,128]{1,0:T(8,128)(2,1)}, bf16[256,128]{1,0:T(8,128)(2,1)}) custom-call(f32[256,256]{1,0:T(8,128)S(1)} %get-tuple-element.68.total, bf16[256,256]{1,0:T(8,128)(2,1)S(1)} %collective-permute-done.9.last), custom_call_target="tpu_custom_call" | custom-call | flops 1 | bytes 1048576 | tf_op jit(solution)/shard_map/finish/pallas_call | solution.py:390
  (1 shorter events, 0.0 us)
Async XLA Ops:
  1.6 11.6 %collective-permute-start = (bf16[256,256]{1,0:T(8,128)(2,1)S(1)}, bf16[256,256]{1,0:T(8,128)(2,1)S(1)}, u32[]{:S(2)}, u32[]{:S(2)}) collective-permute-start(bf16[256,256]{1,0:T(8,128)(2,1)S(1)} %get-tuple-element.34.kv_ref), channel_id=1, source_target_pairs={{0,8},{1,9},{2,10},{3,11},{4,12},{5,13},{6,14},{7,15},{8,16},{9,17... | collective-permute-start | bytes 393224 | tf_op jit(solution)/shard_map/ppermute | solution.py:424
  6.6 8.8 %collective-permute-start.3 = (bf16[256,256]{1,0:T(8,128)(2,1)S(1)}, bf16[256,256]{1,0:T(8,128)(2,1)S(1)}, u32[]{:S(2)}, u32[]{:S(2)}) collective-permute-start(bf16[256,256]{1,0:T(8,128)(2,1)S(1)} %get-tuple-element.43), channel_id=1, source_target_pairs={{0,6},{1,7},{2,4},{3,5},{4,10},{5,11},{6,8},{7,9},{8,14},{9,15},{1... | collective-permute-start | bytes 393224 | tf_op jit(solution)/shard_map/ppermute | solution.py:425
  13.3 5.0 %collective-permute-start.2 = (bf16[256,256]{1,0:T(8,128)(2,1)S(1)}, bf16[256,256]{1,0:T(8,128)(2,1)S(1)}, u32[]{:S(2)}, u32[]{:S(2)}) collective-permute-start(bf16[256,256]{1,0:T(8,128)(2,1)S(1)} %get-tuple-element.70), channel_id=1, source_target_pairs={{0,4},{1,5},{2,6},{3,7},{4,0},{5,1},{6,2},{7,3},{8,12},{9,13},{10,... | collective-permute-start | bytes 393224 | tf_op jit(solution)/shard_map/ppermute | solution.py:418
  14.8 5.0 %collective-permute-start.1 = (bf16[256,256]{1,0:T(8,128)(2,1)S(1)}, bf16[256,256]{1,0:T(8,128)(2,1)S(1)}, u32[]{:S(2)}, u32[]{:S(2)}) collective-permute-start(bf16[256,256]{1,0:T(8,128)(2,1)S(1)} %get-tuple-element.71), channel_id=1, source_target_pairs={{0,2},{1,3},{2,0},{3,1},{4,6},{5,7},{6,4},{7,5},{8,10},{9,11},{10,... | collective-permute-start | bytes 393224 | tf_op jit(solution)/shard_map/ppermute | solution.py:418
  19.9 2.0 %collective-permute-start.4 = (bf16[4,256,256]{2,1,0:T(8,128)(2,1)S(1)}, bf16[4,256,256]{2,1,0:T(8,128)(2,1)S(1)}, u32[]{:S(2)}, u32[]{:S(2)}) collective-permute-start(bf16[4,256,256]{2,1,0:T(8,128)(2,1)S(1)} %pad_maximum_fusion), channel_id=1, source_target_pairs={{0,1},{1,0},{2,3},{3,2},{4,5},{5,4},{6,7},{7,6},{8,9},{9,8},{10,11... | collective-permute-start | bytes 1572872 | tf_op jit(solution)/shard_map/ppermute | solution.py:418
  24.5 2.0 %copy-start = (bf16[4,2048,256]{2,1,0:T(8,128)(2,1)}, bf16[4,2048,256]{2,1,0:T(8,128)(2,1)S(1)}, u32[]{:S(2)}) copy-start(bf16[4,2048,256]{2,1,0:T(8,128)(2,1)S(1)} %get-tuple-element.51.p_even) | copy-start | bytes 12582916
  26.4 2.0 %copy-start.3 = (bf16[4,2048,256]{2,1,0:T(8,128)(2,1)}, bf16[4,2048,256]{2,1,0:T(8,128)(2,1)S(1)}, u32[]{:S(2)}) copy-start(bf16[4,2048,256]{2,1,0:T(8,128)(2,1)S(1)} %get-tuple-element.55.ds_odd) | copy-start | bytes 12582916
  28.4 0.9 %copy-start.5 = (bf16[2048,128]{1,0:T(8,128)(2,1)}, bf16[2048,128]{1,0:T(8,128)(2,1)S(1)}, u32[]{:S(2)}) copy-start(bf16[2048,128]{1,0:T(8,128)(2,1)S(1)} %get-tuple-element.49.do_s) | copy-start | bytes 1572868
  29.3 0.8 %copy-start.8 = (bf16[128,2048]{1,0:T(8,128)(2,1)}, bf16[128,2048]{1,0:T(8,128)(2,1)S(1)}, u32[]{:S(2)}) copy-start(bf16[128,2048]{1,0:T(8,128)(2,1)S(1)} %get-tuple-element.50.do_t) | copy-start | bytes 1572868
  30.1 6.0 %collective-permute-start.5 = (bf16[4,256,256]{2,1,0:T(8,128)(2,1)}, bf16[4,256,256]{2,1,0:T(8,128)(2,1)}, u32[]{:S(2)}, u32[]{:S(2)}) collective-permute-start(bf16[4,256,256]{2,1,0:T(8,128)(2,1)} %get-tuple-element.59), channel_id=1, source_target_pairs={{0,1},{1,0},{2,3},{3,2},{4,5},{5,4},{6,7},{7,6},{8,9},{9,8},{10,11... | collective-permute-start | bytes 1572872 | tf_op jit(solution)/shard_map/ppermute | solution.py:418
  31.7 2.2 %copy-start.1 = (bf16[4,2048,256]{2,1,0:T(8,128)(2,1)S(1)}, bf16[4,2048,256]{2,1,0:T(8,128)(2,1)}, u32[]{:S(2)}) copy-start(bf16[4,2048,256]{2,1,0:T(8,128)(2,1)} %copy-done) | copy-start | bytes 12582916
  33.9 1.0 %copy-start.6 = (bf16[2048,128]{1,0:T(8,128)(2,1)S(1)}, bf16[2048,128]{1,0:T(8,128)(2,1)}, u32[]{:S(2)}) copy-start(bf16[2048,128]{1,0:T(8,128)(2,1)} %copy-done.5) | copy-start | bytes 1572868
  34.9 1.0 %copy-start.9 = (bf16[128,2048]{1,0:T(8,128)(2,1)S(1)}, bf16[128,2048]{1,0:T(8,128)(2,1)}, u32[]{:S(2)}) copy-start(bf16[128,2048]{1,0:T(8,128)(2,1)} %copy-done.8) | copy-start | bytes 1572868
  36.0 6.1 %copy-start.2 = (bf16[4,2048,256]{2,1,0:T(8,128)(2,1)S(1)}, bf16[4,2048,256]{2,1,0:T(8,128)(2,1)}, u32[]{:S(2)}) copy-start(bf16[4,2048,256]{2,1,0:T(8,128)(2,1)} %copy-done) | copy-start | bytes 12582916
  36.0 6.1 %copy-start.4 = (bf16[4,2048,256]{2,1,0:T(8,128)(2,1)S(1)}, bf16[4,2048,256]{2,1,0:T(8,128)(2,1)}, u32[]{:S(2)}) copy-start(bf16[4,2048,256]{2,1,0:T(8,128)(2,1)} %copy-done.3) | copy-start | bytes 12582916
  36.0 6.1 %copy-start.7 = (bf16[2048,128]{1,0:T(8,128)(2,1)S(1)}, bf16[2048,128]{1,0:T(8,128)(2,1)}, u32[]{:S(2)}) copy-start(bf16[2048,128]{1,0:T(8,128)(2,1)} %copy-done.5) | copy-start | bytes 1572868
  36.0 6.1 %copy-start.10 = (bf16[128,2048]{1,0:T(8,128)(2,1)S(1)}, bf16[128,2048]{1,0:T(8,128)(2,1)}, u32[]{:S(2)}) copy-start(bf16[128,2048]{1,0:T(8,128)(2,1)} %copy-done.8) | copy-start | bytes 1572868
  37.5 6.9 %collective-permute-start.8 = (bf16[256,256]{1,0:T(8,128)(2,1)S(1)}, bf16[256,256]{1,0:T(8,128)(2,1)S(1)}, u32[]{:S(2)}, u32[]{:S(2)}) collective-permute-start(bf16[256,256]{1,0:T(8,128)(2,1)S(1)} %get-tuple-element.64), channel_id=1, source_target_pairs={{0,6},{1,7},{2,4},{3,5},{4,2},{5,3},{6,0},{7,1},{8,14},{9,15},{10,... | collective-permute-start | bytes 393224 | tf_op jit(solution)/shard_map/ppermute | solution.py:418
  40.5 6.5 %collective-permute-start.7 = (bf16[256,256]{1,0:T(8,128)(2,1)S(1)}, bf16[256,256]{1,0:T(8,128)(2,1)S(1)}, u32[]{:S(2)}, u32[]{:S(2)}) collective-permute-start(bf16[256,256]{1,0:T(8,128)(2,1)S(1)} %get-tuple-element.65), channel_id=1, source_target_pairs={{0,4},{1,5},{2,6},{3,7},{4,0},{5,1},{6,2},{7,3},{8,12},{9,13},{10,... | collective-permute-start | bytes 393224 | tf_op jit(solution)/shard_map/ppermute | solution.py:418
  42.1 5.0 %collective-permute-start.6 = (bf16[256,256]{1,0:T(8,128)(2,1)S(1)}, bf16[256,256]{1,0:T(8,128)(2,1)S(1)}, u32[]{:S(2)}, u32[]{:S(2)}) collective-permute-start(bf16[256,256]{1,0:T(8,128)(2,1)S(1)} %get-tuple-element.66), channel_id=1, source_target_pairs={{0,2},{1,3},{2,0},{3,1},{4,6},{5,7},{6,4},{7,5},{8,10},{9,11},{10,... | collective-permute-start | bytes 393224 | tf_op jit(solution)/shard_map/ppermute | solution.py:418
  47.2 10.4 %collective-permute-start.9 = (bf16[256,256]{1,0:T(8,128)(2,1)S(1)}, bf16[256,256]{1,0:T(8,128)(2,1)S(1)}, u32[]{:S(2)}, u32[]{:S(2)}) collective-permute-start(bf16[256,256]{1,0:T(8,128)(2,1)S(1)} %get-tuple-element.67), channel_id=1, source_target_pairs={{8,0},{9,1},{10,2},{11,3},{12,4},{13,5},{14,6},{15,7},{16,8},{17,9... | collective-permute-start | bytes 393224 | tf_op jit(solution)/shard_map/ppermute | solution.py:459

commit v5 on v4

--- a/solution.py
+++ b/solution.py
@@ -101,9 +101,8 @@
     return copies
 
 
-def join(keys, values, *refs):
-    *joined, sems = refs
-    for copy in fetch([(source, kv.at[:, pl.ds(lane, HDIM)]) for kv in joined for source, lane in ((keys, 0), (values, HDIM))], sems):
+def join(keys, values, kv, sems):
+    for copy in fetch([(keys, kv.at[:, pl.ds(0, HDIM)]), (values, kv.at[:, pl.ds(HDIM, HDIM)])], sems):
         copy.wait()
 
 
@@ -202,7 +201,7 @@
 
 
 def forward(n_ctx, facts, q_s, q_t, do_r, start, level, acc_in, kv_own, kv_even, kv_odd, p_own_in, p_even_in,
-            o_hbm, k_odd, ds_odd, do_s, do_t, corr, g_passed, p_own, p_even, o_ref, p_odd, acc, top, p_new, kv_now, sems):
+            o_hbm, k_odd, ds_odd, do_s, do_t, corr, g_passed, p_own, p_even, o_ref, p_odd, acc, p_new, kv_now, sems):
     rows = o_ref.shape[0]
     size = rows // n_ctx
     place = Place(n_ctx, rows, facts)
@@ -241,6 +240,10 @@
                 @pl.when((back > 0) & (lax.rem(back, 2) == 0))
                 def _():
                     kv_now[...] = kv_even[at]
+
+                half = lax.div(back, 2)
+                targets = ((back == 0, p_own), (lax.rem(back, 2) == 1, p_odd.at[half]),
+                           ((back > 0) & (lax.rem(back, 2) == 0), p_even.at[jnp.maximum(half - 1, 0)]))
 
                 @pl.loop(0, n_ctx)
                 def _(c):
@@ -252,29 +255,27 @@
                     s = dot(q_s[here, :], kv_now[:, :HDIM], NT) * EXP2_SCALE
                     step(here, (s.reshape(HEADS, size, rows) + off[None]).reshape(HEADS * size, rows))
 
-                if step is replace:
-                    half = lax.div(back, 2)
-                    for fits, target in ((back == 0, p_own), (lax.rem(back, 2) == 1, p_odd.at[half]),
-                                         ((back > 0) & (lax.rem(back, 2) == 0), p_even.at[jnp.maximum(half - 1, 0)])):
-
-                        @pl.when(fits)
-                        def _():
-                            copy = pltpu.make_async_copy(p_new, target, sems.at[0])
-                            copy.start()
-                            copy.wait()
+                    if step is replace:
+                        for fits, target in targets:
+
+                            @pl.when(fits)
+                            def _():
+                                copy = pltpu.make_async_copy(p_new, target.at[here], sems.at[0])
+                                copy.start()
+                                copy.wait()
 
         def highest(here, s):
-            top[here, :] = jnp.maximum(top[here, :], row_max(fold(s)))
+            corr[here, :] = jnp.maximum(corr[here, :], row_max(fold(s)))
 
         def replace(here, s):
-            p = jnp.exp2(s - wide(top[here, :])).astype(BF16)
-            p_new[here, :] = p
+            p = jnp.exp2(s - wide(corr[here, :])).astype(BF16)
+            p_new[...] = p
             acc[here, :] += dot(p, ones_beside(kv_now[:, HDIM:]))
 
         @pl.loop(0, n_ctx)
         def _(c):
             here = pl.ds(c * HEADS * size, HEADS * size)
-            top[here, :] = jnp.full((HEADS * size, HDIM), NEG_FILL, F32)
+            corr[here, :] = jnp.full((HEADS * size, HDIM), NEG_FILL, F32)
             acc[here, :] = jnp.zeros((HEADS * size, 2 * HDIM), F32)
 
         each(highest)
@@ -419,10 +420,10 @@
 
     later = [ctx < ctx ^ max(2 * i, 1) for i in range(pairs)]
 
-    kv, kv_again = run(join, "join", [(block, BF16)] * 2, (keys, values), [], 1, away=(0, 1), copies=4)
+    kv, = run(join, "join", [(block, BF16)], (keys, values), [], 1, away=(0, 1), copies=2)
     near = lambda i: i & (i - 1) == 0
     prev = lax.ppermute(kv, axes, run_route(n_dp, n_ctx))
-    straight = {i: lax.ppermute(kv_again, axes, straight_route(n_dp, n_ctx, 2 * i)) for i in range(1, pairs) if not near(i)}
+    straight = {i: lax.ppermute(kv, axes, straight_route(n_dp, n_ctx, 2 * i)) for i in range(1, pairs) if not near(i)}
     facts, kv_own, q_s, q_t, do_r, start, level, p_own, acc = kernel(
         prepare, [((8, HDIM), jnp.int32), (block, BF16), (by_row, BF16), (by_lane, BF16), (by_row, BF16),
                   ((rows, rows), jnp.int32), (by_row, F32), ((many, rows), BF16), ((many, 2 * HDIM), F32)],
@@ -441,22 +442,27 @@
          (by_row, BF16), (by_lane, BF16), (by_row, F32), ((pairs,) + block, BF16), (p_own.shape, BF16), (p_even.shape, BF16)],
         (facts, q_s, q_t, do_r, start, level, acc, kv_own, kv_even, passed, p_own, p_even),
         [pltpu.VMEM(queries.shape, BF16), pltpu.VMEM((pairs, many, rows), BF16), pltpu.VMEM((many, 2 * HDIM), F32),
-         pltpu.VMEM(by_row, F32), pltpu.VMEM((many, rows), BF16), pltpu.VMEM(block, BF16)],
+         pltpu.VMEM((many // n_ctx, rows), BF16), pltpu.VMEM(block, BF16)],
         5 * pairs * once, aliases=((10, 7), (11, 8)), leaves=(0,), copies=2)
     partner = swap(g_passed, 1).astype(F32)
     shared = (facts, q_t, do_s, do_t, kv_even, p_even, corr)
     ds_even, g_direct = kernel(even, [((pairs - 1, many, rows), BF16), ((pairs - 1,) + block, F32)],
                                shared, [], 3 * (pairs - 1) * once)
-    terms = [partner[0]] + [swap((g_direct[i - 1] + partner[i]).astype(BF16), 2 * i).astype(F32) for i in range(1, pairs)]
+    back = lambda route: [(b, a) for a, b in route]
+    terms = [partner[0]]
+    for i in range(1, pairs):
+        summed = (g_direct[i - 1] + partner[i]).astype(BF16)
+        terms.append(swap(summed, 2 * i) if near(i) else lax.ppermute(summed, axes, back(straight_route(n_dp, n_ctx, 2 * i))))
     grad_queries, g_own, g_prev = kernel(rest, [(queries.shape, BF16), (block, F32), (block, F32)],
                                          shared + (kv_own, p_own, k_odd, ds_odd, ds_even),
                                          [pltpu.VMEM(by_row, F32)], (n_ctx + 7) * once)
     own_total, prev_total = g_own, g_prev
-    for after, term in zip(later, terms):
-        own_total = own_total + jnp.where(after, term, 0.0)
-        prev_total = prev_total + jnp.where(after, 0.0, term)
-    back = [(b, a) for a, b in run_route(n_dp, n_ctx)]
-    last = lax.ppermute(prev_total.astype(BF16), axes, back)
+    for i, term in enumerate(terms):
+        term = term.astype(F32)
+        own_total = own_total + (jnp.where(later[i], term, 0.0) if near(i) else term)
+        if near(i):
+            prev_total = prev_total + jnp.where(later[i], 0.0, term)
+    last = lax.ppermute(prev_total.astype(BF16), axes, back(run_route(n_dp, n_ctx)))
     grad_keys, grad_values = run(finish, "finish", [(keys.shape, BF16), (values.shape, BF16)], (own_total, last), [], 1)
     return (attn_out, grad_queries, grad_keys, grad_values)
 

time: 59.5 us -> 50.1 us (0.84)
  the two profiles are of different devices: /device:TPU:0 before, /device:TPU:18 now
where the time goes in v5:
time: 50.1 us; the launch traced here: 49.5 us
  Pallas kernels  21.3 us (43%)
  starting transfers between devices  17.1 us (34%)
  waiting for transfers between devices  9.81 us (20%)
  between operations  0.79 us (2%)
    pallas_call x7, Pallas kernels, call(): pl.pallas_call(body, out_shape=outs, in_specs=in_specs, out_specs=tuple(o...  21.3 us
    ppermute x6, starting transfers between devices, swap(): return lax.ppermute(blocks, axes, flip_route(n_dp, n_ctx, flip))  6.39 us
    ppermute x1, waiting for transfers between devices, shards(): lax.ppermute(prev_total.astype(BF16), axes, back(run_route(n_dp, n_ctx)))  5.7 us
    ppermute x1, starting transfers between devices, shards(): prev = lax.ppermute(kv, axes, run_route(n_dp, n_ctx))  3.48 us
    ppermute x1, starting transfers between devices, shards(): lax.ppermute(kv, axes, straight_route(n_dp, n_ctx, 2 * i))  3.4 us
    ppermute x6, waiting for transfers between devices, swap(): return lax.ppermute(blocks, axes, flip_route(n_dp, n_ctx, flip))  2.72 us
    ppermute x1, starting transfers between devices, shards(): lax.ppermute(summed, axes, back(straight_route(n_dp, n_ctx, 2 * i)))  1.92 us
    ppermute x1, starting transfers between devices, shards(): lax.ppermute(prev_total.astype(BF16), axes, back(run_route(n_dp, n_ctx)))  1.92 us
  transfers between devices with their start and end apart: 10, of which 3 were waited for; matrix products, arithmetic and copies ran while one was open for 0% of the time, Pallas kernels for 25%

profile of v5, /device:TPU:18, one launch (start us, length us, event | category | flops | bytes accessed | tf_op | source)
XLA Modules:
  0.0 49.5 jit_solution(9635732421056661257)
XLA Ops:
  0.6 0.9 %join.1.kv_ref = bf16[256,256]{1,0:T(8,128)(2,1)S(1)} custom-call(bf16[256,128]{1,0:T(8,128)(2,1)} %keys.1, bf16[256,128]{1,0:T(8,128)(2,1)} %values.1), custom_call_target="tpu_custom_call" | custom-call | flops 1 | bytes 1048576 | tf_op jit(solution)/shard_map/join/pallas_call | solution.py:391
  1.5 3.5 %collective-permute-start = (bf16[256,256]{1,0:T(8,128)(2,1)S(1)}, bf16[256,256]{1,0:T(8,128)(2,1)S(1)}, u32[]{:S(2)}, u32[]{:S(2)}) collective-permute-start(bf16[256,256]{1,0:T(8,128)(2,1)S(1)} %join.1.kv_ref), channel_id=1, source_target_pairs={{0,8},{1,9},{2,10},{3,11},{4,12},{5,13},{6,14},{7,15},{8,16},{9,17... | collective-permute-start | bytes 393224 | tf_op jit(solution)/shard_map/ppermute | solution.py:425
  5.0 3.4 %collective-permute-start.3 = (bf16[256,256]{1,0:T(8,128)(2,1)S(1)}, bf16[256,256]{1,0:T(8,128)(2,1)S(1)}, u32[]{:S(2)}, u32[]{:S(2)}) collective-permute-start(bf16[256,256]{1,0:T(8,128)(2,1)S(1)} %join.1.kv_ref), channel_id=1, source_target_pairs={{0,6},{1,7},{2,4},{3,5},{4,10},{5,11},{6,8},{7,9},{8,14},{9,15},{1... | collective-permute-start | bytes 393224 | tf_op jit(solution)/shard_map/ppermute | solution.py:426
  8.4 2.3 %prepare.1 = (s32[8,128]{1,0:T(8,128)S(1)}, bf16[256,256]{1,0:T(8,128)(2,1)S(1)}, bf16[2048,128]{1,0:T(8,128)(2,1)S(1)}, bf16[128,2048]{1,0:T(8,128)(2,1)S(1)}, ...) custom-call(s32[16]{0:T(128)} %lengths_hbm.1, ...), custom_call_target="tpu_custom_call" | custom-call | flops 268435456 | bytes 1048576 | tf_op jit(solution)/shard_map/prepare/pallas_call | solution.py:391
  10.7 0.0 collective-permute-done.refs_0_
  10.8 0.1 collective-permute-start.2
  10.9 1.5 %collective-permute-start.1 = (bf16[256,256]{1,0:T(8,128)(2,1)S(1)}, bf16[256,256]{1,0:T(8,128)(2,1)S(1)}, u32[]{:S(2)}, u32[]{:S(2)}) collective-permute-start(bf16[256,256]{1,0:T(8,128)(2,1)S(1)} %get-tuple-element.67), channel_id=1, source_target_pairs={{0,2},{1,3},{2,0},{3,1},{4,6},{5,7},{6,4},{7,5},{8,10},{9,11},{10,... | collective-permute-start | bytes 393224 | tf_op jit(solution)/shard_map/ppermute | solution.py:419
  12.4 1.4 %collective-permute-done.3.refs_3_ = bf16[256,256]{1,0:T(8,128)(2,1)S(1)} collective-permute-done((bf16[256,256]{1,0:T(8,128)(2,1)S(1)}, bf16[256,256]{1,0:T(8,128)(2,1)S(1)}, u32[]{:S(2)}, u32[]{:S(2)}) %collective-permute-start.3) | collective-permute-done | bytes 131104 | tf_op jit(solution)/shard_map/ppermute | solution.py:426
  13.8 2.7 %collective-permute-done.2.refs_2_ = bf16[256,256]{1,0:T(8,128)(2,1)S(1)} collective-permute-done((bf16[256,256]{1,0:T(8,128)(2,1)S(1)}, bf16[256,256]{1,0:T(8,128)(2,1)S(1)}, u32[]{:S(2)}, u32[]{:S(2)}) %collective-permute-start.2) | collective-permute-done | bytes 131104 | tf_op jit(solution)/shard_map/ppermute | solution.py:419
  16.5 0.0 collective-permute-done.1.refs_1_
  16.5 0.1 pad_maximum_fusion
  16.6 0.1 collective-permute-start.4
  16.6 2.4 %attend_even.1 = (bf16[4,256,256]{2,1,0:T(8,128)(2,1)S(1)}, bf16[4,2048,256]{2,1,0:T(8,128)(2,1)S(1)}, f32[2048,256]{1,0:T(8,128)S(1)}) custom-call(s32[8,128]{1,0:T(8,128)S(1)} %get-tuple-element.32.facts, bf16[2048,128]{1,0:T(8,128)(2,1)S(1)} %get-tuple-element.33.q_s, s32[256,256]{1,0:T(8,128)S(1)} %get-tuple-element.36.start, ...), custom_call_target="tpu_custom_call" | custom-call | flops 1073741824 | bytes 1048576 | tf_op jit(solution)/shard_map/attend_even/pallas_call | solution.py:391
  19.1 0.0 collective-permute-done.4.kv_odd
  19.1 7.4 %forward.1 = (bf16[256,1024]{1,0:T(8,128)(2,1)}, bf16[4,256,128]{2,1,0:T(8,128)(2,1)S(1)}, bf16[4,2048,256]{2,1,0:T(8,128)(2,1)S(1)}, bf16[2048,128]{1,0:T(8,128...) custom-call(s32[8,128]{1,0:T(8,128)S(1)} %get-tuple-element.32.facts, ...), custom_call_target="tpu_custom_call", output_to_operand_aliasing={{7}: (10, {}), {8}: (11, {})} | custom-call | flops 2684354560 | bytes 1048576 | tf_op jit(solution)/shard_map/forward/pallas_call | solution.py:391
  26.5 1.1 %collective-permute-start.5 = (bf16[4,256,256]{2,1,0:T(8,128)(2,1)S(1)}, bf16[4,256,256]{2,1,0:T(8,128)(2,1)S(1)}, u32[]{:S(2)}, u32[]{:S(2)}) collective-permute-start(bf16[4,256,256]{2,1,0:T(8,128)(2,1)S(1)} %get-tuple-element.55), channel_id=1, source_target_pairs={{0,1},{1,0},{2,3},{3,2},{4,5},{5,4},{6,7},{7,6},{8,9},{9,8},{10,11... | collective-permute-start | bytes 1572872 | tf_op jit(solution)/shard_map/ppermute | solution.py:419
  27.6 2.7 %even.1 = (bf16[3,2048,256]{2,1,0:T(8,128)(2,1)S(1)}, f32[3,256,256]{2,1,0:T(8,128)S(1)}) custom-call(s32[8,128]{1,0:T(8,128)S(1)} %get-tuple-element.32.facts, bf16[128,2048]{1,0:T(8,128)(2,1)S(1)} %get-tuple-element.34.q_t, bf16[2048,128]{1,0:T(8,128)(2,1)S(1)} %get-tuple-element.45.do_s, bf16[128,2048]{1,0:T(8,128)(2,1)S(1)} %get-tuple-element.46.do_t, ...), custom_call_target="tpu_custom_call" | custom-call | flops 1207959552 | bytes 1048576 | tf_op jit(solution)/shard_map/even/pallas_call | solution.py:391
  30.3 0.0 collective-permute-done.5
  30.3 0.1 convert_element_type.33
  30.4 0.1 fusion.11
  30.5 1.9 %collective-permute-start.8 = (bf16[256,256]{1,0:T(8,128)(2,1)S(1)}, bf16[256,256]{1,0:T(8,128)(2,1)S(1)}, u32[]{:S(2)}, u32[]{:S(2)}) collective-permute-start(bf16[256,256]{1,0:T(8,128)(2,1)S(1)} %get-tuple-element.60), channel_id=1, source_target_pairs={{6,0},{7,1},{4,2},{5,3},{10,4},{11,5},{8,6},{9,7},{14,8},{15,9},{1... | collective-permute-start | bytes 393224 | tf_op jit(solution)/shard_map/ppermute | solution.py:455
  32.4 0.1 collective-permute-start.7
  32.5 3.5 %collective-permute-start.6 = (bf16[256,256]{1,0:T(8,128)(2,1)S(1)}, bf16[256,256]{1,0:T(8,128)(2,1)S(1)}, u32[]{:S(2)}, u32[]{:S(2)}) collective-permute-start(bf16[256,256]{1,0:T(8,128)(2,1)S(1)} %get-tuple-element.62), channel_id=1, source_target_pairs={{0,2},{1,3},{2,0},{3,1},{4,6},{5,7},{6,4},{7,5},{8,10},{9,11},{10,... | collective-permute-start | bytes 393224 | tf_op jit(solution)/shard_map/ppermute | solution.py:419
  36.0 5.0 %rest.1 = (bf16[256,1024]{1,0:T(8,128)(2,1)}, f32[256,256]{1,0:T(8,128)S(1)}, f32[256,256]{1,0:T(8,128)S(1)}) custom-call(s32[8,128]{1,0:T(8,128)S(1)} %get-tuple-element.32.facts, bf16[128,2048]{1,0:T(8,128)(2,1)S(1)} %get-tuple-element.34.q_t, bf16[2048,128]{1,0:T(8,128)(2,1)S(1)} %get-tuple-element.45.do_s, bf16[128,2048]{1,0:T(8,128)(2,1)S(1)} %get-tuple-element.46.do_t, ...), custom_call_target="tpu_custom_call" | custom-call | flops 2013265920 | bytes 1048576 | tf_op jit(solution)/shard_map/rest/pallas_call | solution.py:391
  41.0 0.0 collective-permute-done.8
  41.0 0.0 collective-permute-done.7
  41.0 0.0 collective-permute-done.6
  41.0 0.1 fusion.5
  41.2 1.9 %collective-permute-start.9 = (bf16[256,256]{1,0:T(8,128)(2,1)S(1)}, bf16[256,256]{1,0:T(8,128)(2,1)S(1)}, u32[]{:S(2)}, u32[]{:S(2)}) collective-permute-start(bf16[256,256]{1,0:T(8,128)(2,1)S(1)} %get-tuple-element.63), channel_id=1, source_target_pairs={{8,0},{9,1},{10,2},{11,3},{12,4},{13,5},{14,6},{15,7},{16,8},{17,9... | collective-permute-start | bytes 393224 | tf_op jit(solution)/shard_map/ppermute | solution.py:465
  43.1 5.7 %collective-permute-done.9.last = bf16[256,256]{1,0:T(8,128)(2,1)S(1)} collective-permute-done((bf16[256,256]{1,0:T(8,128)(2,1)S(1)}, bf16[256,256]{1,0:T(8,128)(2,1)S(1)}, u32[]{:S(2)}, u32[]{:S(2)}) %collective-permute-start.9) | collective-permute-done | bytes 131104 | tf_op jit(solution)/shard_map/ppermute | solution.py:465
  48.8 0.7 %finish.1 = (bf16[256,128]{1,0:T(8,128)(2,1)}, bf16[256,128]{1,0:T(8,128)(2,1)}) custom-call(f32[256,256]{1,0:T(8,128)S(1)} %get-tuple-element.64.total, bf16[256,256]{1,0:T(8,128)(2,1)S(1)} %collective-permute-done.9.last), custom_call_target="tpu_custom_call" | custom-call | flops 1 | bytes 1048576 | tf_op jit(solution)/shard_map/finish/pallas_call | solution.py:391
  (1 shorter events, 0.0 us)
Async XLA Ops:
  1.5 9.2 %collective-permute-start = (bf16[256,256]{1,0:T(8,128)(2,1)S(1)}, bf16[256,256]{1,0:T(8,128)(2,1)S(1)}, u32[]{:S(2)}, u32[]{:S(2)}) collective-permute-start(bf16[256,256]{1,0:T(8,128)(2,1)S(1)} %join.1.kv_ref), channel_id=1, source_target_pairs={{0,8},{1,9},{2,10},{3,11},{4,12},{5,13},{6,14},{7,15},{8,16},{9,17... | collective-permute-start | bytes 393224 | tf_op jit(solution)/shard_map/ppermute | solution.py:425
  5.0 8.8 %collective-permute-start.3 = (bf16[256,256]{1,0:T(8,128)(2,1)S(1)}, bf16[256,256]{1,0:T(8,128)(2,1)S(1)}, u32[]{:S(2)}, u32[]{:S(2)}) collective-permute-start(bf16[256,256]{1,0:T(8,128)(2,1)S(1)} %join.1.kv_ref), channel_id=1, source_target_pairs={{0,6},{1,7},{2,4},{3,5},{4,10},{5,11},{6,8},{7,9},{8,14},{9,15},{1... | collective-permute-start | bytes 393224 | tf_op jit(solution)/shard_map/ppermute | solution.py:426
  10.8 5.7 %collective-permute-start.2 = (bf16[256,256]{1,0:T(8,128)(2,1)S(1)}, bf16[256,256]{1,0:T(8,128)(2,1)S(1)}, u32[]{:S(2)}, u32[]{:S(2)}) collective-permute-start(bf16[256,256]{1,0:T(8,128)(2,1)S(1)} %get-tuple-element.66), channel_id=1, source_target_pairs={{0,4},{1,5},{2,6},{3,7},{4,0},{5,1},{6,2},{7,3},{8,12},{9,13},{10,... | collective-permute-start | bytes 393224 | tf_op jit(solution)/shard_map/ppermute | solution.py:419
  10.9 5.6 %collective-permute-start.1 = (bf16[256,256]{1,0:T(8,128)(2,1)S(1)}, bf16[256,256]{1,0:T(8,128)(2,1)S(1)}, u32[]{:S(2)}, u32[]{:S(2)}) collective-permute-start(bf16[256,256]{1,0:T(8,128)(2,1)S(1)} %get-tuple-element.67), channel_id=1, source_target_pairs={{0,2},{1,3},{2,0},{3,1},{4,6},{5,7},{6,4},{7,5},{8,10},{9,11},{10,... | collective-permute-start | bytes 393224 | tf_op jit(solution)/shard_map/ppermute | solution.py:419
  16.6 2.5 %collective-permute-start.4 = (bf16[4,256,256]{2,1,0:T(8,128)(2,1)S(1)}, bf16[4,256,256]{2,1,0:T(8,128)(2,1)S(1)}, u32[]{:S(2)}, u32[]{:S(2)}) collective-permute-start(bf16[4,256,256]{2,1,0:T(8,128)(2,1)S(1)} %pad_maximum_fusion), channel_id=1, source_target_pairs={{0,1},{1,0},{2,3},{3,2},{4,5},{5,4},{6,7},{7,6},{8,9},{9,8},{10,11... | collective-permute-start | bytes 1572872 | tf_op jit(solution)/shard_map/ppermute | solution.py:419
  26.5 3.8 %collective-permute-start.5 = (bf16[4,256,256]{2,1,0:T(8,128)(2,1)S(1)}, bf16[4,256,256]{2,1,0:T(8,128)(2,1)S(1)}, u32[]{:S(2)}, u32[]{:S(2)}) collective-permute-start(bf16[4,256,256]{2,1,0:T(8,128)(2,1)S(1)} %get-tuple-element.55), channel_id=1, source_target_pairs={{0,1},{1,0},{2,3},{3,2},{4,5},{5,4},{6,7},{7,6},{8,9},{9,8},{10,11... | collective-permute-start | bytes 1572872 | tf_op jit(solution)/shard_map/ppermute | solution.py:419
  30.5 10.5 %collective-permute-start.8 = (bf16[256,256]{1,0:T(8,128)(2,1)S(1)}, bf16[256,256]{1,0:T(8,128)(2,1)S(1)}, u32[]{:S(2)}, u32[]{:S(2)}) collective-permute-start(bf16[256,256]{1,0:T(8,128)(2,1)S(1)} %get-tuple-element.60), channel_id=1, source_target_pairs={{6,0},{7,1},{4,2},{5,3},{10,4},{11,5},{8,6},{9,7},{14,8},{15,9},{1... | collective-permute-start | bytes 393224 | tf_op jit(solution)/shard_map/ppermute | solution.py:455
  32.4 8.6 %collective-permute-start.7 = (bf16[256,256]{1,0:T(8,128)(2,1)S(1)}, bf16[256,256]{1,0:T(8,128)(2,1)S(1)}, u32[]{:S(2)}, u32[]{:S(2)}) collective-permute-start(bf16[256,256]{1,0:T(8,128)(2,1)S(1)} %get-tuple-element.61), channel_id=1, source_target_pairs={{0,4},{1,5},{2,6},{3,7},{4,0},{5,1},{6,2},{7,3},{8,12},{9,13},{10,... | collective-permute-start | bytes 393224 | tf_op jit(solution)/shard_map/ppermute | solution.py:419
  32.5 8.5 %collective-permute-start.6 = (bf16[256,256]{1,0:T(8,128)(2,1)S(1)}, bf16[256,256]{1,0:T(8,128)(2,1)S(1)}, u32[]{:S(2)}, u32[]{:S(2)}) collective-permute-start(bf16[256,256]{1,0:T(8,128)(2,1)S(1)} %get-tuple-element.62), channel_id=1, source_target_pairs={{0,2},{1,3},{2,0},{3,1},{4,6},{5,7},{6,4},{7,5},{8,10},{9,11},{10,... | collective-permute-start | bytes 393224 | tf_op jit(solution)/shard_map/ppermute | solution.py:419
  41.2 7.6 %collective-permute-start.9 = (bf16[256,256]{1,0:T(8,128)(2,1)S(1)}, bf16[256,256]{1,0:T(8,128)(2,1)S(1)}, u32[]{:S(2)}, u32[]{:S(2)}) collective-permute-start(bf16[256,256]{1,0:T(8,128)(2,1)S(1)} %get-tuple-element.63), channel_id=1, source_target_pairs={{8,0},{9,1},{10,2},{11,3},{12,4},{13,5},{14,6},{15,7},{16,8},{17,9... | collective-permute-start | bytes 393224 | tf_op jit(solution)/shard_map/ppermute | solution.py:465
